TPU v7x, 256 devices: a whole 4x4x8 slice. The times are simulated.
256 devices in a mesh: half: 2 (over core), member: 16 (over y, x), tile: 8 (over z).
Axes of the slice: x: 4, y: 4, z: 8, core: 2. Of those that a mesh axis runs over, the one named last changes fastest.
Arguments:
- state: float32 [32, 16, 512, 1024], P(('half', 'member'), None, 'tile'), may hold values from -6 to 6
- weights: float32 [32, 512, 1024], P(('half', 'member'), 'tile'), may hold values from -6 to 6
- land_mask: int32 [512, 1024], P('tile'), may hold values 0 or 1
- level_gain: float32 [16], replicated, may hold values from 0.3 to 1
- depth: float32 [16], replicated, may hold values from 0.5 to 2
- obs_row: int32 [131072], P('tile'), may hold values from 1 to 62
- obs_col: int32 [131072], P('tile'), may hold values from 0 to 1023
- obs_quad: int32 [131072], P('tile'), may hold values from 0 to 3
- obs_frac: float32 [2, 131072], P(None, 'tile'), may hold values from 0 to 1
- obs_value: float32 [131072], P('tile'), may hold values from -6 to 6
- obs_error: float32 [131072], P('tile'), may hold values from 0.3 to 3
- noise: float32 [32, 131072], P(('half', 'member'), 'tile'), may hold values from -6 to 6
Outputs:
- stepped: float32 [32, 16, 512, 1024], P(('half', 'member'), None, 'tile')
- new_weights: float32 [32, 512, 1024], P(('half', 'member'), 'tile')
- misfit: float32 [32, 131072], P(None, ('half', 'member', 'tile'))
All inputs are finite; a program needn't handle non-finite values. No bound on the sum of `land_mask` on one device may be relied on, other than what follows from the above.
Results may differ from a plain program's by a relative error of at most 0.000071.
Values sent between devices are 32-bit elements; how exact they have to be, the bound alone decides.
No kernel may reach another device: no remote copies, remote signals or barrier semaphores. Data moves between devices by JAX's collectives and lax.ppermute only.
A program may use at most 128 MiB of HBM per device.

v0:
```python
import math

import jax
import jax.numpy as jnp
from jax import lax
from jax.sharding import PartitionSpec as P


def with_halo(block, sides, width):
    for axis, dim in sides:
        count = lax.axis_size(axis)
        forward = [(i, i + 1) for i in range(count - 1)]
        backward = [(target, source) for source, target in forward]
        low = lax.ppermute(
            lax.slice_in_dim(block, block.shape[dim] - width, None, axis=dim), axis, forward
        )
        high = lax.ppermute(lax.slice_in_dim(block, 0, width, axis=dim), axis, backward)
        block = jnp.concatenate([low, block, high], axis=dim)
    return block


def interpolate(column, row_index, col_index, obs_quad, obs_frac):
    width = column.shape[1]
    row_step = jnp.where(obs_quad % 2 == 1, 1, -1).astype(jnp.int32)
    col_step = jnp.where(obs_quad // 2 == 1, 1, -1).astype(jnp.int32)
    row_other = row_index + row_step
    col_other = (col_index + col_step) % width
    flat = column.reshape(-1)
    corner_aa = jnp.take(flat, row_index * width + col_index)
    corner_ab = jnp.take(flat, row_index * width + col_other)
    corner_ba = jnp.take(flat, row_other * width + col_index)
    corner_bb = jnp.take(flat, row_other * width + col_other)
    first = obs_frac[0]
    second = obs_frac[1]
    return (
        (1.0 - first) * (1.0 - second) * corner_aa
        + (1.0 - first) * second * corner_ab
        + first * (1.0 - second) * corner_ba
        + first * second * corner_bb
    )


def on_device(
    state,
    weights,
    land_mask,
    level_gain,
    depth,
    obs_row,
    obs_col,
    obs_quad,
    obs_frac,
    obs_value,
    obs_error,
    noise,
):
    highest = lax.Precision.HIGHEST
    members = lax.axis_size(("half", "member"))
    member_index = lax.axis_index(("half", "member"))
    tile_count = lax.axis_size("tile")
    obs_local = obs_row.shape[0]
    shard_size = obs_local // members
    total_obs = obs_local * tile_count
    padded = with_halo(state, (("tile", 2),), 1)
    laplacian = (
        padded[:, :, :-2]
        + padded[:, :, 2:]
        + jnp.roll(state, 1, axis=3)
        + jnp.roll(state, -1, axis=3)
        - 4.0 * state
    )
    diffusivity = 0.24 * jax.nn.sigmoid(weights)
    ocean_cells = land_mask.astype(jnp.float32)
    stepped = (
        state
        + level_gain[None, :, None, None] * (ocean_cells[None] * diffusivity)[:, None] * laplacian
    )
    levels_here = state.shape[1]
    column = jnp.sum(depth[:, None, None] * stepped[0], axis=0) / math.sqrt(levels_here)
    predicted = interpolate(column, obs_row, obs_col, obs_quad, obs_frac)
    perturbed = obs_value + noise[0]
    grouped, noisy_grouped = (
        lax.all_to_all(
            predicted.reshape(members, shard_size),
            ("half", "member"),
            split_axis=0,
            concat_axis=0,
            tiled=True,
        ),
        lax.all_to_all(
            perturbed.reshape(members, shard_size),
            ("half", "member"),
            split_axis=0,
            concat_axis=0,
            tiled=True,
        ),
    )
    error_shard = lax.dynamic_slice_in_dim(obs_error, member_index * shard_size, shard_size, 0)
    misfit = noisy_grouped - grouped
    anomaly = grouped - jnp.mean(grouped, axis=0, keepdims=True)
    weighted = anomaly / error_shard[None]
    gram = jnp.einsum("ko,jo->kj", weighted, anomaly, precision=highest)
    products = jnp.einsum("ko,jo->kj", weighted, misfit, precision=highest)
    gram, products = lax.psum((gram, products), ("half", "member", "tile"))
    identity = jnp.eye(members, dtype=jnp.float32)
    factor = jnp.linalg.cholesky(identity + gram / total_obs)
    coefficients = jax.scipy.linalg.cho_solve((factor, True), products / total_obs)
    combination = identity + coefficients - jnp.mean(coefficients, axis=0, keepdims=True)
    own_column = lax.dynamic_slice_in_dim(combination, member_index, 1, 1)[:, 0]
    initial = jnp.zeros(weights.shape[1:], jnp.float32)
    new_weights = (
        initial
        + jnp.einsum(
            "k,krc->rc",
            own_column,
            lax.all_gather(weights, ("half", "member"), axis=0, tiled=True),
            precision=highest,
        )
    )[None]
    return (stepped, new_weights, misfit)


def solution(mesh):
    in_specs = (
        P(("half", "member"), None, "tile", None),
        P(("half", "member"), "tile", None),
        P("tile", None),
        P(),
        P(),
        P("tile"),
        P("tile"),
        P("tile"),
        P(None, "tile"),
        P("tile"),
        P("tile"),
        P(("half", "member"), "tile"),
    )
    out_specs = (
        P(("half", "member"), None, "tile", None),
        P(("half", "member"), "tile", None),
        P(None, ("half", "member", "tile")),
    )
    return jax.shard_map(
        on_device, mesh=mesh, in_specs=in_specs, out_specs=out_specs, check_vma=False
    )
```

profile of v0, /device:TPU:1, one launch (start us, length us, event | category | flops | bytes accessed | tf_op | source)
XLA Modules:
  0.0 536.1 jit_solution(11448985625103804217)
XLA Ops:
  7.2 0.0 all-gather.2.cloned.1.call-start
  7.2 0.7 all-gather.2.cloned.1.call-update
  7.9 1.3 fusion.40
  9.2 4.4 collective-permute-start
  13.6 1.3 collective-permute-start.1
  14.9 1.4 fusion.41
  16.3 1.1 broadcast_clamp_fusion.2
  17.4 0.0 copy-start.6
  17.4 0.0 copy-start
  17.4 0.0 copy-start.1
  17.4 0.0 copy-start.7
  17.4 0.0 copy-start.8
  17.4 0.0 copy-start.9
  17.5 0.0 copy-start.10
  17.5 8.0 %fusion.42 = (f32[1,16,64,1023]{3,2,1,0:T(8,128)}, f32[1,16,64,1023]{3,2,1,0:T(8,128)}) fusion(f32[1,16,64,1024]{3,2,1,0:T(8,128)} %param.14), kind=kLoop, calls=%fused_computation.86 | loop fusion | bytes 16760832 | tf_op jit(solution)/shard_map/jit(_roll_static)/slice | solution.py:68
  25.5 0.0 copy-done.6
  25.5 0.1 fusion.43
  25.6 0.0 copy-done
  25.6 0.0 copy-done.1
  25.6 0.1 fusion.9
  25.7 0.8 dynamic_slice.6
  26.5 0.0 copy-done.7
  26.5 0.0 copy-done.8
  26.5 0.6 add.116
  27.1 0.0 collective-permute-done
  27.1 0.0 collective-permute-done.1
  27.1 0.0 copy-done.9
  27.1 0.0 copy-done.10
  27.1 11.0 %fusion.8 = (f32[64,1024]{1,0:T(8,128)S(1)}, f32[1,16,64,1024]{3,2,1,0:T(8,128)}) fusion(f32[16]{0:T(128)S(1)} %copy-done.9, f32[1,16,64,1024]{3,2,1,0:T(8,128)} %param.14, f32[1,16,64,1]{3,2,1,0:T(8,128)S(1)} %get-tuple-element.13, f32[1,16,64,1023]{3,2,1,0:T(8,128)} %get-tuple-element.15, f32[1,16,64,1023]{3,2,1,0:T(8,128)} %get-tuple-element.14, ...), kind=kLoop, calls=%fused_computation.15 | loop fusion | flops 14614528 | bytes 17432704 | tf_op jit(solution)/shard_map/reduce_sum | solution.py:79
  38.2 90.5 %gather_fusion = f32[16384]{0:T(1024)S(1)} fusion(f32[65536]{0:T(1024)S(1)} %bitcast.48, s32[16384]{0:T(1024)S(1)} %get-tuple-element.21), kind=kCustom, calls=%fused_computation.clone | custom fusion | bytes 196608 | tf_op jit(solution)/shard_map/jit(_take)/gather | solution.py:29
  128.8 90.5 %gather_fusion.1 = f32[16384]{0:T(1024)S(1)} fusion(f32[65536]{0:T(1024)S(1)} %bitcast.49, s32[16384]{0:T(1024)S(1)} %get-tuple-element.16), kind=kCustom, calls=%fused_computation.1.clone | custom fusion | bytes 196608 | tf_op jit(solution)/shard_map/jit(_take)/gather | solution.py:30
  219.3 90.5 %gather_fusion.2 = f32[16384]{0:T(1024)S(1)} fusion(f32[65536]{0:T(1024)S(1)} %bitcast.50, s32[16384]{0:T(1024)S(1)} %get-tuple-element.18), kind=kCustom, calls=%fused_computation.2.clone | custom fusion | bytes 196608 | tf_op jit(solution)/shard_map/jit(_take)/gather | solution.py:31
  309.8 0.0 copy-start.2
  309.9 0.0 copy-start.3
  309.9 0.0 copy-start.4
  309.9 90.5 %gather_fusion.3 = f32[16384]{0:T(1024)S(1)} fusion(f32[65536]{0:T(1024)S(1)} %bitcast.51, s32[16384]{0:T(1024)S(1)} %get-tuple-element.17), kind=kCustom, calls=%fused_computation.3.clone | custom fusion | bytes 196608 | tf_op jit(solution)/shard_map/jit(_take)/gather | solution.py:32
  400.4 0.0 copy-done.2
  400.4 0.0 copy-done.3
  400.4 0.0 copy-done.4
  400.5 0.8 fusion.19
  401.3 8.1 %all-to-all-start = ((f32[32,1,512]{2,1,0:T(1,128)}), f32[32,1,512]{2,1,0:T(1,128)S(1)}, u32[]{:S(2)}, u32[]{:S(2)}) async-start(f32[32,1,512]{2,1,0:T(1,128)} %bitcast.5), calls=%async_computation | async-start | bytes 131072 | tf_op jit(solution)/shard_map/all_to_all | solution.py:83
  409.4 7.1 %all-to-all-done = f32[32,1,512]{2,1,0:T(1,128)S(1)} async-done(((f32[32,1,512]{2,1,0:T(1,128)}), f32[32,1,512]{2,1,0:T(1,128)S(1)}, u32[]{:S(2)}, u32[]{:S(2)}) %all-to-all-start) | async-done | bytes 65568 | tf_op jit(solution)/shard_map/all_to_all | solution.py:83
  416.5 4.2 all-to-all-start.1
  420.7 0.1 reduce_sum.28
  420.8 7.0 %all-to-all-done.1 = f32[32,1,512]{2,1,0:T(1,128)S(1)} async-done(((f32[32,1,512]{2,1,0:T(1,128)}), f32[32,1,512]{2,1,0:T(1,128)S(1)}, u32[]{:S(2)}, u32[]{:S(2)}) %all-to-all-start.1) | async-done | bytes 65568 | tf_op jit(solution)/shard_map/all_to_all | solution.py:90
  427.8 0.1 broadcast_divide_fusion
  427.9 0.0 copy-start.5
  427.9 0.2 fusion.16
  428.1 0.2 fusion.13
  428.3 79.0 %all-reduce = (f32[32,32]{1,0:T(8,128)S(1)}, f32[32,32]{1,0:T(8,128)S(1)}) all-reduce(f32[32,32]{1,0:T(8,128)S(1)} %fusion.13, f32[32,32]{1,0:T(8,128)S(1)} %fusion.16), channel_id=1, replica_groups=mesh['half'=2,'member'=16,'tile'=8] {'half','member','tile'}, use_global_device_ids=true, to_apply=%region_2.4 | all-reduce | flops 2048 | bytes 16384 | tf_op jit(solution)/shard_map/psum | solution.py:104
  507.3 0.1 copy.19
  507.4 2.9 cholesky.14
  510.3 0.6 compare_reduce_fusion
  511.0 0.7 fusion.26
  511.6 2.4 custom-call.10
  514.1 0.2 fusion.31
  514.3 0.3 fusion.44
  514.6 0.1 copy.26
  514.7 0.6 dynamic-slice
  515.3 0.8 fusion.28
  516.1 0.0 all-gather.2.cloned.1.call-done
  516.2 12.3 %fusion = f32[1,64,1024]{2,0,1:T(1,128)S(1)} fusion(f32[32,64,1024]{2,1,0:T(8,128)} %all-gather.2.cloned.1.call-done, f32[32]{0:T(128)S(1)} %fusion.28), kind=kOutput, calls=%fused_computation.4 | convolution fusion | flops 25165824 | bytes 8650880 | tf_op jit(solution)/shard_map/k,krc->rc/dot_general | solution.py:113
  528.5 0.0 copy-done.5
  528.5 0.8 copy.22
  (10 shorter events, 0.2 us)
Async XLA Ops:
  7.2 509.0 %all-gather.2.cloned.1.call-start = ((), (), s32[]{:S(2)}) async-start(), calls=%async_computation.2 | async-start | bytes 8650752 | tf_op jit(solution)/shard_map/all_gather | solution.py:116
  9.2 17.9 %collective-permute-start = (f32[1,16,1,1024]{3,2,1,0:T(1,128)S(1)}, f32[1,16,1,1024]{3,2,1,0:T(1,128)S(1)}, u32[]{:S(2)}, u32[]{:S(2)}) collective-permute-start(f32[1,16,1,1024]{3,2,1,0:T(1,128)S(1)} %get-tuple-element.10), channel_id=1, source_target_pairs={{0,1},{1,2},{2,3},{3,4},{4,5},{5,6},{6,7},{8,9},{9,10},{10,11},{11... | collective-permute-start | bytes 196616 | tf_op jit(solution)/shard_map/ppermute | solution.py:14
  13.6 13.6 %collective-permute-start.1 = (f32[1,16,1,1024]{3,2,1,0:T(1,128)S(1)}, f32[1,16,1,1024]{3,2,1,0:T(1,128)S(1)}, u32[]{:S(2)}, u32[]{:S(2)}) collective-permute-start(f32[1,16,1,1024]{3,2,1,0:T(1,128)S(1)} %get-tuple-element.11), channel_id=1, source_target_pairs={{1,0},{2,1},{3,2},{4,3},{5,4},{6,5},{7,6},{9,8},{10,9},{11,10},{12... | collective-permute-start | bytes 196616 | tf_op jit(solution)/shard_map/ppermute | solution.py:17
  17.4 8.1 %copy-start.6 = (f32[2,16384]{1,0:T(2,128)S(1)}, f32[2,16384]{1,0:T(2,128)}, u32[]{:S(2)}) copy-start(f32[2,16384]{1,0:T(2,128)} %param.22) | copy-start | bytes 393220
  17.4 8.2 %copy-start = (f32[1,64,1024]{2,1,0:T(8,128)S(1)}, f32[1,64,1024]{2,1,0:T(8,128)}, u32[]{:S(2)}) copy-start(f32[1,64,1024]{2,1,0:T(8,128)} %param.15) | copy-start | bytes 786436
  17.4 8.2 %copy-start.1 = (s32[64,1024]{1,0:T(8,128)S(1)}, s32[64,1024]{1,0:T(8,128)}, u32[]{:S(2)}) copy-start(s32[64,1024]{1,0:T(8,128)} %param.16) | copy-start | bytes 786436
  17.4 9.1 %copy-start.7 = (f32[16384]{0:T(1024)S(1)}, f32[16384]{0:T(1024)}, u32[]{:S(2)}) copy-start(f32[16384]{0:T(1024)} %param.23) | copy-start | bytes 196612
  17.4 9.1 %copy-start.8 = (f32[1,16384]{1,0:T(1,128)S(1)}, f32[1,16384]{1,0:T(1,128)}, u32[]{:S(2)}) copy-start(f32[1,16384]{1,0:T(1,128)} %param.25) | copy-start | bytes 196612
  17.4 9.7 %copy-start.9 = (f32[16]{0:T(128)S(1)}, f32[16]{0:T(128)}, u32[]{:S(2)}) copy-start(f32[16]{0:T(128)} %param.18) | copy-start | bytes 196
  17.5 9.7 %copy-start.10 = (f32[16]{0:T(128)S(1)}, f32[16]{0:T(128)}, u32[]{:S(2)}) copy-start(f32[16]{0:T(128)} %param.17) | copy-start | bytes 196
  309.8 90.6 %copy-start.2 = (s32[16384]{0:T(1024)S(1)}, s32[16384]{0:T(1024)}, u32[]{:S(2)}) copy-start(s32[16384]{0:T(1024)} %param.19) | copy-start | bytes 196612
  309.9 90.6 %copy-start.3 = (s32[16384]{0:T(1024)S(1)}, s32[16384]{0:T(1024)}, u32[]{:S(2)}) copy-start(s32[16384]{0:T(1024)} %param.20) | copy-start | bytes 196612
  309.9 90.6 %copy-start.4 = (s32[16384]{0:T(1024)S(1)}, s32[16384]{0:T(1024)}, u32[]{:S(2)}) copy-start(s32[16384]{0:T(1024)} %param.21) | copy-start | bytes 196612
  401.3 15.2 %all-to-all-start = ((f32[32,1,512]{2,1,0:T(1,128)}), f32[32,1,512]{2,1,0:T(1,128)S(1)}, u32[]{:S(2)}, u32[]{:S(2)}) async-start(f32[32,1,512]{2,1,0:T(1,128)} %bitcast.5), calls=%async_computation | async-start | bytes 131072 | tf_op jit(solution)/shard_map/all_to_all | solution.py:83
  416.5 11.3 %all-to-all-start.1 = ((f32[32,1,512]{2,1,0:T(1,128)}), f32[32,1,512]{2,1,0:T(1,128)S(1)}, u32[]{:S(2)}, u32[]{:S(2)}) async-start(f32[32,1,512]{2,1,0:T(1,128)} %bitcast.10), calls=%async_computation.1 | async-start | bytes 131072 | tf_op jit(solution)/shard_map/all_to_all | solution.py:90
  427.9 100.6 %copy-start.5 = (f32[32,1,512]{2,0,1:T(8,128)}, f32[32,1,512]{2,0,1:T(8,128)S(1)}, u32[]{:S(2)}) copy-start(f32[32,1,512]{2,0,1:T(8,128)S(1)} %copy.43) | copy-start | bytes 196612
Sparse Core Ops, SparseCore 0:
  10.6 62.1 all-gather.1
where the time goes:
time: 537 us; the launch traced here: 536 us
  local copies, waits for them, and re-layouts  375 us (70%)
  blocking collectives  79 us (15%)
  other arithmetic  21.4 us (4%)
  starting transfers between devices  18 us (3%)
  waiting for transfers between devices  14.8 us (3%)
  between operations  14.4 us (3%)
  matrix products  13.2 us (2%)
    gather x1, local copies, waits for them, and re-layouts, interpolate(): corner_aa = jnp.take(flat, row_index * width + col_index)  90.5 us
    gather x1, local copies, waits for them, and re-layouts, interpolate(): corner_ab = jnp.take(flat, row_index * width + col_other)  90.5 us
    gather x1, local copies, waits for them, and re-layouts, interpolate(): corner_ba = jnp.take(flat, row_other * width + col_index)  90.5 us
    gather x1, local copies, waits for them, and re-layouts, interpolate(): corner_bb = jnp.take(flat, row_other * width + col_other)  90.5 us
    psum x1, blocking collectives, on_device(): gram, products = lax.psum((gram, products), ('half', 'member', 'tile'))  79 us
    dot_general x1, matrix products, on_device(): jnp.einsum('k,krc->rc', own_column, lax.all_gather(weights, ('half', 'mem...  12.3 us
    reduce_sum x1, other arithmetic, on_device(): jnp.sum(depth[:, None, None] * stepped[0], axis=0) / math.sqrt(levels_here)  11 us
  transfers between devices with their start and end apart: 5, of which 2 were waited for; matrix products, arithmetic and copies ran while one was open for 74% of the time, Pallas kernels for 0%

commit v1 on v0

v1 whole, which is shorter than its diff:
```python
import math

import jax
import jax.numpy as jnp
from jax import lax
from jax.experimental import pallas as pl
from jax.experimental.pallas import tpu as pltpu
from jax.sharding import PartitionSpec as P

LANES = 128
SUBLANES = 8
LEVELS_STEP = 2


def step_and_sample(
    gain_ref,
    depth_ref,
    state_ref,
    low_ref,
    high_ref,
    weights_ref,
    land_ref,
    row_ref,
    col_ref,
    quad_ref,
    frac_ref,
    perturbed_ref,
    stepped_ref,
    predicted_ref,
    residual_ref,
    diffusivity_ref,
    column_ref,
    even_ref,
    odd_ref,
):
    step = pl.program_id(0)
    steps = pl.num_programs(0)
    levels, rows, cols = state_ref.shape
    sub = lax.broadcasted_iota(jnp.int32, (SUBLANES, cols), 0)

    @pl.when(step == 0)
    def _():
        diffusivity_ref[...] = land_ref[...].astype(jnp.float32) * (
            0.24 * jax.nn.sigmoid(weights_ref[...])
        )
        column_ref[...] = jnp.zeros_like(column_ref)

    for start in range(0, rows, SUBLANES):
        here = pl.ds(start, SUBLANES)
        total = column_ref[here, :]
        diffusivity = diffusivity_ref[here, :]
        for level in range(levels):
            centre = state_ref[level, here, :]
            if start == 0:
                above_row = low_ref[level]
            else:
                above_row = state_ref[level, pl.ds(start - 1, 1), :]
            if start + SUBLANES == rows:
                below_row = high_ref[level]
            else:
                below_row = state_ref[level, pl.ds(start + SUBLANES, 1), :]
            above = jnp.where(sub == 0, above_row, pltpu.roll(centre, 1, 0))
            below = jnp.where(
                sub == SUBLANES - 1, below_row, pltpu.roll(centre, SUBLANES - 1, 0)
            )
            laplacian = (
                above
                + below
                + pltpu.roll(centre, 1, 1)
                + pltpu.roll(centre, cols - 1, 1)
                - 4.0 * centre
            )
            number = step * levels + level
            stepped = centre + gain_ref[number] * diffusivity * laplacian
            stepped_ref[level, here, :] = stepped
            total = total + depth_ref[number] * stepped
        column_ref[here, :] = total

    @pl.when(step == steps - 1)
    def _():
        scale = 1.0 / math.sqrt(levels * steps)
        lane = lax.broadcasted_iota(jnp.int32, (SUBLANES, LANES), 1)
        doubled = (2 * lane) % LANES
        first_half = lane < LANES // 2

        def pick(table, index):
            return jnp.take_along_axis(table, index, axis=1, mode="promise_in_bounds")

        for start in range(0, rows, SUBLANES):
            here = pl.ds(start, SUBLANES)
            for part in range(cols // (2 * LANES)):
                left = column_ref[here, pl.ds(2 * part * LANES, LANES)] * scale
                right = column_ref[here, pl.ds((2 * part + 1) * LANES, LANES)] * scale
                out = pl.ds(part * LANES, LANES)
                even_ref[here, out] = jnp.where(
                    first_half, pick(left, doubled), pick(right, doubled)
                )
                odd_ref[here, out] = jnp.where(
                    first_half, pick(left, doubled + 1), pick(right, doubled + 1)
                )

        sub_here = lax.broadcasted_iota(jnp.int32, (SUBLANES, LANES), 0)

        def sample(i, carry):
            def spread(value):
                return jnp.broadcast_to(value, (SUBLANES, LANES))

            one = pl.ds(i, 1)
            row = spread(row_ref[one, :])
            col = spread(col_ref[one, :])
            quad = spread(quad_ref[one, :])
            place = pl.ds(pl.multiple_of(i * LANES, LANES), LANES)
            first = spread(frac_ref[pl.ds(0, 1), place])
            second = spread(frac_ref[pl.ds(1, 1), place])
            row_other = row + jnp.where((quad & 1) == 1, 1, -1)
            col_other = (col + jnp.where((quad >> 1) == 1, 1, -1)) & (cols - 1)
            is_even = (col & 1) == 0
            even_at = jnp.where(is_even, col, col_other) >> 1
            odd_at = jnp.where(is_even, col_other, col) >> 1
            even_by = jnp.where(is_even, 1.0 - second, second)
            odd_by = jnp.where(is_even, second, 1.0 - second)
            even_lane, even_part = even_at & (LANES - 1), even_at // LANES
            odd_lane, odd_part = odd_at & (LANES - 1), odd_at // LANES
            parts = cols // (2 * LANES)
            even_here = [even_part == part for part in range(1, parts)]
            odd_here = [odd_part == part for part in range(1, parts)]
            total = jnp.zeros((SUBLANES, LANES), jnp.float32)
            for start in range(0, rows, SUBLANES):
                here = pl.ds(start, SUBLANES)
                even = pick(even_ref[here, pl.ds(0, LANES)], even_lane)
                odd = pick(odd_ref[here, pl.ds(0, LANES)], odd_lane)
                for part in range(1, parts):
                    out = pl.ds(part * LANES, LANES)
                    even = jnp.where(
                        even_here[part - 1], pick(even_ref[here, out], even_lane), even
                    )
                    odd = jnp.where(
                        odd_here[part - 1], pick(odd_ref[here, out], odd_lane), odd
                    )
                by_row = jnp.where(
                    sub_here == row - start,
                    1.0 - first,
                    jnp.where(sub_here == row_other - start, first, 0.0),
                )
                total = total + by_row * (even_by * even + odd_by * odd)
            predicted_ref[one, :] = jnp.sum(total, axis=0, keepdims=True)
            return carry

        lax.fori_loop(0, row_ref.shape[0], sample, 0, unroll=2)
        residual_ref[...] = perturbed_ref[...] - predicted_ref[...]


def forward(
    level_gain, depth, state, low, high, weights, land_mask, row, col, quad, frac, perturbed
):
    levels, rows, cols = state.shape
    per = LEVELS_STEP

    def whole(array):
        return pl.BlockSpec(array.shape, lambda i: (0,) * array.ndim)

    smem = pl.BlockSpec(memory_space=pltpu.SMEM)
    halo = pl.BlockSpec((per, 1, cols), lambda i: (i, 0, 0))
    field = pl.BlockSpec((per, rows, cols), lambda i: (i, 0, 0))
    return pl.pallas_call(
        step_and_sample,
        grid=(levels // per,),
        in_specs=[smem, smem, field, halo, halo]
        + [whole(array) for array in (weights, land_mask, row, col, quad, frac, perturbed)],
        out_specs=[field, whole(row), whole(row)],
        out_shape=[
            jax.ShapeDtypeStruct(state.shape, jnp.float32),
            jax.ShapeDtypeStruct(row.shape, jnp.float32),
            jax.ShapeDtypeStruct(row.shape, jnp.float32),
        ],
        scratch_shapes=[
            pltpu.VMEM((rows, cols), jnp.float32),
            pltpu.VMEM((rows, cols), jnp.float32),
            pltpu.VMEM((rows, cols // 2), jnp.float32),
            pltpu.VMEM((rows, cols // 2), jnp.float32),
        ],
        compiler_params=pltpu.CompilerParams(vmem_limit_bytes=24 * 1024 * 1024),
        name="step_and_sample",
    )(level_gain, depth, state, low, high, weights, land_mask, row, col, quad, frac, perturbed)


def on_device(
    state,
    weights,
    land_mask,
    level_gain,
    depth,
    obs_row,
    obs_col,
    obs_quad,
    obs_frac,
    obs_value,
    obs_error,
    noise,
):
    highest = lax.Precision.HIGHEST
    axes = ("half", "member")
    members = lax.axis_size(axes)
    member_index = lax.axis_index(axes)
    tile_count = lax.axis_size("tile")
    obs_local = obs_row.shape[0]
    shard_size = obs_local // members
    total_obs = obs_local * tile_count
    own = state[0]
    up = [(i, i + 1) for i in range(tile_count - 1)]
    down = [(target, source) for source, target in up]
    low = lax.ppermute(own[:, -1:], "tile", up)
    high = lax.ppermute(own[:, :1], "tile", down)
    grid = (obs_local // LANES, LANES)
    perturbed = (obs_value + noise[0]).reshape(grid)
    stepped, predicted, residual = forward(
        level_gain,
        depth,
        own,
        low,
        high,
        weights[0],
        land_mask,
        obs_row.reshape(grid),
        obs_col.reshape(grid),
        obs_quad.reshape(grid),
        obs_frac,
        perturbed,
    )
    grouped = lax.all_to_all(
        predicted.reshape(members, shard_size), axes, split_axis=0, concat_axis=0, tiled=True
    )
    misfit = lax.all_to_all(
        residual.reshape(members, shard_size), axes, split_axis=0, concat_axis=0, tiled=True
    )
    error_shard = lax.dynamic_slice_in_dim(obs_error, member_index * shard_size, shard_size, 0)
    anomaly = grouped - jnp.mean(grouped, axis=0, keepdims=True)
    weighted = anomaly / error_shard[None]
    gram = jnp.einsum("ko,jo->kj", weighted, anomaly, precision=highest)
    products = jnp.einsum("ko,jo->kj", weighted, misfit, precision=highest)
    gram, products = lax.psum((gram, products), ("half", "member", "tile"))
    identity = jnp.eye(members, dtype=jnp.float32)
    factor = jnp.linalg.cholesky(identity + gram / total_obs)
    coefficients = jax.scipy.linalg.cho_solve((factor, True), products / total_obs)
    combination = identity + coefficients - jnp.mean(coefficients, axis=0, keepdims=True)
    own_column = lax.dynamic_slice_in_dim(combination, member_index, 1, 1)[:, 0]
    new_weights = jnp.einsum(
        "k,krc->rc",
        own_column,
        lax.all_gather(weights, axes, axis=0, tiled=True),
        precision=highest,
    )[None]
    return (stepped[None], new_weights, misfit)


def solution(mesh):
    in_specs = (
        P(("half", "member"), None, "tile", None),
        P(("half", "member"), "tile", None),
        P("tile", None),
        P(),
        P(),
        P("tile"),
        P("tile"),
        P("tile"),
        P(None, "tile"),
        P("tile"),
        P("tile"),
        P(("half", "member"), "tile"),
    )
    out_specs = (
        P(("half", "member"), None, "tile", None),
        P(("half", "member"), "tile", None),
        P(None, ("half", "member", "tile")),
    )
    return jax.shard_map(
        on_device, mesh=mesh, in_specs=in_specs, out_specs=out_specs, check_vma=False
    )
```

time: 537 us -> 189 us (0.35)
  local copies, waits for them, and re-layouts: 375 us -> 12.4 us
  Pallas kernels: 0 us -> 25.1 us
  other arithmetic: 21.4 us -> 8.56 us
    gather x4 -> x0, local copies, waits for them, and re-layouts: 362 us -> none  [the longest x1 90.5 us: interpolate(): corner_aa = jnp.take(flat, row_index * width + col_index)]
    pallas_call x0 -> x1, Pallas kernels: none -> 25.1 us  [forward(): pl.pallas_call(step_and_sample, grid=(levels // per,), in_specs=[smem, sm...]
    reduce_sum x1 -> x0, other arithmetic: 11 us -> none  [on_device(): jnp.sum(depth[:, None, None] * stepped[0], axis=0) / math.sqrt(levels_here)]
    slice x4 -> x1, local copies, waits for them, and re-layouts: 10.8 us -> 1.3 us  [on_device(): high = lax.ppermute(own[:, :1], 'tile', down)]
    unnamed x25 -> x22, local copies, waits for them, and re-layouts: 0.21 us -> 8.92 us
  transfers between devices with their start and end apart: 5 -> 5, of which waited for: 2 -> 3; matrix products, arithmetic and copies ran while one was open for 74% -> 7% of each run, Pallas kernels for 0% -> 13%
where the time goes in v1:
time: 189 us; the launch traced here: 188 us
  blocking collectives  78.3 us (41%)
  Pallas kernels  25.1 us (13%)
  starting transfers between devices  18.9 us (10%)
  waiting for transfers between devices  17.6 us (9%)
  between operations  14.2 us (8%)
  matrix products  13.2 us (7%)
  local copies, waits for them, and re-layouts  12.4 us (7%)
  other arithmetic  8.56 us (5%)
    psum x1, blocking collectives, on_device(): gram, products = lax.psum((gram, products), ('half', 'member', 'tile'))  78.3 us
    pallas_call x1, Pallas kernels, forward(): pl.pallas_call(step_and_sample, grid=(levels // per,), in_specs=[smem, sm...  25.1 us
    dot_general x1, matrix products, on_device(): jnp.einsum('k,krc->rc', own_column, lax.all_gather(weights, axes, axis=0,...  12.3 us
    all_to_all x1, starting transfers between devices, on_device(): lax.all_to_all(residual.reshape(members, shard_size), axes, split_axis=0,...  9.01 us
    unnamed x22, local copies, waits for them, and re-layouts  8.92 us
    all_to_all x1, waiting for transfers between devices, on_device(): lax.all_to_all(predicted.reshape(members, shard_size), axes, split_axis=0...  7.04 us
    all_to_all x1, waiting for transfers between devices, on_device(): lax.all_to_all(residual.reshape(members, shard_size), axes, split_axis=0,...  6.88 us
    ppermute x1, starting transfers between devices, on_device(): low = lax.ppermute(own[:, -1:], 'tile', up)  4.37 us
  transfers between devices with their start and end apart: 5, of which 3 were waited for; matrix products, arithmetic and copies ran while one was open for 7% of the time, Pallas kernels for 13%

profile of v1, /device:TPU:1, one launch (start us, length us, event | category | flops | bytes accessed | tf_op | source)
XLA Modules:
  0.0 188.4 jit_solution(9465000781173435177)
XLA Ops:
  7.2 0.0 all-gather.2.cloned.1.call-start
  7.2 0.7 all-gather.2.cloned.1.call-update
  7.9 1.3 fusion.23
  9.2 4.4 %collective-permute-start = (f32[16,1,1024]{2,1,0:T(1,128)S(1)}, f32[16,1,1024]{2,1,0:T(1,128)S(1)}, u32[]{:S(2)}, u32[]{:S(2)}) collective-permute-start(f32[16,1,1024]{2,1,0:T(1,128)S(1)} %get-tuple-element.14), channel_id=1, source_target_pairs={{0,1},{1,2},{2,3},{3,4},{4,5},{5,6},{6,7},{8,9},{9,10},{10,11},{11... | collective-permute-start | bytes 196616 | tf_op jit(solution)/shard_map/ppermute | solution.py:212
  13.6 1.3 collective-permute-start.1
  14.9 0.9 add_bitcast_fusion.perturbed_ref
  15.8 0.0 collective-permute-done.low_ref
  15.8 3.0 %collective-permute-done.1.high_ref = f32[16,1,1024]{2,1,0:T(1,128)S(1)} collective-permute-done((f32[16,1,1024]{2,1,0:T(1,128)S(1)}, f32[16,1,1024]{2,1,0:T(1,128)S(1)}, u32[]{:S(2)}, u32[]{:S(2)}) %collective-permute-start.1) | collective-permute-done | bytes 65568 | tf_op jit(solution)/shard_map/ppermute | solution.py:213
  18.8 0.0 copy-start
  18.8 2.2 %copy-done = f32[1,16,64,1024]{3,2,1,0:T(8,128)S(1)} copy-done((f32[1,16,64,1024]{3,2,1,0:T(8,128)S(1)}, f32[1,16,64,1024]{3,2,1,0:T(8,128)}, u32[]{:S(2)}) %copy-start) | copy-done | bytes 4194328
  21.0 0.0 copy-start.1
  21.0 0.9 copy-done.1
  21.9 0.0 copy-start.2
  21.9 0.9 copy-done.2
  22.9 0.0 copy-start.3
  22.9 0.9 copy-done.3
  23.8 0.0 copy-start.4
  23.8 0.8 copy-done.4
  24.6 0.0 copy-start.5
  24.6 0.8 copy-done.5
  25.5 0.0 copy-start.6
  25.5 0.8 copy-done.6
  26.3 0.0 copy-start.7
  26.3 0.7 copy-done.7
  27.0 0.0 copy-start.8
  27.0 0.7 copy-done.8
  27.6 25.1 %step_and_sample.1 = (f32[16,64,1024]{2,1,0:T(8,128)}, f32[128,128]{1,0:T(8,128)}, f32[128,128]{1,0:T(8,128)}) custom-call(f32[16]{0:T(128)S(1)} %copy-done.7, f32[16]{0:T(128)S(1)} %copy-done.8, f32[16,64,1024]{2,1,0:T(8,128)S(1)} %bitcast.42, f32[16,1,1024]{2,1,0:T(1,128)S(1)} %collective-permute-done.low_ref, ...), custom_call_target="tpu_custom_call" | custom-call | tf_op jit(solution)/shard_map/step_and_sample/pallas_call | solution.py:165
  52.8 9.0 %all-to-all-start.1 = ((f32[32,1,512]{2,1,0:T(1,128)}), f32[32,1,512]{2,1,0:T(1,128)S(1)}, u32[]{:S(2)}, u32[]{:S(2)}) async-start(f32[32,1,512]{2,1,0:T(1,128)} %bitcast.12), calls=%async_computation.1 | async-start | bytes 131072 | tf_op jit(solution)/shard_map/all_to_all | solution.py:233
  61.8 0.8 dynamic_slice.6
  62.6 6.9 %all-to-all-done.1 = f32[32,1,512]{2,1,0:T(1,128)S(1)} async-done(((f32[32,1,512]{2,1,0:T(1,128)}), f32[32,1,512]{2,1,0:T(1,128)S(1)}, u32[]{:S(2)}, u32[]{:S(2)}) %all-to-all-start.1) | async-done | bytes 65568 | tf_op jit(solution)/shard_map/all_to_all | solution.py:233
  69.4 4.2 %all-to-all-start = ((f32[32,1,512]{2,1,0:T(1,128)}), f32[32,1,512]{2,1,0:T(1,128)S(1)}, u32[]{:S(2)}, u32[]{:S(2)}) async-start(f32[32,1,512]{2,1,0:T(1,128)} %bitcast.8), calls=%async_computation | async-start | bytes 131072 | tf_op jit(solution)/shard_map/all_to_all | solution.py:230
  73.7 0.0 copy-start.9
  73.7 7.0 %all-to-all-done = f32[32,1,512]{2,1,0:T(1,128)S(1)} async-done(((f32[32,1,512]{2,1,0:T(1,128)}), f32[32,1,512]{2,1,0:T(1,128)S(1)}, u32[]{:S(2)}, u32[]{:S(2)}) %all-to-all-start) | async-done | bytes 65568 | tf_op jit(solution)/shard_map/all_to_all | solution.py:230
  80.8 0.1 reduce_sum.18
  80.8 0.1 broadcast_divide_fusion
  80.9 0.2 fusion.2
  81.1 0.2 fusion.5
  81.3 78.3 %all-reduce = (f32[32,32]{1,0:T(8,128)S(1)}, f32[32,32]{1,0:T(8,128)S(1)}) all-reduce(f32[32,32]{1,0:T(8,128)S(1)} %fusion.2, f32[32,32]{1,0:T(8,128)S(1)} %fusion.5), channel_id=1, replica_groups=mesh['half'=2,'member'=16,'tile'=8] {'half','member','tile'}, use_global_device_ids=true, to_apply=%region_1.0 | all-reduce | flops 2048 | bytes 16384 | tf_op jit(solution)/shard_map/psum | solution.py:241
  159.6 0.1 copy.20
  159.7 2.9 %cholesky.14 = f32[32,32]{1,0:T(8,128)S(1)} custom-call(f32[32,32]{1,0:T(8,128)S(1)} %fusion.17), custom_call_target="Cholesky" | custom-call | tf_op jit(solution)/shard_map/jit(cholesky)/cholesky | solution.py:243
  162.6 0.6 compare_reduce_fusion
  163.3 0.7 fusion.10
  163.9 2.4 %custom-call.10 = f32[1,32,32]{1,2,0:T(8,128)S(1)} custom-call(f32[1,32,32]{2,1,0:T(8,128)S(1)} %fusion.10), custom_call_target="InvertDiagBlocksLowerTriangular" | custom-call | tf_op jit(solution)/shard_map/jit(_cho_solve)/triangular_solve | solution.py:244
  166.4 0.2 fusion.15
  166.6 0.3 fusion.24
  166.9 0.1 copy.28
  167.0 0.6 dynamic-slice
  167.6 0.8 fusion.12
  168.4 0.0 all-gather.2.cloned.1.call-done
  168.5 12.3 %fusion = f32[1,64,1024]{2,0,1:T(1,128)S(1)} fusion(f32[32,64,1024]{2,1,0:T(8,128)} %all-gather.2.cloned.1.call-done, f32[32]{0:T(128)S(1)} %fusion.12), kind=kOutput, calls=%fused_computation | convolution fusion | flops 25165824 | bytes 8650880 | tf_op jit(solution)/shard_map/k,krc->rc/dot_general | solution.py:247
  180.8 0.8 copy.24
  181.5 0.0 copy-done.9
  (8 shorter events, 0.1 us)
Async XLA Ops:
  7.2 161.3 %all-gather.2.cloned.1.call-start = ((), (), s32[]{:S(2)}) async-start(), calls=%async_computation.2 | async-start | bytes 8650752 | tf_op jit(solution)/shard_map/all_gather | solution.py:250
  9.2 6.6 %collective-permute-start = (f32[16,1,1024]{2,1,0:T(1,128)S(1)}, f32[16,1,1024]{2,1,0:T(1,128)S(1)}, u32[]{:S(2)}, u32[]{:S(2)}) collective-permute-start(f32[16,1,1024]{2,1,0:T(1,128)S(1)} %get-tuple-element.14), channel_id=1, source_target_pairs={{0,1},{1,2},{2,3},{3,4},{4,5},{5,6},{6,7},{8,9},{9,10},{10,11},{11... | collective-permute-start | bytes 196616 | tf_op jit(solution)/shard_map/ppermute | solution.py:212
  13.6 5.2 %collective-permute-start.1 = (f32[16,1,1024]{2,1,0:T(1,128)S(1)}, f32[16,1,1024]{2,1,0:T(1,128)S(1)}, u32[]{:S(2)}, u32[]{:S(2)}) collective-permute-start(f32[16,1,1024]{2,1,0:T(1,128)S(1)} %get-tuple-element.13), channel_id=1, source_target_pairs={{1,0},{2,1},{3,2},{4,3},{5,4},{6,5},{7,6},{9,8},{10,9},{11,10},{12... | collective-permute-start | bytes 196616 | tf_op jit(solution)/shard_map/ppermute | solution.py:213
  18.8 2.2 %copy-start = (f32[1,16,64,1024]{3,2,1,0:T(8,128)S(1)}, f32[1,16,64,1024]{3,2,1,0:T(8,128)}, u32[]{:S(2)}) copy-start(f32[1,16,64,1024]{3,2,1,0:T(8,128)} %param.12) | copy-start | bytes 12582916
  21.0 0.9 copy-start.1
  21.9 0.9 copy-start.2
  22.9 0.9 copy-start.3
  23.8 0.8 copy-start.4
  24.6 0.8 copy-start.5
  25.5 0.8 copy-start.6
  26.3 0.7 copy-start.7
  27.0 0.7 copy-start.8
  52.8 16.7 %all-to-all-start.1 = ((f32[32,1,512]{2,1,0:T(1,128)}), f32[32,1,512]{2,1,0:T(1,128)S(1)}, u32[]{:S(2)}, u32[]{:S(2)}) async-start(f32[32,1,512]{2,1,0:T(1,128)} %bitcast.12), calls=%async_computation.1 | async-start | bytes 131072 | tf_op jit(solution)/shard_map/all_to_all | solution.py:233
  69.4 11.3 %all-to-all-start = ((f32[32,1,512]{2,1,0:T(1,128)}), f32[32,1,512]{2,1,0:T(1,128)S(1)}, u32[]{:S(2)}, u32[]{:S(2)}) async-start(f32[32,1,512]{2,1,0:T(1,128)} %bitcast.8), calls=%async_computation | async-start | bytes 131072 | tf_op jit(solution)/shard_map/all_to_all | solution.py:230
  73.7 107.8 %copy-start.9 = (f32[32,1,512]{2,0,1:T(8,128)}, f32[32,1,512]{2,0,1:T(8,128)S(1)}, u32[]{:S(2)}) copy-start(f32[32,1,512]{2,0,1:T(8,128)S(1)} %copy.44) | copy-start | bytes 196612
Sparse Core Ops, SparseCore 0:
  10.6 62.8 all-gather.1

commit v2 on v1

v2 whole, which is shorter than its diff:
```python
import functools
import math

import jax
import jax.numpy as jnp
from jax import lax
from jax.experimental import pallas as pl
from jax.experimental.pallas import tpu as pltpu
from jax.sharding import PartitionSpec as P

LANES = 128
SUBLANES = 8
LEVELS_STEP = 8
OBS_STEP = 2048
KEYS = 256
VMEM_BYTES = 60 * 1024 * 1024


def pick(table, index):
    return jnp.take_along_axis(table, index, axis=1, mode="promise_in_bounds")


def step_and_sample(
    gain_ref,
    depth_ref,
    state_ref,
    low_ref,
    high_ref,
    weights_ref,
    land_ref,
    row_ref,
    col_ref,
    quad_ref,
    frac_ref,
    value_ref,
    noise_ref,
    stepped_ref,
    sampled_ref,
    diffusivity_ref,
    column_ref,
    even_ref,
    odd_ref,
):
    step = pl.program_id(0)
    steps = pl.num_programs(0)
    levels, rows, cols = state_ref.shape
    sub = lax.broadcasted_iota(jnp.int32, (SUBLANES, cols), 0)

    @pl.when(step == 0)
    def _():
        diffusivity_ref[...] = land_ref[...].astype(jnp.float32) * (
            0.24 * jax.nn.sigmoid(weights_ref[...])
        )
        column_ref[...] = jnp.zeros_like(column_ref)

    for start in range(0, rows, SUBLANES):
        here = pl.ds(start, SUBLANES)
        total = column_ref[here, :]
        diffusivity = diffusivity_ref[here, :]
        for level in range(levels):
            centre = state_ref[level, here, :]
            if start == 0:
                above_row = low_ref[level]
            else:
                above_row = state_ref[level, pl.ds(start - 1, 1), :]
            if start + SUBLANES == rows:
                below_row = high_ref[level]
            else:
                below_row = state_ref[level, pl.ds(start + SUBLANES, 1), :]
            above = jnp.where(sub == 0, above_row, pltpu.roll(centre, 1, 0))
            below = jnp.where(
                sub == SUBLANES - 1, below_row, pltpu.roll(centre, SUBLANES - 1, 0)
            )
            laplacian = (
                above
                + below
                + pltpu.roll(centre, 1, 1)
                + pltpu.roll(centre, cols - 1, 1)
                - 4.0 * centre
            )
            number = step * levels + level
            stepped = centre + gain_ref[number] * diffusivity * laplacian
            stepped_ref[level, here, :] = stepped
            total = total + depth_ref[number] * stepped
        column_ref[here, :] = total

    @pl.when(step == steps - 1)
    def _():
        scale = 1.0 / math.sqrt(levels * steps)
        lane = lax.broadcasted_iota(jnp.int32, (SUBLANES, LANES), 1)
        doubled = (2 * lane) % LANES
        first_half = lane < LANES // 2
        for block in range(cols // (2 * LANES)):
            evens, odds = [], []
            for start in range(0, rows, SUBLANES):
                here = pl.ds(start, SUBLANES)
                left = column_ref[here, pl.ds(2 * block * LANES, LANES)] * scale
                right = column_ref[here, pl.ds((2 * block + 1) * LANES, LANES)] * scale
                evens.append(jnp.where(first_half, pick(left, doubled), pick(right, doubled)))
                odds.append(
                    jnp.where(first_half, pick(left, doubled + 1), pick(right, doubled + 1))
                )
            part, key = divmod(block * LANES, KEYS)
            for ref, pieces in ((even_ref, evens), (odd_ref, odds)):
                table = jnp.concatenate(pieces, axis=0)
                coarse = table.astype(jnp.bfloat16)
                fine = (table - coarse.astype(jnp.float32)).astype(jnp.bfloat16)
                ref[pl.ds(2 * part * rows, rows), pl.ds(key, LANES)] = coarse
                ref[pl.ds((2 * part + 1) * rows, rows), pl.ds(key, LANES)] = fine

        count = OBS_STEP // LANES
        keys = lax.broadcasted_iota(jnp.int32, (KEYS, OBS_STEP), 0)
        grid_row = lax.broadcasted_iota(jnp.int32, (rows, OBS_STEP), 0)
        shard_rows = SUBLANES // 2

        def look_up(ref, at):
            chosen = jnp.where(keys == (at & (KEYS - 1)), 1.0, 0.0).astype(jnp.bfloat16)
            found = jnp.dot(ref[...], chosen, preferred_element_type=jnp.float32)
            result = found[:rows] + found[rows : 2 * rows]
            for part in range(1, cols // (2 * KEYS)):
                base = 2 * part * rows
                other = found[base : base + rows] + found[base + rows : base + 2 * rows]
                result = jnp.where(at // KEYS == part, other, result)
            return result

        def sample(i, carry):
            def line(ref):
                return jnp.concatenate(
                    [ref[pl.ds(i * count + q, 1), :] for q in range(count)], axis=1
                )

            row, col, quad = line(row_ref), line(col_ref), line(quad_ref)
            place = pl.ds(pl.multiple_of(i * OBS_STEP, OBS_STEP), OBS_STEP)
            first = frac_ref[pl.ds(0, 1), place]
            second = frac_ref[pl.ds(1, 1), place]
            row_other = row + jnp.where((quad & 1) == 1, 1, -1)
            col_other = (col + jnp.where((quad >> 1) == 1, 1, -1)) & (cols - 1)
            is_even = (col & 1) == 0
            even_at = jnp.where(is_even, col, col_other) >> 1
            odd_at = jnp.where(is_even, col_other, col) >> 1
            even_by = jnp.where(is_even, 1.0 - second, second)
            odd_by = jnp.where(is_even, second, 1.0 - second)
            along = even_by * look_up(even_ref, even_at) + odd_by * look_up(odd_ref, odd_at)
            by_row = jnp.where(
                grid_row == row, 1.0 - first, jnp.where(grid_row == row_other, first, 0.0)
            )
            predicted = jnp.sum(by_row * along, axis=0, keepdims=True)
            residual = line(value_ref) + line(noise_ref) - predicted
            for q in range(count):
                shard, inner = divmod(q, shard_rows)
                to = (i * (count // shard_rows) + shard) * SUBLANES + inner
                lanes = slice(q * LANES, (q + 1) * LANES)
                sampled_ref[pl.ds(to, 1), :] = predicted[:, lanes]
                sampled_ref[pl.ds(to + shard_rows, 1), :] = residual[:, lanes]
            return carry

        lax.fori_loop(0, row_ref.shape[0] // count, sample, 0)


def forward(level_gain, depth, state, low, high, weights, land_mask, obs):
    levels, rows, cols = state.shape
    per = LEVELS_STEP
    members_rows = 2 * obs[0].shape[0]

    def whole(shape):
        return pl.BlockSpec(shape, lambda i: (0,) * len(shape))

    smem = pl.BlockSpec(memory_space=pltpu.SMEM)
    halo = pl.BlockSpec((per, 1, cols), lambda i: (i, 0, 0))
    field = pl.BlockSpec((per, rows, cols), lambda i: (i, 0, 0))
    table = pltpu.VMEM((2 * rows * cols // (2 * KEYS), KEYS), jnp.bfloat16)
    return pl.pallas_call(
        step_and_sample,
        grid=(levels // per,),
        in_specs=[smem, smem, field, halo, halo]
        + [whole(array.shape) for array in (weights, land_mask, *obs)],
        out_specs=[field, whole((members_rows, LANES))],
        out_shape=[
            jax.ShapeDtypeStruct(state.shape, jnp.float32),
            jax.ShapeDtypeStruct((members_rows, LANES), jnp.float32),
        ],
        scratch_shapes=[
            pltpu.VMEM((rows, cols), jnp.float32),
            pltpu.VMEM((rows, cols), jnp.float32),
            table,
            table,
        ],
        compiler_params=pltpu.CompilerParams(vmem_limit_bytes=VMEM_BYTES),
        name="step_and_sample",
    )(level_gain, depth, state, low, high, weights, land_mask, *obs)


def shard_products(index_ref, grouped_ref, error_ref, misfit_ref, products_ref):
    members = misfit_ref.shape[0]
    half_rows = SUBLANES // 2

    def lines(first):
        return jnp.concatenate(
            [grouped_ref[pl.ds(first + q, members, stride=SUBLANES), :] for q in range(half_rows)],
            axis=1,
        )

    grouped, misfit = lines(0), lines(half_rows)
    misfit_ref[...] = misfit
    error = jnp.concatenate(
        [error_ref[pl.ds(index_ref[0] * half_rows + q, 1), :] for q in range(half_rows)], axis=1
    )
    anomaly = grouped - jnp.sum(grouped, axis=0, keepdims=True) * (1.0 / members)
    weighted = anomaly / error
    blank = jnp.zeros((LANES - 2 * members, grouped.shape[1]), jnp.float32)
    products_ref[...] = lax.dot_general(
        weighted,
        jnp.concatenate([anomaly, misfit, blank], axis=0),
        (((1,), (1,)), ((), ())),
        precision=lax.Precision.HIGHEST,
        preferred_element_type=jnp.float32,
    )


def solve_and_combine(
    total_obs, index_ref, *refs
):
    *product_refs, weights_ref, out_ref, held_ref, by_ref, sems = refs
    members, rows, _ = weights_ref.shape
    parts = sems.shape[0]
    part_rows = rows // parts

    def copy(part):
        here = pl.ds(part * part_rows, part_rows)
        return pltpu.make_async_copy(
            weights_ref.at[:, here, :], held_ref.at[:, here, :], sems.at[part]
        )

    for part in range(parts):
        copy(part).start()

    row = lax.broadcasted_iota(jnp.int32, (members, LANES), 0)
    lane = lax.broadcasted_iota(jnp.int32, (members, LANES), 1)
    system = product_refs[0][...]
    for ref in product_refs[1:]:
        system = system + ref[...]
    system = system / total_obs + jnp.where(row == lane, 1.0, 0.0)
    for k in range(members):
        pivot_row = system[k : k + 1, :] * (1.0 / system[k : k + 1, k : k + 1])
        system = jnp.where(row == k, pivot_row, system - system[:, k : k + 1] * pivot_row)
    index = index_ref[0]
    own = jnp.sum(
        jnp.where(lane == members + index, system, 0.0), axis=1, keepdims=True
    )
    own = own - jnp.sum(own, axis=0, keepdims=True) * (1.0 / members)
    by_ref[...] = jnp.where(row == index, 1.0, 0.0) + own

    for part in range(parts):
        copy(part).wait()
        for start in range(part * part_rows, (part + 1) * part_rows, SUBLANES):
            here = pl.ds(start, SUBLANES)
            total = jnp.zeros((SUBLANES, weights_ref.shape[2]), jnp.float32)
            for k in range(members):
                total = total + by_ref[pl.ds(k, 1), pl.ds(0, 1)] * held_ref[k, here, :]
            out_ref[here, :] = total


def combine(total_obs, index, products, weights):
    members, rows, cols = weights.shape
    parts = 4
    vmem = pl.BlockSpec(memory_space=pltpu.VMEM)
    return pl.pallas_call(
        functools.partial(solve_and_combine, total_obs),
        in_specs=[pl.BlockSpec(memory_space=pltpu.SMEM)]
        + [vmem] * len(products)
        + [pl.BlockSpec(memory_space=pl.ANY)],
        out_specs=vmem,
        out_shape=jax.ShapeDtypeStruct((rows, cols), jnp.float32),
        scratch_shapes=[
            pltpu.VMEM((members, rows, cols), jnp.float32),
            pltpu.VMEM((members, LANES), jnp.float32),
            pltpu.SemaphoreType.DMA((parts,)),
        ],
        compiler_params=pltpu.CompilerParams(vmem_limit_bytes=VMEM_BYTES),
        name="solve_and_combine",
    )(index, *products, weights)


def exchange(array, axis, moves):
    return [array] + [lax.ppermute(array, axis, list(enumerate(move))) for move in moves]


def on_device(
    state,
    weights,
    land_mask,
    level_gain,
    depth,
    obs_row,
    obs_col,
    obs_quad,
    obs_frac,
    obs_value,
    obs_error,
    noise,
):
    axes = ("half", "member")
    members = lax.axis_size(axes)
    index = lax.axis_index(axes).astype(jnp.int32).reshape(1)
    chips = lax.axis_size("member")
    side = math.isqrt(chips)
    tile_count = lax.axis_size("tile")
    obs_local = obs_row.shape[0]
    total_obs = obs_local * tile_count
    own = state[0]
    up = [(i, i + 1) for i in range(tile_count - 1)]
    down = [(target, source) for source, target in up]
    low = lax.ppermute(own[:, -1:], "tile", up)
    high = lax.ppermute(own[:, :1], "tile", down)
    grid = (obs_local // LANES, LANES)
    obs = (
        obs_row.reshape(grid),
        obs_col.reshape(grid),
        obs_quad.reshape(grid),
        obs_frac,
        obs_value.reshape(grid),
        noise.reshape(grid),
    )
    gathered = lax.all_gather(weights, axes, axis=0, tiled=True)
    stepped, sampled = forward(level_gain, depth, own, low, high, weights[0], land_mask, obs)
    grouped = lax.all_to_all(
        sampled.reshape(members, SUBLANES, LANES), axes, split_axis=0, concat_axis=0, tiled=True
    )
    vmem = pl.BlockSpec(memory_space=pltpu.VMEM)
    misfit, products = pl.pallas_call(
        shard_products,
        in_specs=[pl.BlockSpec(memory_space=pltpu.SMEM), vmem, vmem],
        out_specs=[vmem, vmem],
        out_shape=[
            jax.ShapeDtypeStruct((members, obs_local // members), jnp.float32),
            jax.ShapeDtypeStruct((members, LANES), jnp.float32),
        ],
        compiler_params=pltpu.CompilerParams(vmem_limit_bytes=VMEM_BYTES),
        name="shard_products",
    )(index, grouped.reshape(members * SUBLANES, LANES), obs_error.reshape(grid))

    def along_x(shift):
        return [(m // side) * side + (m % side + shift) % side for m in range(chips)]

    def along_y(shift):
        return [(m + shift * side) % chips for m in range(chips)]

    def along_z(shift):
        return [(t + shift) % tile_count for t in range(tile_count)]

    products = sum(exchange(products, "half", [(1, 0)]))
    products = sum(exchange(products, "member", [along_x(s) for s in (1, 3, 2)]))
    products = sum(exchange(products, "member", [along_y(s) for s in (1, 3, 2)]))
    products = sum(exchange(products, "tile", [along_z(1)]))
    products = exchange(products, "tile", [along_z(s) for s in (2, 6, 4)])
    new_weights = combine(total_obs, index, products, gathered)
    return (stepped[None], new_weights[None], misfit)


def solution(mesh):
    in_specs = (
        P(("half", "member"), None, "tile", None),
        P(("half", "member"), "tile", None),
        P("tile", None),
        P(),
        P(),
        P("tile"),
        P("tile"),
        P("tile"),
        P(None, "tile"),
        P("tile"),
        P("tile"),
        P(("half", "member"), "tile"),
    )
    out_specs = (
        P(("half", "member"), None, "tile", None),
        P(("half", "member"), "tile", None),
        P(None, ("half", "member", "tile")),
    )
    return jax.shard_map(
        on_device, mesh=mesh, in_specs=in_specs, out_specs=out_specs, check_vma=False
    )
```

time: 189 us -> 100 us (0.53)
  the two profiles are of different devices: /device:TPU:1 before, /device:TPU:32 now
where the time goes in v2:
time: 100 us
  starting transfers between devices  30.3 us (30%)
  waiting for transfers between devices  30.3 us (30%)
  Pallas kernels  21.3 us (21%)
  between operations  14.1 us (14%)
  local copies, waits for them, and re-layouts  3.17 us (3%)
    ppermute x11, starting transfers between devices, exchange(): lax.ppermute(array, axis, list(enumerate(move)))  18.9 us
    ppermute x11, waiting for transfers between devices, exchange(): lax.ppermute(array, axis, list(enumerate(move)))  17.8 us
    pallas_call x1, Pallas kernels, forward(): pl.pallas_call(step_and_sample, grid=(levels // per,), in_specs=[smem, sm...  14.4 us
    all_to_all x1, waiting for transfers between devices, on_device(): lax.all_to_all(sampled.reshape(members, SUBLANES, LANES), axes, split_axi...  7.82 us
    all_to_all x1, starting transfers between devices, on_device(): lax.all_to_all(sampled.reshape(members, SUBLANES, LANES), axes, split_axi...  5.6 us
    pallas_call x1, Pallas kernels, combine(): pl.pallas_call(functools.partial(solve_and_combine, total_obs), in_specs=...  5.15 us
    ppermute x1, waiting for transfers between devices, on_device(): low = lax.ppermute(own[:, -1:], 'tile', up)  3.76 us
    ppermute x1, starting transfers between devices, on_device(): high = lax.ppermute(own[:, :1], 'tile', down)  3.75 us
  transfers between devices with their start and end apart: 15, of which 12 were waited for; matrix products, arithmetic and copies ran while one was open for 2% of the time, Pallas kernels for 16%

profile of v2, /device:TPU:32, one launch (start us, length us, event | category | flops | bytes accessed | tf_op | source)
XLA Modules:
  0.0 100.0 jit_solution(13658870107605321847)
XLA Ops:
  7.2 0.0 all-gather.2.cloned.1.call-start
  7.2 0.7 all-gather.2.cloned.1.call-update
  7.9 1.3 %fusion = (f32[16,1,1024]{2,1,0:T(1,128)S(1)}, f32[16,1,1024]{2,1,0:T(1,128)S(1)}) fusion(f32[16,64,1024]{2,1,0:T(8,128)} %bitcast.13), kind=kLoop, calls=%fused_computation.2 | loop fusion | bytes 262144 | tf_op jit(solution)/shard_map/slice | solution.py:314
  9.2 3.8 %collective-permute-start.1 = (f32[16,1,1024]{2,1,0:T(1,128)S(1)}, f32[16,1,1024]{2,1,0:T(1,128)S(1)}, u32[]{:S(2)}, u32[]{:S(2)}) collective-permute-start(f32[16,1,1024]{2,1,0:T(1,128)S(1)} %get-tuple-element.11), channel_id=1, source_target_pairs={{1,0},{2,1},{3,2},{4,3},{5,4},{6,5},{7,6},{9,8},{10,9},{11,10},{12... | collective-permute-start | bytes 196616 | tf_op jit(solution)/shard_map/ppermute | solution.py:314
  13.0 2.1 %collective-permute-start = (f32[16,1,1024]{2,1,0:T(1,128)S(1)}, f32[16,1,1024]{2,1,0:T(1,128)S(1)}, u32[]{:S(2)}, u32[]{:S(2)}) collective-permute-start(f32[16,1,1024]{2,1,0:T(1,128)S(1)} %get-tuple-element.12), channel_id=1, source_target_pairs={{0,1},{1,2},{2,3},{3,4},{4,5},{5,6},{6,7},{8,9},{9,10},{10,11},{11... | collective-permute-start | bytes 196616 | tf_op jit(solution)/shard_map/ppermute | solution.py:313
  15.1 0.3 collective-permute-done.1.high_ref
  15.4 0.0 copy-start.1
  15.4 3.8 %collective-permute-done.low_ref = f32[16,1,1024]{2,1,0:T(1,128)S(1)} collective-permute-done((f32[16,1,1024]{2,1,0:T(1,128)S(1)}, f32[16,1,1024]{2,1,0:T(1,128)S(1)}, u32[]{:S(2)}, u32[]{:S(2)}) %collective-permute-start) | collective-permute-done | bytes 65568 | tf_op jit(solution)/shard_map/ppermute | solution.py:313
  19.1 0.0 copy-start.2
  19.1 0.0 copy-done.1
  19.1 0.6 copy-done.2
  19.8 14.4 %step_and_sample.1 = (f32[16,64,1024]{2,1,0:T(8,128)}, f32[256,128]{1,0:T(8,128)}) custom-call(f32[16]{0:T(128)} %gain_ref.1, f32[16]{0:T(128)} %depth_ref.1, f32[16,64,1024]{2,1,0:T(8,128)} %bitcast.14, f32[16,1,1024]{2,1,0:T(1,128)} %copy-done.2, f32[16,1,1024]{2,1,0:T(1,128)} %copy-done.1, f32[64,1024]{1,0:T(8,128)} %bitcast.15, s32[64,1024]{1,0:T(8,128)} %land_ref.1, ...), custom_call_target="tpu_custom_call" | custom-call | tf_op jit(solution)/shard_map/step_and_sample/pallas_call | solution.py:172
  34.1 5.6 %all-to-all-start = ((f32[32,8,128]{2,1,0:T(8,128)}), f32[32,8,128]{2,1,0:T(8,128)S(1)}, u32[]{:S(2)}, u32[]{:S(2)}) async-start(f32[32,8,128]{2,1,0:T(8,128)} %bitcast.18), calls=%async_computation | async-start | bytes 262144 | tf_op jit(solution)/shard_map/all_to_all | solution.py:326
  39.7 7.8 %all-to-all-done = f32[32,8,128]{2,1,0:T(8,128)S(1)} async-done(((f32[32,8,128]{2,1,0:T(8,128)}), f32[32,8,128]{2,1,0:T(8,128)S(1)}, u32[]{:S(2)}, u32[]{:S(2)}) %all-to-all-start) | async-done | bytes 131104 | tf_op jit(solution)/shard_map/all_to_all | solution.py:326
  47.6 0.0 copy-start
  47.6 0.7 copy-done
  48.2 1.8 %shard_products.1 = (f32[32,512]{1,0:T(8,128)}, f32[32,128]{1,0:T(8,128)}) custom-call(s32[1]{0:T(128)} %bitcast.8.index_ref, f32[256,128]{1,0:T(8,128)} %bitcast.16, f32[128,128]{1,0:T(8,128)} %bitcast.24), custom_call_target="tpu_custom_call" | custom-call | tf_op jit(solution)/shard_map/shard_products/pallas_call | solution.py:330
  50.0 0.0 collective-permute-start.2
  50.0 1.4 %collective-permute-done.2 = f32[32,128]{1,0:T(8,128)S(1)} collective-permute-done((f32[32,128]{1,0:T(8,128)}, f32[32,128]{1,0:T(8,128)S(1)}, u32[]{:S(2)}, u32[]{:S(2)}) %collective-permute-start.2) | collective-permute-done | bytes 16416 | tf_op jit(solution)/shard_map/ppermute | solution.py:285
  51.4 0.7 add.28
  52.1 1.4 %collective-permute-start.5 = (f32[32,128]{1,0:T(8,128)S(1)}, f32[32,128]{1,0:T(8,128)S(1)}, u32[]{:S(2)}, u32[]{:S(2)}) collective-permute-start(f32[32,128]{1,0:T(8,128)S(1)} %add.28), channel_id=1, source_target_pairs={{0,16},{8,24},{16,0},{24,8},{32,48},{40,56},{48,32},{56,40},{64,80... | collective-permute-start | bytes 49160 | tf_op jit(solution)/shard_map/ppermute | solution.py:285
  53.5 1.9 %collective-permute-start.4 = (f32[32,128]{1,0:T(8,128)S(1)}, f32[32,128]{1,0:T(8,128)S(1)}, u32[]{:S(2)}, u32[]{:S(2)}) collective-permute-start(f32[32,128]{1,0:T(8,128)S(1)} %add.28), channel_id=1, source_target_pairs={{0,24},{8,0},{16,8},{24,16},{32,56},{40,32},{48,40},{56,48},{64,88... | collective-permute-start | bytes 49160 | tf_op jit(solution)/shard_map/ppermute | solution.py:285
  55.4 0.2 collective-permute-start.3
  55.5 2.1 %collective-permute-done.5 = f32[32,128]{1,0:T(8,128)S(1)} collective-permute-done((f32[32,128]{1,0:T(8,128)S(1)}, f32[32,128]{1,0:T(8,128)S(1)}, u32[]{:S(2)}, u32[]{:S(2)}) %collective-permute-start.5) | collective-permute-done | bytes 16416 | tf_op jit(solution)/shard_map/ppermute | solution.py:285
  57.7 0.0 collective-permute-done.4
  57.7 2.9 %collective-permute-done.3 = f32[32,128]{1,0:T(8,128)S(1)} collective-permute-done((f32[32,128]{1,0:T(8,128)S(1)}, f32[32,128]{1,0:T(8,128)S(1)}, u32[]{:S(2)}, u32[]{:S(2)}) %collective-permute-start.3) | collective-permute-done | bytes 16416 | tf_op jit(solution)/shard_map/ppermute | solution.py:285
  60.6 1.6 %collective-permute-start.8 = (f32[32,128]{1,0:T(8,128)S(1)}, f32[32,128]{1,0:T(8,128)S(1)}, u32[]{:S(2)}, u32[]{:S(2)}) collective-permute-start(f32[32,128]{1,0:T(8,128)S(1)} %add_add_fusion.1), channel_id=1, source_target_pairs={{0,64},{8,72},{16,80},{24,88},{32,96},{40,104},{48,112},{56,120},{... | collective-permute-start | bytes 49160 | tf_op jit(solution)/shard_map/ppermute | solution.py:285
  62.2 1.6 %collective-permute-start.7 = (f32[32,128]{1,0:T(8,128)S(1)}, f32[32,128]{1,0:T(8,128)S(1)}, u32[]{:S(2)}, u32[]{:S(2)}) collective-permute-start(f32[32,128]{1,0:T(8,128)S(1)} %add_add_fusion.1), channel_id=1, source_target_pairs={{0,96},{8,104},{16,112},{24,120},{32,0},{40,8},{48,16},{56,24},{64... | collective-permute-start | bytes 49160 | tf_op jit(solution)/shard_map/ppermute | solution.py:285
  63.8 0.4 collective-permute-start.6
  64.2 2.0 %collective-permute-done.8 = f32[32,128]{1,0:T(8,128)S(1)} collective-permute-done((f32[32,128]{1,0:T(8,128)S(1)}, f32[32,128]{1,0:T(8,128)S(1)}, u32[]{:S(2)}, u32[]{:S(2)}) %collective-permute-start.8) | collective-permute-done | bytes 16416 | tf_op jit(solution)/shard_map/ppermute | solution.py:285
  66.2 0.1 collective-permute-done.7
  66.2 2.9 %collective-permute-done.6 = f32[32,128]{1,0:T(8,128)S(1)} collective-permute-done((f32[32,128]{1,0:T(8,128)S(1)}, f32[32,128]{1,0:T(8,128)S(1)}, u32[]{:S(2)}, u32[]{:S(2)}) %collective-permute-start.6) | collective-permute-done | bytes 16416 | tf_op jit(solution)/shard_map/ppermute | solution.py:285
  69.1 1.9 %collective-permute-start.9 = (f32[32,128]{1,0:T(8,128)S(1)}, f32[32,128]{1,0:T(8,128)S(1)}, u32[]{:S(2)}, u32[]{:S(2)}) collective-permute-start(f32[32,128]{1,0:T(8,128)S(1)} %add_add_fusion), channel_id=1, source_target_pairs={{0,1},{1,2},{2,3},{3,4},{4,5},{5,6},{6,7},{7,0},{8,9},{9,10},{10,1... | collective-permute-start | bytes 49160 | tf_op jit(solution)/shard_map/ppermute | solution.py:285
  71.0 1.8 %collective-permute-done.9 = f32[32,128]{1,0:T(8,128)S(1)} collective-permute-done((f32[32,128]{1,0:T(8,128)S(1)}, f32[32,128]{1,0:T(8,128)S(1)}, u32[]{:S(2)}, u32[]{:S(2)}) %collective-permute-start.9) | collective-permute-done | bytes 16416 | tf_op jit(solution)/shard_map/ppermute | solution.py:285
  72.8 0.0 copy-start.3
  72.8 7.0 %collective-permute-start.12 = (f32[32,128]{1,0:T(8,128)S(1)}, f32[32,128]{1,0:T(8,128)S(1)}, u32[]{:S(2)}, u32[]{:S(2)}) collective-permute-start(f32[32,128]{1,0:T(8,128)S(1)} %add.35.refs_0_), channel_id=1, source_target_pairs={{0,4},{1,5},{2,6},{3,7},{4,0},{5,1},{6,2},{7,3},{8,12},{9,13},{10,... | collective-permute-start | bytes 49160 | tf_op jit(solution)/shard_map/ppermute | solution.py:285
  79.8 1.7 %collective-permute-start.11 = (f32[32,128]{1,0:T(8,128)S(1)}, f32[32,128]{1,0:T(8,128)S(1)}, u32[]{:S(2)}, u32[]{:S(2)}) collective-permute-start(f32[32,128]{1,0:T(8,128)S(1)} %add.35.refs_0_), channel_id=1, source_target_pairs={{0,6},{1,7},{2,0},{3,1},{4,2},{5,3},{6,4},{7,5},{8,14},{9,15},{10,... | collective-permute-start | bytes 49160 | tf_op jit(solution)/shard_map/ppermute | solution.py:285
  81.5 1.2 %collective-permute-start.10 = (f32[32,128]{1,0:T(8,128)S(1)}, f32[32,128]{1,0:T(8,128)S(1)}, u32[]{:S(2)}, u32[]{:S(2)}) collective-permute-start(f32[32,128]{1,0:T(8,128)S(1)} %add.35.refs_0_), channel_id=1, source_target_pairs={{0,2},{1,3},{2,4},{3,5},{4,6},{5,7},{6,0},{7,1},{8,10},{9,11},{10,... | collective-permute-start | bytes 49160 | tf_op jit(solution)/shard_map/ppermute | solution.py:285
  82.7 0.0 collective-permute-done.12.refs_3_
  82.7 0.0 copy-start.4
  82.7 1.7 %collective-permute-done.11.refs_2_ = f32[32,128]{1,0:T(8,128)S(1)} collective-permute-done((f32[32,128]{1,0:T(8,128)S(1)}, f32[32,128]{1,0:T(8,128)S(1)}, u32[]{:S(2)}, u32[]{:S(2)}) %collective-permute-start.11) | collective-permute-done | bytes 16416 | tf_op jit(solution)/shard_map/ppermute | solution.py:285
  84.5 0.0 copy-start.5
  84.5 2.9 %collective-permute-done.10.refs_1_ = f32[32,128]{1,0:T(8,128)S(1)} collective-permute-done((f32[32,128]{1,0:T(8,128)S(1)}, f32[32,128]{1,0:T(8,128)S(1)}, u32[]{:S(2)}, u32[]{:S(2)}) %collective-permute-start.10) | collective-permute-done | bytes 16416 | tf_op jit(solution)/shard_map/ppermute | solution.py:285
  87.4 0.0 copy-start.6
  87.4 0.0 all-gather.2.cloned.1.call-done.refs_4_
  87.4 0.0 copy-done.3
  87.4 0.0 copy-done.4
  87.4 0.0 copy-done.5
  87.4 0.6 copy-done.6
  88.0 5.2 %solve_and_combine.1 = f32[64,1024]{1,0:T(8,128)} custom-call(s32[1]{0:T(128)} %bitcast.8.index_ref, f32[32,128]{1,0:T(8,128)} %copy-done.3, f32[32,128]{1,0:T(8,128)} %copy-done.6, f32[32,128]{1,0:T(8,128)} %copy-done.5, f32[32,128]{1,0:T(8,128)} %copy-done.4, f32[32,64,1024]{2,1,0:T(8,128)} %all-gather.2.cloned.1.call-done.refs_4_), custom_call_target="tpu_custom_call" | custom-call | tf_op jit(solution)/shard_map/solve_and_combine/pallas_call | solution.py:267
  (3 shorter events, 0.0 us)
Async XLA Ops:
  7.2 80.2 %all-gather.2.cloned.1.call-start = ((), (), s32[]{:S(2)}) async-start(), calls=%async_computation.1 | async-start | bytes 8650752 | tf_op jit(solution)/shard_map/all_gather | solution.py:324
  9.2 6.2 %collective-permute-start.1 = (f32[16,1,1024]{2,1,0:T(1,128)S(1)}, f32[16,1,1024]{2,1,0:T(1,128)S(1)}, u32[]{:S(2)}, u32[]{:S(2)}) collective-permute-start(f32[16,1,1024]{2,1,0:T(1,128)S(1)} %get-tuple-element.11), channel_id=1, source_target_pairs={{1,0},{2,1},{3,2},{4,3},{5,4},{6,5},{7,6},{9,8},{10,9},{11,10},{12... | collective-permute-start | bytes 196616 | tf_op jit(solution)/shard_map/ppermute | solution.py:314
  13.0 6.2 %collective-permute-start = (f32[16,1,1024]{2,1,0:T(1,128)S(1)}, f32[16,1,1024]{2,1,0:T(1,128)S(1)}, u32[]{:S(2)}, u32[]{:S(2)}) collective-permute-start(f32[16,1,1024]{2,1,0:T(1,128)S(1)} %get-tuple-element.12), channel_id=1, source_target_pairs={{0,1},{1,2},{2,3},{3,4},{4,5},{5,6},{6,7},{8,9},{9,10},{10,11},{11... | collective-permute-start | bytes 196616 | tf_op jit(solution)/shard_map/ppermute | solution.py:313
  15.4 3.8 %copy-start.1 = (f32[16,1,1024]{2,1,0:T(1,128)}, f32[16,1,1024]{2,1,0:T(1,128)S(1)}, u32[]{:S(2)}) copy-start(f32[16,1,1024]{2,1,0:T(1,128)S(1)} %collective-permute-done.1.high_ref) | copy-start | bytes 196612
  19.1 0.6 copy-start.2
  34.1 13.4 %all-to-all-start = ((f32[32,8,128]{2,1,0:T(8,128)}), f32[32,8,128]{2,1,0:T(8,128)S(1)}, u32[]{:S(2)}, u32[]{:S(2)}) async-start(f32[32,8,128]{2,1,0:T(8,128)} %bitcast.18), calls=%async_computation | async-start | bytes 262144 | tf_op jit(solution)/shard_map/all_to_all | solution.py:326
  47.6 0.7 copy-start
  50.0 1.4 %collective-permute-start.2 = (f32[32,128]{1,0:T(8,128)}, f32[32,128]{1,0:T(8,128)S(1)}, u32[]{:S(2)}, u32[]{:S(2)}) collective-permute-start(f32[32,128]{1,0:T(8,128)} %get-tuple-element.9), channel_id=1, source_target_pairs={{0,128},{128,0},{1,129},{129,1},{2,130},{130,2},{3,131},{131,3},{4... | collective-permute-start | bytes 49160 | tf_op jit(solution)/shard_map/ppermute | solution.py:285
  52.1 5.6 %collective-permute-start.5 = (f32[32,128]{1,0:T(8,128)S(1)}, f32[32,128]{1,0:T(8,128)S(1)}, u32[]{:S(2)}, u32[]{:S(2)}) collective-permute-start(f32[32,128]{1,0:T(8,128)S(1)} %add.28), channel_id=1, source_target_pairs={{0,16},{8,24},{16,0},{24,8},{32,48},{40,56},{48,32},{56,40},{64,80... | collective-permute-start | bytes 49160 | tf_op jit(solution)/shard_map/ppermute | solution.py:285
  53.5 4.2 %collective-permute-start.4 = (f32[32,128]{1,0:T(8,128)S(1)}, f32[32,128]{1,0:T(8,128)S(1)}, u32[]{:S(2)}, u32[]{:S(2)}) collective-permute-start(f32[32,128]{1,0:T(8,128)S(1)} %add.28), channel_id=1, source_target_pairs={{0,24},{8,0},{16,8},{24,16},{32,56},{40,32},{48,40},{56,48},{64,88... | collective-permute-start | bytes 49160 | tf_op jit(solution)/shard_map/ppermute | solution.py:285
  55.4 5.2 %collective-permute-start.3 = (f32[32,128]{1,0:T(8,128)S(1)}, f32[32,128]{1,0:T(8,128)S(1)}, u32[]{:S(2)}, u32[]{:S(2)}) collective-permute-start(f32[32,128]{1,0:T(8,128)S(1)} %add.28), channel_id=1, source_target_pairs={{0,8},{8,16},{16,24},{24,0},{32,40},{40,48},{48,56},{56,32},{64,72... | collective-permute-start | bytes 49160 | tf_op jit(solution)/shard_map/ppermute | solution.py:285
  60.6 5.6 %collective-permute-start.8 = (f32[32,128]{1,0:T(8,128)S(1)}, f32[32,128]{1,0:T(8,128)S(1)}, u32[]{:S(2)}, u32[]{:S(2)}) collective-permute-start(f32[32,128]{1,0:T(8,128)S(1)} %add_add_fusion.1), channel_id=1, source_target_pairs={{0,64},{8,72},{16,80},{24,88},{32,96},{40,104},{48,112},{56,120},{... | collective-permute-start | bytes 49160 | tf_op jit(solution)/shard_map/ppermute | solution.py:285
  62.2 4.1 %collective-permute-start.7 = (f32[32,128]{1,0:T(8,128)S(1)}, f32[32,128]{1,0:T(8,128)S(1)}, u32[]{:S(2)}, u32[]{:S(2)}) collective-permute-start(f32[32,128]{1,0:T(8,128)S(1)} %add_add_fusion.1), channel_id=1, source_target_pairs={{0,96},{8,104},{16,112},{24,120},{32,0},{40,8},{48,16},{56,24},{64... | collective-permute-start | bytes 49160 | tf_op jit(solution)/shard_map/ppermute | solution.py:285
  63.8 5.3 %collective-permute-start.6 = (f32[32,128]{1,0:T(8,128)S(1)}, f32[32,128]{1,0:T(8,128)S(1)}, u32[]{:S(2)}, u32[]{:S(2)}) collective-permute-start(f32[32,128]{1,0:T(8,128)S(1)} %add_add_fusion.1), channel_id=1, source_target_pairs={{0,32},{8,40},{16,48},{24,56},{32,64},{40,72},{48,80},{56,88},{64,... | collective-permute-start | bytes 49160 | tf_op jit(solution)/shard_map/ppermute | solution.py:285
  69.1 3.7 %collective-permute-start.9 = (f32[32,128]{1,0:T(8,128)S(1)}, f32[32,128]{1,0:T(8,128)S(1)}, u32[]{:S(2)}, u32[]{:S(2)}) collective-permute-start(f32[32,128]{1,0:T(8,128)S(1)} %add_add_fusion), channel_id=1, source_target_pairs={{0,1},{1,2},{2,3},{3,4},{4,5},{5,6},{6,7},{7,0},{8,9},{9,10},{10,1... | collective-permute-start | bytes 49160 | tf_op jit(solution)/shard_map/ppermute | solution.py:285
  72.8 14.5 %copy-start.3 = (f32[32,128]{1,0:T(8,128)}, f32[32,128]{1,0:T(8,128)S(1)}, u32[]{:S(2)}) copy-start(f32[32,128]{1,0:T(8,128)S(1)} %add.35.refs_0_) | copy-start | bytes 49156
  72.8 9.9 %collective-permute-start.12 = (f32[32,128]{1,0:T(8,128)S(1)}, f32[32,128]{1,0:T(8,128)S(1)}, u32[]{:S(2)}, u32[]{:S(2)}) collective-permute-start(f32[32,128]{1,0:T(8,128)S(1)} %add.35.refs_0_), channel_id=1, source_target_pairs={{0,4},{1,5},{2,6},{3,7},{4,0},{5,1},{6,2},{7,3},{8,12},{9,13},{10,... | collective-permute-start | bytes 49160 | tf_op jit(solution)/shard_map/ppermute | solution.py:285
  79.8 4.6 %collective-permute-start.11 = (f32[32,128]{1,0:T(8,128)S(1)}, f32[32,128]{1,0:T(8,128)S(1)}, u32[]{:S(2)}, u32[]{:S(2)}) collective-permute-start(f32[32,128]{1,0:T(8,128)S(1)} %add.35.refs_0_), channel_id=1, source_target_pairs={{0,6},{1,7},{2,0},{3,1},{4,2},{5,3},{6,4},{7,5},{8,14},{9,15},{10,... | collective-permute-start | bytes 49160 | tf_op jit(solution)/shard_map/ppermute | solution.py:285
  81.5 5.8 %collective-permute-start.10 = (f32[32,128]{1,0:T(8,128)S(1)}, f32[32,128]{1,0:T(8,128)S(1)}, u32[]{:S(2)}, u32[]{:S(2)}) collective-permute-start(f32[32,128]{1,0:T(8,128)S(1)} %add.35.refs_0_), channel_id=1, source_target_pairs={{0,2},{1,3},{2,4},{3,5},{4,6},{5,7},{6,0},{7,1},{8,10},{9,11},{10,... | collective-permute-start | bytes 49160 | tf_op jit(solution)/shard_map/ppermute | solution.py:285
  82.7 4.6 %copy-start.4 = (f32[32,128]{1,0:T(8,128)}, f32[32,128]{1,0:T(8,128)S(1)}, u32[]{:S(2)}) copy-start(f32[32,128]{1,0:T(8,128)S(1)} %collective-permute-done.12.refs_3_) | copy-start | bytes 49156
  84.5 2.9 %copy-start.5 = (f32[32,128]{1,0:T(8,128)}, f32[32,128]{1,0:T(8,128)S(1)}, u32[]{:S(2)}) copy-start(f32[32,128]{1,0:T(8,128)S(1)} %collective-permute-done.11.refs_2_) | copy-start | bytes 49156
  87.4 0.6 copy-start.6
Sparse Core Ops, SparseCore 0:
  10.6 61.2 all-gather.1

commit v3 on v2

--- a/solution.py
+++ b/solution.py
@@ -13,7 +13,9 @@
 LEVELS_STEP = 8
 OBS_STEP = 2048
 KEYS = 256
+PACK_ROWS = 3 * SUBLANES
 VMEM_BYTES = 60 * 1024 * 1024
+SMALL_VMEM_BYTES = 8 * 1024 * 1024
 
 
 def pick(table, index):
@@ -52,6 +54,12 @@
             0.24 * jax.nn.sigmoid(weights_ref[...])
         )
         column_ref[...] = jnp.zeros_like(column_ref)
+        for tile in range(rows * cols // (SUBLANES * LANES)):
+            at_row, at_col = divmod(tile * LANES, cols)
+            to = (tile // 2) * PACK_ROWS + (1 + tile % 2) * SUBLANES
+            sampled_ref[pl.ds(to, SUBLANES), :] = weights_ref[
+                pl.ds(at_row * SUBLANES, SUBLANES), pl.ds(at_col, LANES)
+            ]
 
     for start in range(0, rows, SUBLANES):
         here = pl.ds(start, SUBLANES)
@@ -148,7 +156,7 @@
             residual = line(value_ref) + line(noise_ref) - predicted
             for q in range(count):
                 shard, inner = divmod(q, shard_rows)
-                to = (i * (count // shard_rows) + shard) * SUBLANES + inner
+                to = (i * (count // shard_rows) + shard) * PACK_ROWS + inner
                 lanes = slice(q * LANES, (q + 1) * LANES)
                 sampled_ref[pl.ds(to, 1), :] = predicted[:, lanes]
                 sampled_ref[pl.ds(to + shard_rows, 1), :] = residual[:, lanes]
@@ -160,7 +168,7 @@
 def forward(level_gain, depth, state, low, high, weights, land_mask, obs):
     levels, rows, cols = state.shape
     per = LEVELS_STEP
-    members_rows = 2 * obs[0].shape[0]
+    packed = (obs[0].shape[0] // (SUBLANES // 2) * PACK_ROWS, LANES)
 
     def whole(shape):
         return pl.BlockSpec(shape, lambda i: (0,) * len(shape))
@@ -174,10 +182,10 @@
         grid=(levels // per,),
         in_specs=[smem, smem, field, halo, halo]
         + [whole(array.shape) for array in (weights, land_mask, *obs)],
-        out_specs=[field, whole((members_rows, LANES))],
+        out_specs=[field, whole(packed)],
         out_shape=[
             jax.ShapeDtypeStruct(state.shape, jnp.float32),
-            jax.ShapeDtypeStruct((members_rows, LANES), jnp.float32),
+            jax.ShapeDtypeStruct(packed, jnp.float32),
         ],
         scratch_shapes=[
             pltpu.VMEM((rows, cols), jnp.float32),
@@ -196,7 +204,7 @@
 
     def lines(first):
         return jnp.concatenate(
-            [grouped_ref[pl.ds(first + q, members, stride=SUBLANES), :] for q in range(half_rows)],
+            [grouped_ref[pl.ds(first + q, members, stride=PACK_ROWS), :] for q in range(half_rows)],
             axis=1,
         )
 
@@ -210,75 +218,56 @@
     blank = jnp.zeros((LANES - 2 * members, grouped.shape[1]), jnp.float32)
     products_ref[...] = lax.dot_general(
         weighted,
-        jnp.concatenate([anomaly, misfit, blank], axis=0),
+        jnp.concatenate([misfit, anomaly, blank], axis=0),
         (((1,), (1,)), ((), ())),
         precision=lax.Precision.HIGHEST,
         preferred_element_type=jnp.float32,
     )
 
 
-def solve_and_combine(
-    total_obs, index_ref, *refs
-):
-    *product_refs, weights_ref, out_ref, held_ref, by_ref, sems = refs
-    members, rows, _ = weights_ref.shape
-    parts = sems.shape[0]
-    part_rows = rows // parts
-
-    def copy(part):
-        here = pl.ds(part * part_rows, part_rows)
-        return pltpu.make_async_copy(
-            weights_ref.at[:, here, :], held_ref.at[:, here, :], sems.at[part]
-        )
-
-    for part in range(parts):
-        copy(part).start()
-
+def solve_and_combine(total_obs, *refs):
+    *product_refs, grouped_ref, out_ref = refs
+    members = product_refs[0].shape[0]
+    piece = PACK_ROWS - SUBLANES
     row = lax.broadcasted_iota(jnp.int32, (members, LANES), 0)
     lane = lax.broadcasted_iota(jnp.int32, (members, LANES), 1)
     system = product_refs[0][...]
     for ref in product_refs[1:]:
         system = system + ref[...]
-    system = system / total_obs + jnp.where(row == lane, 1.0, 0.0)
+    system = system / total_obs + jnp.where(row + members == lane, 1.0, 0.0)
     for k in range(members):
-        pivot_row = system[k : k + 1, :] * (1.0 / system[k : k + 1, k : k + 1])
-        system = jnp.where(row == k, pivot_row, system - system[:, k : k + 1] * pivot_row)
-    index = index_ref[0]
-    own = jnp.sum(
-        jnp.where(lane == members + index, system, 0.0), axis=1, keepdims=True
-    )
-    own = own - jnp.sum(own, axis=0, keepdims=True) * (1.0 / members)
-    by_ref[...] = jnp.where(row == index, 1.0, 0.0) + own
-
-    for part in range(parts):
-        copy(part).wait()
-        for start in range(part * part_rows, (part + 1) * part_rows, SUBLANES):
-            here = pl.ds(start, SUBLANES)
-            total = jnp.zeros((SUBLANES, weights_ref.shape[2]), jnp.float32)
-            for k in range(members):
-                total = total + by_ref[pl.ds(k, 1), pl.ds(0, 1)] * held_ref[k, here, :]
-            out_ref[here, :] = total
-
-
-def combine(total_obs, index, products, weights):
-    members, rows, cols = weights.shape
-    parts = 4
+        at = slice(members + k, members + k + 1)
+        pivot_row = system[k : k + 1, :] * (1.0 / system[k : k + 1, at])
+        system = jnp.where(row == k, pivot_row, system - system[:, at] * pivot_row)
+    coefficients = system[:, :members]
+    combination = coefficients - jnp.sum(coefficients, axis=0, keepdims=True) * (1.0 / members)
+    combination = combination + jnp.where(row == lane, 1.0, 0.0)[:, :members]
+    weights = jnp.concatenate(
+        [grouped_ref[pl.ds(SUBLANES + s, members, stride=PACK_ROWS), :] for s in range(piece)],
+        axis=1,
+    )
+    combined = lax.dot_general(
+        combination,
+        weights,
+        (((0,), (0,)), ((), ())),
+        precision=lax.Precision.HIGHEST,
+        preferred_element_type=jnp.float32,
+    )
+    for s in range(piece):
+        out_ref[pl.ds(s, members, stride=piece), :] = combined[:, s * LANES : (s + 1) * LANES]
+
+
+def combine(total_obs, products, grouped):
+    members = products[0].shape[0]
     vmem = pl.BlockSpec(memory_space=pltpu.VMEM)
     return pl.pallas_call(
         functools.partial(solve_and_combine, total_obs),
-        in_specs=[pl.BlockSpec(memory_space=pltpu.SMEM)]
-        + [vmem] * len(products)
-        + [pl.BlockSpec(memory_space=pl.ANY)],
+        in_specs=[vmem] * (len(products) + 1),
         out_specs=vmem,
-        out_shape=jax.ShapeDtypeStruct((rows, cols), jnp.float32),
-        scratch_shapes=[
-            pltpu.VMEM((members, rows, cols), jnp.float32),
-            pltpu.VMEM((members, LANES), jnp.float32),
-            pltpu.SemaphoreType.DMA((parts,)),
-        ],
-        compiler_params=pltpu.CompilerParams(vmem_limit_bytes=VMEM_BYTES),
+        out_shape=jax.ShapeDtypeStruct((members * (PACK_ROWS - SUBLANES), LANES), jnp.float32),
+        compiler_params=pltpu.CompilerParams(vmem_limit_bytes=SMALL_VMEM_BYTES),
         name="solve_and_combine",
-    )(index, *products, weights)
+    )(*products, grouped)
 
 
 def exchange(array, axis, moves):
@@ -321,11 +310,11 @@
         obs_value.reshape(grid),
         noise.reshape(grid),
     )
-    gathered = lax.all_gather(weights, axes, axis=0, tiled=True)
     stepped, sampled = forward(level_gain, depth, own, low, high, weights[0], land_mask, obs)
     grouped = lax.all_to_all(
-        sampled.reshape(members, SUBLANES, LANES), axes, split_axis=0, concat_axis=0, tiled=True
-    )
+        sampled.reshape(members, PACK_ROWS, LANES), axes, split_axis=0, concat_axis=0, tiled=True
+    )
+    grouped = grouped.reshape(members * PACK_ROWS, LANES)
     vmem = pl.BlockSpec(memory_space=pltpu.VMEM)
     misfit, products = pl.pallas_call(
         shard_products,
@@ -335,9 +324,9 @@
             jax.ShapeDtypeStruct((members, obs_local // members), jnp.float32),
             jax.ShapeDtypeStruct((members, LANES), jnp.float32),
         ],
-        compiler_params=pltpu.CompilerParams(vmem_limit_bytes=VMEM_BYTES),
+        compiler_params=pltpu.CompilerParams(vmem_limit_bytes=SMALL_VMEM_BYTES),
         name="shard_products",
-    )(index, grouped.reshape(members * SUBLANES, LANES), obs_error.reshape(grid))
+    )(index, grouped, obs_error.reshape(grid))
 
     def along_x(shift):
         return [(m // side) * side + (m % side + shift) % side for m in range(chips)]
@@ -353,8 +342,21 @@
     products = sum(exchange(products, "member", [along_y(s) for s in (1, 3, 2)]))
     products = sum(exchange(products, "tile", [along_z(1)]))
     products = exchange(products, "tile", [along_z(s) for s in (2, 6, 4)])
-    new_weights = combine(total_obs, index, products, gathered)
-    return (stepped[None], new_weights[None], misfit)
+    combined = combine(total_obs, products, grouped)
+    tiles = lax.all_to_all(
+        combined.reshape(members, PACK_ROWS - SUBLANES, LANES),
+        axes,
+        split_axis=0,
+        concat_axis=0,
+        tiled=True,
+    )
+    _, rows, cols = weights.shape
+    new_weights = (
+        tiles.reshape(rows // SUBLANES, cols // LANES, SUBLANES, LANES)
+        .transpose(0, 2, 1, 3)
+        .reshape(weights.shape)
+    )
+    return (stepped[None], new_weights, misfit)
 
 
 def solution(mesh):

time: 100 us -> 97.8 us (0.978)
  the two profiles are of different devices: /device:TPU:32 before, /device:TPU:1 now
where the time goes in v3:
time: 97.8 us; the launch traced here: 97.5 us
  starting transfers between devices  32.4 us (33%)
  waiting for transfers between devices  26.4 us (27%)
  Pallas kernels  18.3 us (19%)
  blocking collectives  17 us (17%)
  local copies, waits for them, and re-layouts  2.67 us (3%)
    ppermute x11, starting transfers between devices, exchange(): lax.ppermute(array, axis, list(enumerate(move)))  17.7 us
    all_to_all x1, blocking collectives, on_device(): lax.all_to_all(combined.reshape(members, PACK_ROWS - SUBLANES, LANES), ax...  17 us
    pallas_call x1, Pallas kernels, forward(): pl.pallas_call(step_and_sample, grid=(levels // per,), in_specs=[smem, sm...  14.6 us
    ppermute x11, waiting for transfers between devices, exchange(): lax.ppermute(array, axis, list(enumerate(move)))  12.9 us
    all_to_all x1, waiting for transfers between devices, on_device(): lax.all_to_all(sampled.reshape(members, PACK_ROWS, LANES), axes, split_ax...  9.53 us
    all_to_all x1, starting transfers between devices, on_device(): lax.all_to_all(sampled.reshape(members, PACK_ROWS, LANES), axes, split_ax...  9.04 us
    ppermute x1, starting transfers between devices, on_device(): low = lax.ppermute(own[:, -1:], 'tile', up)  4.37 us
    ppermute x1, waiting for transfers between devices, on_device(): high = lax.ppermute(own[:, :1], 'tile', down)  3.87 us
  transfers between devices with their start and end apart: 14, of which 9 were waited for; matrix products, arithmetic and copies ran while one was open for 0% of the time, Pallas kernels for 0%

profile of v3, /device:TPU:1, one launch (start us, length us, event | category | flops | bytes accessed | tf_op | source)
XLA Modules:
  0.0 97.5 jit_solution(9476805375626360367)
XLA Ops:
  0.6 0.0 copy-start
  0.6 1.3 %fusion = (f32[16,1,1024]{2,1,0:T(1,128)S(1)}, f32[16,1,1024]{2,1,0:T(1,128)S(1)}) fusion(f32[16,64,1024]{2,1,0:T(8,128)} %bitcast.22), kind=kLoop, calls=%fused_computation.2 | loop fusion | bytes 262144 | tf_op jit(solution)/shard_map/slice | solution.py:303
  2.0 4.4 %collective-permute-start = (f32[16,1,1024]{2,1,0:T(1,128)S(1)}, f32[16,1,1024]{2,1,0:T(1,128)S(1)}, u32[]{:S(2)}, u32[]{:S(2)}) collective-permute-start(f32[16,1,1024]{2,1,0:T(1,128)S(1)} %get-tuple-element.12), channel_id=1, source_target_pairs={{0,1},{1,2},{2,3},{3,4},{4,5},{5,6},{6,7},{8,9},{9,10},{10,11},{11... | collective-permute-start | bytes 196616 | tf_op jit(solution)/shard_map/ppermute | solution.py:302
  6.4 1.3 %collective-permute-start.1 = (f32[16,1,1024]{2,1,0:T(1,128)S(1)}, f32[16,1,1024]{2,1,0:T(1,128)S(1)}, u32[]{:S(2)}, u32[]{:S(2)}) collective-permute-start(f32[16,1,1024]{2,1,0:T(1,128)S(1)} %get-tuple-element.11), channel_id=1, source_target_pairs={{1,0},{2,1},{3,2},{4,3},{5,4},{6,5},{7,6},{9,8},{10,9},{11,10},{12... | collective-permute-start | bytes 196616 | tf_op jit(solution)/shard_map/ppermute | solution.py:303
  7.7 0.0 collective-permute-done.low_ref
  7.7 0.0 copy-start.1
  7.7 3.9 %collective-permute-done.1.high_ref = f32[16,1,1024]{2,1,0:T(1,128)S(1)} collective-permute-done((f32[16,1,1024]{2,1,0:T(1,128)S(1)}, f32[16,1,1024]{2,1,0:T(1,128)S(1)}, u32[]{:S(2)}, u32[]{:S(2)}) %collective-permute-start.1) | collective-permute-done | bytes 65568 | tf_op jit(solution)/shard_map/ppermute | solution.py:303
  11.6 0.0 copy-start.2
  11.6 0.0 copy-done.1
  11.6 0.6 copy-done.2
  12.2 14.6 %step_and_sample.1 = (f32[16,64,1024]{2,1,0:T(8,128)}, f32[768,128]{1,0:T(8,128)}) custom-call(f32[16]{0:T(128)} %gain_ref.1, f32[16]{0:T(128)} %depth_ref.1, f32[16,64,1024]{2,1,0:T(8,128)} %bitcast.23, f32[16,1,1024]{2,1,0:T(1,128)} %copy-done.1, f32[16,1,1024]{2,1,0:T(1,128)} %copy-done.2, f32[64,1024]{1,0:T(8,128)} %bitcast.26, s32[64,1024]{1,0:T(8,128)} %land_ref.1, ...), custom_call_target="tpu_custom_call" | custom-call | tf_op jit(solution)/shard_map/step_and_sample/pallas_call | solution.py:180
  26.8 9.0 %all-to-all-start = ((f32[32,24,128]{2,1,0:T(8,128)}), f32[32,24,128]{2,1,0:T(8,128)S(1)}, u32[]{:S(2)}, u32[]{:S(2)}) async-start(f32[32,24,128]{2,1,0:T(8,128)} %bitcast.25), calls=%async_computation | async-start | bytes 786432 | tf_op jit(solution)/shard_map/all_to_all | solution.py:314
  35.8 9.5 %all-to-all-done = f32[32,24,128]{2,1,0:T(8,128)S(1)} async-done(((f32[32,24,128]{2,1,0:T(8,128)}), f32[32,24,128]{2,1,0:T(8,128)S(1)}, u32[]{:S(2)}, u32[]{:S(2)}) %all-to-all-start) | async-done | bytes 393248 | tf_op jit(solution)/shard_map/all_to_all | solution.py:314
  45.4 0.0 copy-done
  45.4 0.7 shard_products.1
  46.0 1.2 %collective-permute-start.2 = (f32[32,128]{1,0:T(8,128)S(1)}, f32[32,128]{1,0:T(8,128)S(1)}, u32[]{:S(2)}, u32[]{:S(2)}) collective-permute-start(f32[32,128]{1,0:T(8,128)S(1)} %get-tuple-element.9), channel_id=1, source_target_pairs={{0,128},{128,0},{1,129},{129,1},{2,130},{130,2},{3,131},{131,3},{4... | collective-permute-start | bytes 49160 | tf_op jit(solution)/shard_map/ppermute | solution.py:274
  47.2 0.8 collective-permute-done.2
  48.1 0.1 collective-permute-start.3
  48.2 2.5 %collective-permute-start.4 = (f32[32,128]{1,0:T(8,128)S(1)}, f32[32,128]{1,0:T(8,128)S(1)}, u32[]{:S(2)}, u32[]{:S(2)}) collective-permute-start(f32[32,128]{1,0:T(8,128)S(1)} %add.28), channel_id=1, source_target_pairs={{0,24},{8,0},{16,8},{24,16},{32,56},{40,32},{48,40},{56,48},{64,88... | collective-permute-start | bytes 49160 | tf_op jit(solution)/shard_map/ppermute | solution.py:274
  50.8 0.0 collective-permute-start.5
  50.8 1.1 %collective-permute-done.3 = f32[32,128]{1,0:T(8,128)S(1)} collective-permute-done((f32[32,128]{1,0:T(8,128)S(1)}, f32[32,128]{1,0:T(8,128)S(1)}, u32[]{:S(2)}, u32[]{:S(2)}) %collective-permute-start.3) | collective-permute-done | bytes 16416 | tf_op jit(solution)/shard_map/ppermute | solution.py:274
  51.9 0.0 collective-permute-done.4
  51.9 3.0 %collective-permute-done.5 = f32[32,128]{1,0:T(8,128)S(1)} collective-permute-done((f32[32,128]{1,0:T(8,128)S(1)}, f32[32,128]{1,0:T(8,128)S(1)}, u32[]{:S(2)}, u32[]{:S(2)}) %collective-permute-start.5) | collective-permute-done | bytes 16416 | tf_op jit(solution)/shard_map/ppermute | solution.py:274
  54.9 0.3 collective-permute-start.6
  55.2 2.3 %collective-permute-start.7 = (f32[32,128]{1,0:T(8,128)S(1)}, f32[32,128]{1,0:T(8,128)S(1)}, u32[]{:S(2)}, u32[]{:S(2)}) collective-permute-start(f32[32,128]{1,0:T(8,128)S(1)} %add_add_fusion.1), channel_id=1, source_target_pairs={{0,96},{8,104},{16,112},{24,120},{32,0},{40,8},{48,16},{56,24},{64... | collective-permute-start | bytes 49160 | tf_op jit(solution)/shard_map/ppermute | solution.py:274
  57.5 0.1 collective-permute-start.8
  57.6 1.0 %collective-permute-done.6 = f32[32,128]{1,0:T(8,128)S(1)} collective-permute-done((f32[32,128]{1,0:T(8,128)S(1)}, f32[32,128]{1,0:T(8,128)S(1)}, u32[]{:S(2)}, u32[]{:S(2)}) %collective-permute-start.6) | collective-permute-done | bytes 16416 | tf_op jit(solution)/shard_map/ppermute | solution.py:274
  58.7 0.0 collective-permute-done.7
  58.7 3.0 %collective-permute-done.8 = f32[32,128]{1,0:T(8,128)S(1)} collective-permute-done((f32[32,128]{1,0:T(8,128)S(1)}, f32[32,128]{1,0:T(8,128)S(1)}, u32[]{:S(2)}, u32[]{:S(2)}) %collective-permute-start.8) | collective-permute-done | bytes 16416 | tf_op jit(solution)/shard_map/ppermute | solution.py:274
  61.6 1.6 %collective-permute-start.9 = (f32[32,128]{1,0:T(8,128)S(1)}, f32[32,128]{1,0:T(8,128)S(1)}, u32[]{:S(2)}, u32[]{:S(2)}) collective-permute-start(f32[32,128]{1,0:T(8,128)S(1)} %add_add_fusion), channel_id=1, source_target_pairs={{0,1},{1,2},{2,3},{3,4},{4,5},{5,6},{6,7},{7,0},{8,9},{9,10},{10,1... | collective-permute-start | bytes 49160 | tf_op jit(solution)/shard_map/ppermute | solution.py:274
  63.3 2.8 %collective-permute-done.9 = f32[32,128]{1,0:T(8,128)S(1)} collective-permute-done((f32[32,128]{1,0:T(8,128)S(1)}, f32[32,128]{1,0:T(8,128)S(1)}, u32[]{:S(2)}, u32[]{:S(2)}) %collective-permute-start.9) | collective-permute-done | bytes 16416 | tf_op jit(solution)/shard_map/ppermute | solution.py:274
  66.1 3.5 %collective-permute-start.10 = (f32[32,128]{1,0:T(8,128)S(1)}, f32[32,128]{1,0:T(8,128)S(1)}, u32[]{:S(2)}, u32[]{:S(2)}) collective-permute-start(f32[32,128]{1,0:T(8,128)S(1)} %add.35.refs_0_), channel_id=1, source_target_pairs={{0,2},{1,3},{2,4},{3,5},{4,6},{5,7},{6,0},{7,1},{8,10},{9,11},{10,... | collective-permute-start | bytes 49160 | tf_op jit(solution)/shard_map/ppermute | solution.py:274
  69.5 0.2 collective-permute-start.11
  69.7 5.8 %collective-permute-start.12 = (f32[32,128]{1,0:T(8,128)S(1)}, f32[32,128]{1,0:T(8,128)S(1)}, u32[]{:S(2)}, u32[]{:S(2)}) collective-permute-start(f32[32,128]{1,0:T(8,128)S(1)} %add.35.refs_0_), channel_id=1, source_target_pairs={{0,4},{1,5},{2,6},{3,7},{4,0},{5,1},{6,2},{7,3},{8,12},{9,13},{10,... | collective-permute-start | bytes 49160 | tf_op jit(solution)/shard_map/ppermute | solution.py:274
  75.5 0.0 collective-permute-done.10.refs_1_
  75.5 0.0 collective-permute-done.11.refs_2_
  75.5 1.2 %collective-permute-done.12.refs_3_ = f32[32,128]{1,0:T(8,128)S(1)} collective-permute-done((f32[32,128]{1,0:T(8,128)S(1)}, f32[32,128]{1,0:T(8,128)S(1)}, u32[]{:S(2)}, u32[]{:S(2)}) %collective-permute-start.12) | collective-permute-done | bytes 16416 | tf_op jit(solution)/shard_map/ppermute | solution.py:274
  76.7 3.1 %solve_and_combine.1 = f32[512,128]{1,0:T(8,128)S(1)} custom-call(f32[32,128]{1,0:T(8,128)S(1)} %add.35.refs_0_, f32[32,128]{1,0:T(8,128)S(1)} %collective-permute-done.10.refs_1_, f32[32,128]{1,0:T(8,128)S(1)} %collective-permute-done.11.refs_2_, f32[32,128]{1,0:T(8,128)S(1)} %collective-permute-done.12.refs_3_, f32[768,128]{1,0:T(8,128)S(1)} %bitcast.19), custom_call_target="tpu_custom_call" | custom-call | tf_op jit(solution)/shard_map/solve_and_combine/pallas_call | solution.py:263
  79.8 17.0 %all_to_all.10 = f32[32,16,128]{2,1,0:T(8,128)S(1)} all-to-all(f32[32,16,128]{2,1,0:T(8,128)S(1)} %bitcast.20), channel_id=1, replica_groups=mesh['half'=2,'member'=16,'tile'=8] {'half','member'}, dimensions={0} | all-to-all | bytes 524288 | tf_op jit(solution)/shard_map/all_to_all | solution.py:346
  96.8 0.7 copy.16
  (4 shorter events, 0.0 us)
Async XLA Ops:
  0.6 44.7 %copy-start = (f32[16384]{0:T(1024)S(1)}, f32[16384]{0:T(1024)}, u32[]{:S(2)}) copy-start(f32[16384]{0:T(1024)} %param.22) | copy-start | bytes 196612
  2.0 5.7 %collective-permute-start = (f32[16,1,1024]{2,1,0:T(1,128)S(1)}, f32[16,1,1024]{2,1,0:T(1,128)S(1)}, u32[]{:S(2)}, u32[]{:S(2)}) collective-permute-start(f32[16,1,1024]{2,1,0:T(1,128)S(1)} %get-tuple-element.12), channel_id=1, source_target_pairs={{0,1},{1,2},{2,3},{3,4},{4,5},{5,6},{6,7},{8,9},{9,10},{10,11},{11... | collective-permute-start | bytes 196616 | tf_op jit(solution)/shard_map/ppermute | solution.py:302
  6.4 5.2 %collective-permute-start.1 = (f32[16,1,1024]{2,1,0:T(1,128)S(1)}, f32[16,1,1024]{2,1,0:T(1,128)S(1)}, u32[]{:S(2)}, u32[]{:S(2)}) collective-permute-start(f32[16,1,1024]{2,1,0:T(1,128)S(1)} %get-tuple-element.11), channel_id=1, source_target_pairs={{1,0},{2,1},{3,2},{4,3},{5,4},{6,5},{7,6},{9,8},{10,9},{11,10},{12... | collective-permute-start | bytes 196616 | tf_op jit(solution)/shard_map/ppermute | solution.py:303
  7.7 3.9 %copy-start.1 = (f32[16,1,1024]{2,1,0:T(1,128)}, f32[16,1,1024]{2,1,0:T(1,128)S(1)}, u32[]{:S(2)}) copy-start(f32[16,1,1024]{2,1,0:T(1,128)S(1)} %collective-permute-done.low_ref) | copy-start | bytes 196612
  11.6 0.6 copy-start.2
  26.8 18.6 %all-to-all-start = ((f32[32,24,128]{2,1,0:T(8,128)}), f32[32,24,128]{2,1,0:T(8,128)S(1)}, u32[]{:S(2)}, u32[]{:S(2)}) async-start(f32[32,24,128]{2,1,0:T(8,128)} %bitcast.25), calls=%async_computation | async-start | bytes 786432 | tf_op jit(solution)/shard_map/all_to_all | solution.py:314
  46.0 2.1 %collective-permute-start.2 = (f32[32,128]{1,0:T(8,128)S(1)}, f32[32,128]{1,0:T(8,128)S(1)}, u32[]{:S(2)}, u32[]{:S(2)}) collective-permute-start(f32[32,128]{1,0:T(8,128)S(1)} %get-tuple-element.9), channel_id=1, source_target_pairs={{0,128},{128,0},{1,129},{129,1},{2,130},{130,2},{3,131},{131,3},{4... | collective-permute-start | bytes 49160 | tf_op jit(solution)/shard_map/ppermute | solution.py:274
  48.1 3.8 %collective-permute-start.3 = (f32[32,128]{1,0:T(8,128)S(1)}, f32[32,128]{1,0:T(8,128)S(1)}, u32[]{:S(2)}, u32[]{:S(2)}) collective-permute-start(f32[32,128]{1,0:T(8,128)S(1)} %add.28), channel_id=1, source_target_pairs={{0,8},{8,16},{16,24},{24,0},{32,40},{40,48},{48,56},{56,32},{64,72... | collective-permute-start | bytes 49160 | tf_op jit(solution)/shard_map/ppermute | solution.py:274
  48.2 3.7 %collective-permute-start.4 = (f32[32,128]{1,0:T(8,128)S(1)}, f32[32,128]{1,0:T(8,128)S(1)}, u32[]{:S(2)}, u32[]{:S(2)}) collective-permute-start(f32[32,128]{1,0:T(8,128)S(1)} %add.28), channel_id=1, source_target_pairs={{0,24},{8,0},{16,8},{24,16},{32,56},{40,32},{48,40},{56,48},{64,88... | collective-permute-start | bytes 49160 | tf_op jit(solution)/shard_map/ppermute | solution.py:274
  50.8 4.1 %collective-permute-start.5 = (f32[32,128]{1,0:T(8,128)S(1)}, f32[32,128]{1,0:T(8,128)S(1)}, u32[]{:S(2)}, u32[]{:S(2)}) collective-permute-start(f32[32,128]{1,0:T(8,128)S(1)} %add.28), channel_id=1, source_target_pairs={{0,16},{8,24},{16,0},{24,8},{32,48},{40,56},{48,32},{56,40},{64,80... | collective-permute-start | bytes 49160 | tf_op jit(solution)/shard_map/ppermute | solution.py:274
  54.9 3.8 %collective-permute-start.6 = (f32[32,128]{1,0:T(8,128)S(1)}, f32[32,128]{1,0:T(8,128)S(1)}, u32[]{:S(2)}, u32[]{:S(2)}) collective-permute-start(f32[32,128]{1,0:T(8,128)S(1)} %add_add_fusion.1), channel_id=1, source_target_pairs={{0,32},{8,40},{16,48},{24,56},{32,64},{40,72},{48,80},{56,88},{64,... | collective-permute-start | bytes 49160 | tf_op jit(solution)/shard_map/ppermute | solution.py:274
  55.2 3.5 %collective-permute-start.7 = (f32[32,128]{1,0:T(8,128)S(1)}, f32[32,128]{1,0:T(8,128)S(1)}, u32[]{:S(2)}, u32[]{:S(2)}) collective-permute-start(f32[32,128]{1,0:T(8,128)S(1)} %add_add_fusion.1), channel_id=1, source_target_pairs={{0,96},{8,104},{16,112},{24,120},{32,0},{40,8},{48,16},{56,24},{64... | collective-permute-start | bytes 49160 | tf_op jit(solution)/shard_map/ppermute | solution.py:274
  57.5 4.1 %collective-permute-start.8 = (f32[32,128]{1,0:T(8,128)S(1)}, f32[32,128]{1,0:T(8,128)S(1)}, u32[]{:S(2)}, u32[]{:S(2)}) collective-permute-start(f32[32,128]{1,0:T(8,128)S(1)} %add_add_fusion.1), channel_id=1, source_target_pairs={{0,64},{8,72},{16,80},{24,88},{32,96},{40,104},{48,112},{56,120},{... | collective-permute-start | bytes 49160 | tf_op jit(solution)/shard_map/ppermute | solution.py:274
  61.6 4.5 %collective-permute-start.9 = (f32[32,128]{1,0:T(8,128)S(1)}, f32[32,128]{1,0:T(8,128)S(1)}, u32[]{:S(2)}, u32[]{:S(2)}) collective-permute-start(f32[32,128]{1,0:T(8,128)S(1)} %add_add_fusion), channel_id=1, source_target_pairs={{0,1},{1,2},{2,3},{3,4},{4,5},{5,6},{6,7},{7,0},{8,9},{9,10},{10,1... | collective-permute-start | bytes 49160 | tf_op jit(solution)/shard_map/ppermute | solution.py:274
  66.1 9.4 %collective-permute-start.10 = (f32[32,128]{1,0:T(8,128)S(1)}, f32[32,128]{1,0:T(8,128)S(1)}, u32[]{:S(2)}, u32[]{:S(2)}) collective-permute-start(f32[32,128]{1,0:T(8,128)S(1)} %add.35.refs_0_), channel_id=1, source_target_pairs={{0,2},{1,3},{2,4},{3,5},{4,6},{5,7},{6,0},{7,1},{8,10},{9,11},{10,... | collective-permute-start | bytes 49160 | tf_op jit(solution)/shard_map/ppermute | solution.py:274
  69.5 5.9 %collective-permute-start.11 = (f32[32,128]{1,0:T(8,128)S(1)}, f32[32,128]{1,0:T(8,128)S(1)}, u32[]{:S(2)}, u32[]{:S(2)}) collective-permute-start(f32[32,128]{1,0:T(8,128)S(1)} %add.35.refs_0_), channel_id=1, source_target_pairs={{0,6},{1,7},{2,0},{3,1},{4,2},{5,3},{6,4},{7,5},{8,14},{9,15},{10,... | collective-permute-start | bytes 49160 | tf_op jit(solution)/shard_map/ppermute | solution.py:274
  69.7 6.9 %collective-permute-start.12 = (f32[32,128]{1,0:T(8,128)S(1)}, f32[32,128]{1,0:T(8,128)S(1)}, u32[]{:S(2)}, u32[]{:S(2)}) collective-permute-start(f32[32,128]{1,0:T(8,128)S(1)} %add.35.refs_0_), channel_id=1, source_target_pairs={{0,4},{1,5},{2,6},{3,7},{4,0},{5,1},{6,2},{7,3},{8,12},{9,13},{10,... | collective-permute-start | bytes 49160 | tf_op jit(solution)/shard_map/ppermute | solution.py:274

commit v4 on v3

--- a/solution.py
+++ b/solution.py
@@ -216,24 +216,41 @@
     anomaly = grouped - jnp.sum(grouped, axis=0, keepdims=True) * (1.0 / members)
     weighted = anomaly / error
     blank = jnp.zeros((LANES - 2 * members, grouped.shape[1]), jnp.float32)
-    products_ref[...] = lax.dot_general(
+    products = lax.dot_general(
         weighted,
         jnp.concatenate([misfit, anomaly, blank], axis=0),
         (((1,), (1,)), ((), ())),
         precision=lax.Precision.HIGHEST,
         preferred_element_type=jnp.float32,
     )
-
-
-def solve_and_combine(total_obs, *refs):
-    *product_refs, grouped_ref, out_ref = refs
-    members = product_refs[0].shape[0]
+    half = members // 2
+    packed = jnp.concatenate(
+        [products[:half, : 2 * members], products[half:, : 2 * members]], axis=1
+    )
+    for receiver in range(products_ref.shape[0] // half):
+        products_ref[pl.ds(receiver * half, half), :] = packed
+
+
+def total_of(ref, rows):
+    total = ref[pl.ds(0, rows), :]
+    for sender in range(1, ref.shape[0] // rows):
+        total = total + ref[pl.ds(sender * rows, rows), :]
+    return total
+
+
+def sum_and_spread(rows, parts_ref, out_ref):
+    total = total_of(parts_ref, rows)
+    for receiver in range(out_ref.shape[0] // rows):
+        out_ref[pl.ds(receiver * rows, rows), :] = total
+
+
+def solve_and_combine(total_obs, parts_ref, grouped_ref, out_ref):
     piece = PACK_ROWS - SUBLANES
-    row = lax.broadcasted_iota(jnp.int32, (members, LANES), 0)
-    lane = lax.broadcasted_iota(jnp.int32, (members, LANES), 1)
-    system = product_refs[0][...]
-    for ref in product_refs[1:]:
-        system = system + ref[...]
+    members = out_ref.shape[0] // piece
+    packed = total_of(parts_ref, members // 2)
+    row = lax.broadcasted_iota(jnp.int32, (members, 2 * members), 0)
+    lane = lax.broadcasted_iota(jnp.int32, (members, 2 * members), 1)
+    system = jnp.concatenate([packed[:, : 2 * members], packed[:, 2 * members :]], axis=0)
     system = system / total_obs + jnp.where(row + members == lane, 1.0, 0.0)
     for k in range(members):
         at = slice(members + k, members + k + 1)
@@ -257,21 +274,24 @@
         out_ref[pl.ds(s, members, stride=piece), :] = combined[:, s * LANES : (s + 1) * LANES]
 
 
-def combine(total_obs, products, grouped):
-    members = products[0].shape[0]
+def local(kernel, name, out_shapes, *args):
     vmem = pl.BlockSpec(memory_space=pltpu.VMEM)
+    smem = pl.BlockSpec(memory_space=pltpu.SMEM)
     return pl.pallas_call(
-        functools.partial(solve_and_combine, total_obs),
-        in_specs=[vmem] * (len(products) + 1),
-        out_specs=vmem,
-        out_shape=jax.ShapeDtypeStruct((members * (PACK_ROWS - SUBLANES), LANES), jnp.float32),
+        kernel,
+        in_specs=[smem if array.dtype == jnp.int32 else vmem for array in args],
+        out_specs=[vmem] * len(out_shapes),
+        out_shape=[jax.ShapeDtypeStruct(shape, jnp.float32) for shape in out_shapes],
         compiler_params=pltpu.CompilerParams(vmem_limit_bytes=SMALL_VMEM_BYTES),
-        name="solve_and_combine",
-    )(*products, grouped)
-
-
-def exchange(array, axis, moves):
-    return [array] + [lax.ppermute(array, axis, list(enumerate(move))) for move in moves]
+        name=name,
+    )(*args)
+
+
+def swap(array, axes):
+    count = lax.axis_size(axes)
+    pieces = array.reshape(count, array.shape[0] // count, array.shape[1])
+    moved = lax.all_to_all(pieces, axes, split_axis=0, concat_axis=0, tiled=True)
+    return moved.reshape(array.shape)
 
 
 def on_device(
@@ -291,8 +311,6 @@
     axes = ("half", "member")
     members = lax.axis_size(axes)
     index = lax.axis_index(axes).astype(jnp.int32).reshape(1)
-    chips = lax.axis_size("member")
-    side = math.isqrt(chips)
     tile_count = lax.axis_size("tile")
     obs_local = obs_row.shape[0]
     total_obs = obs_local * tile_count
@@ -311,45 +329,30 @@
         noise.reshape(grid),
     )
     stepped, sampled = forward(level_gain, depth, own, low, high, weights[0], land_mask, obs)
-    grouped = lax.all_to_all(
-        sampled.reshape(members, PACK_ROWS, LANES), axes, split_axis=0, concat_axis=0, tiled=True
-    )
-    grouped = grouped.reshape(members * PACK_ROWS, LANES)
-    vmem = pl.BlockSpec(memory_space=pltpu.VMEM)
-    misfit, products = pl.pallas_call(
+    grouped = swap(sampled, axes)
+    packed_rows = members // 2
+    misfit, products = local(
         shard_products,
-        in_specs=[pl.BlockSpec(memory_space=pltpu.SMEM), vmem, vmem],
-        out_specs=[vmem, vmem],
-        out_shape=[
-            jax.ShapeDtypeStruct((members, obs_local // members), jnp.float32),
-            jax.ShapeDtypeStruct((members, LANES), jnp.float32),
-        ],
-        compiler_params=pltpu.CompilerParams(vmem_limit_bytes=SMALL_VMEM_BYTES),
-        name="shard_products",
-    )(index, grouped, obs_error.reshape(grid))
-
-    def along_x(shift):
-        return [(m // side) * side + (m % side + shift) % side for m in range(chips)]
-
-    def along_y(shift):
-        return [(m + shift * side) % chips for m in range(chips)]
-
-    def along_z(shift):
-        return [(t + shift) % tile_count for t in range(tile_count)]
-
-    products = sum(exchange(products, "half", [(1, 0)]))
-    products = sum(exchange(products, "member", [along_x(s) for s in (1, 3, 2)]))
-    products = sum(exchange(products, "member", [along_y(s) for s in (1, 3, 2)]))
-    products = sum(exchange(products, "tile", [along_z(1)]))
-    products = exchange(products, "tile", [along_z(s) for s in (2, 6, 4)])
-    combined = combine(total_obs, products, grouped)
-    tiles = lax.all_to_all(
-        combined.reshape(members, PACK_ROWS - SUBLANES, LANES),
-        axes,
-        split_axis=0,
-        concat_axis=0,
-        tiled=True,
-    )
+        "shard_products",
+        [(members, obs_local // members), (members * packed_rows, LANES)],
+        index,
+        grouped,
+        obs_error.reshape(grid),
+    )
+    (products,) = local(
+        functools.partial(sum_and_spread, packed_rows),
+        "sum_and_spread",
+        [(tile_count * packed_rows, LANES)],
+        swap(products, axes),
+    )
+    (combined,) = local(
+        functools.partial(solve_and_combine, total_obs),
+        "solve_and_combine",
+        [(members * (PACK_ROWS - SUBLANES), LANES)],
+        swap(products, "tile"),
+        grouped,
+    )
+    tiles = swap(combined, axes)
     _, rows, cols = weights.shape
     new_weights = (
         tiles.reshape(rows // SUBLANES, cols // LANES, SUBLANES, LANES)

time: 97.8 us -> 91.1 us (0.931)
  blocking collectives: 17 us -> 43.1 us
  starting transfers between devices: 32.4 us -> 15 us
  waiting for transfers between devices: 26.4 us -> 10.8 us
    all_to_all x1 -> x3, blocking collectives: 17 us -> 43.1 us  [swap(): lax.all_to_all(pieces, axes, split_axis=0, concat_axis=0, tiled=True)]
    ppermute x11 -> x0, starting transfers between devices: 17.7 us -> none  [exchange(): lax.ppermute(array, axis, list(enumerate(move)))]
    ppermute x11 -> x0, waiting for transfers between devices: 12.9 us -> none  [exchange(): lax.ppermute(array, axis, list(enumerate(move)))]
    ppermute x1, waiting for transfers between devices: 3.87 us -> 0.01 us  [on_device(): high = lax.ppermute(own[:, :1], 'tile', down)]
    ppermute x1, waiting for transfers between devices: 0.01 us -> 1.29 us  [on_device(): low = lax.ppermute(own[:, -1:], 'tile', up)]
    pallas_call x2 -> x3, Pallas kernels: 3.75 us -> 3.79 us  [local(): pl.pallas_call(kernel, in_specs=[smem if array.dtype == jnp.int32 else vm...]
  transfers between devices with their start and end apart: 14 -> 3, of which waited for: 9 -> 2; matrix products, arithmetic and copies ran while one was open for 0% -> 0% of each run, Pallas kernels for 0% -> 0%
where the time goes in v4:
time: 91.1 us; the launch traced here: 90.7 us
  blocking collectives  43.1 us (47%)
  Pallas kernels  18.4 us (20%)
  starting transfers between devices  15 us (16%)
  waiting for transfers between devices  10.8 us (12%)
  local copies, waits for them, and re-layouts  2.67 us (3%)
    all_to_all x3, blocking collectives, swap(): lax.all_to_all(pieces, axes, split_axis=0, concat_axis=0, tiled=True)  43.1 us
    pallas_call x1, Pallas kernels, forward(): pl.pallas_call(step_and_sample, grid=(levels // per,), in_specs=[smem, sm...  14.6 us
    all_to_all x1, waiting for transfers between devices, swap(): lax.all_to_all(pieces, axes, split_axis=0, concat_axis=0, tiled=True)  9.53 us
    all_to_all x1, starting transfers between devices, swap(): lax.all_to_all(pieces, axes, split_axis=0, concat_axis=0, tiled=True)  8.72 us
    ppermute x1, starting transfers between devices, on_device(): low = lax.ppermute(own[:, -1:], 'tile', up)  5 us
    pallas_call x3, Pallas kernels, local(): pl.pallas_call(kernel, in_specs=[smem if array.dtype == jnp.int32 else vm...  3.79 us
  transfers between devices with their start and end apart: 3, of which 2 were waited for; matrix products, arithmetic and copies ran while one was open for 0% of the time, Pallas kernels for 0%

profile of v4, /device:TPU:1, one launch (start us, length us, event | category | flops | bytes accessed | tf_op | source)
XLA Modules:
  0.0 90.7 jit_solution(15269963833223243996)
XLA Ops:
  0.6 0.0 copy-start
  0.6 1.3 %fusion = (f32[16,1,1024]{2,1,0:T(1,128)S(1)}, f32[16,1,1024]{2,1,0:T(1,128)S(1)}) fusion(f32[16,64,1024]{2,1,0:T(8,128)} %bitcast.30), kind=kLoop, calls=%fused_computation | loop fusion | bytes 262144 | tf_op jit(solution)/shard_map/slice | solution.py:321
  2.0 1.3 %collective-permute-start.1 = (f32[16,1,1024]{2,1,0:T(1,128)S(1)}, f32[16,1,1024]{2,1,0:T(1,128)S(1)}, u32[]{:S(2)}, u32[]{:S(2)}) collective-permute-start(f32[16,1,1024]{2,1,0:T(1,128)S(1)} %get-tuple-element.11), channel_id=1, source_target_pairs={{1,0},{2,1},{3,2},{4,3},{5,4},{6,5},{7,6},{9,8},{10,9},{11,10},{12... | collective-permute-start | bytes 196616 | tf_op jit(solution)/shard_map/ppermute | solution.py:321
  3.3 5.0 %collective-permute-start = (f32[16,1,1024]{2,1,0:T(1,128)S(1)}, f32[16,1,1024]{2,1,0:T(1,128)S(1)}, u32[]{:S(2)}, u32[]{:S(2)}) collective-permute-start(f32[16,1,1024]{2,1,0:T(1,128)S(1)} %get-tuple-element.12), channel_id=1, source_target_pairs={{0,1},{1,2},{2,3},{3,4},{4,5},{5,6},{6,7},{8,9},{9,10},{10,11},{11... | collective-permute-start | bytes 196616 | tf_op jit(solution)/shard_map/ppermute | solution.py:320
  8.3 0.0 collective-permute-done.1.high_ref
  8.3 0.0 copy-start.1
  8.3 1.3 %collective-permute-done.low_ref = f32[16,1,1024]{2,1,0:T(1,128)S(1)} collective-permute-done((f32[16,1,1024]{2,1,0:T(1,128)S(1)}, f32[16,1,1024]{2,1,0:T(1,128)S(1)}, u32[]{:S(2)}, u32[]{:S(2)}) %collective-permute-start) | collective-permute-done | bytes 65568 | tf_op jit(solution)/shard_map/ppermute | solution.py:320
  9.6 0.0 copy-start.2
  9.6 0.0 copy-done.1
  9.6 0.6 copy-done.2
  10.2 14.6 %step_and_sample.1 = (f32[16,64,1024]{2,1,0:T(8,128)}, f32[768,128]{1,0:T(8,128)}) custom-call(f32[16]{0:T(128)} %gain_ref.1, f32[16]{0:T(128)} %depth_ref.1, f32[16,64,1024]{2,1,0:T(8,128)} %bitcast.31, f32[16,1,1024]{2,1,0:T(1,128)} %copy-done.2, f32[16,1,1024]{2,1,0:T(1,128)} %copy-done.1, f32[64,1024]{1,0:T(8,128)} %bitcast.34, s32[64,1024]{1,0:T(8,128)} %land_ref.1, ...), custom_call_target="tpu_custom_call" | custom-call | tf_op jit(solution)/shard_map/step_and_sample/pallas_call | solution.py:180
  24.8 8.7 %all-to-all-start = ((f32[32,24,128]{2,1,0:T(8,128)}), f32[32,24,128]{2,1,0:T(8,128)S(1)}, u32[]{:S(2)}, u32[]{:S(2)}) async-start(f32[32,24,128]{2,1,0:T(8,128)} %bitcast.33), calls=%async_computation | async-start | bytes 786432 | tf_op jit(solution)/shard_map/all_to_all | solution.py:293
  33.5 9.5 %all-to-all-done = f32[32,24,128]{2,1,0:T(8,128)S(1)} async-done(((f32[32,24,128]{2,1,0:T(8,128)}), f32[32,24,128]{2,1,0:T(8,128)S(1)}, u32[]{:S(2)}, u32[]{:S(2)}) %all-to-all-start) | async-done | bytes 393248 | tf_op jit(solution)/shard_map/all_to_all | solution.py:293
  43.1 0.0 copy-done
  43.1 0.7 shard_products.1
  43.7 12.4 %all_to_all.20 = f32[32,16,128]{2,1,0:T(8,128)S(1)} all-to-all(f32[32,16,128]{2,1,0:T(8,128)S(1)} %bitcast.27), channel_id=1, replica_groups=mesh['half'=2,'member'=16,'tile'=8] {'half','member'}, dimensions={0} | all-to-all | bytes 524288 | tf_op jit(solution)/shard_map/all_to_all | solution.py:293
  56.2 16.9 %all_to_all.21 = f32[8,16,128]{2,1,0:T(8,128)S(1)} all-to-all(f32[8,16,128]{2,1,0:T(8,128)S(1)} %bitcast.26), channel_id=1, replica_groups=mesh['half'=2,'member'=16,'tile'=8] {'tile'}, dimensions={0} | all-to-all | bytes 131072 | tf_op jit(solution)/shard_map/all_to_all | solution.py:293
  73.1 3.1 %solve_and_combine.1 = f32[512,128]{1,0:T(8,128)S(1)} custom-call(f32[128,128]{1,0:T(8,128)S(1)} %bitcast.28, f32[768,128]{1,0:T(8,128)S(1)} %bitcast.23), custom_call_target="tpu_custom_call" | custom-call | tf_op jit(solution)/shard_map/solve_and_combine/pallas_call | solution.py:280
  76.2 13.8 %all_to_all.22 = f32[32,16,128]{2,1,0:T(8,128)S(1)} all-to-all(f32[32,16,128]{2,1,0:T(8,128)S(1)} %bitcast.25), channel_id=1, replica_groups=mesh['half'=2,'member'=16,'tile'=8] {'half','member'}, dimensions={0} | all-to-all | bytes 524288 | tf_op jit(solution)/shard_map/all_to_all | solution.py:293
  90.0 0.7 copy.16
  (1 shorter events, 0.0 us)
Async XLA Ops:
  0.6 42.4 %copy-start = (f32[16384]{0:T(1024)S(1)}, f32[16384]{0:T(1024)}, u32[]{:S(2)}) copy-start(f32[16384]{0:T(1024)} %param.22) | copy-start | bytes 196612
  2.0 6.3 %collective-permute-start.1 = (f32[16,1,1024]{2,1,0:T(1,128)S(1)}, f32[16,1,1024]{2,1,0:T(1,128)S(1)}, u32[]{:S(2)}, u32[]{:S(2)}) collective-permute-start(f32[16,1,1024]{2,1,0:T(1,128)S(1)} %get-tuple-element.11), channel_id=1, source_target_pairs={{1,0},{2,1},{3,2},{4,3},{5,4},{6,5},{7,6},{9,8},{10,9},{11,10},{12... | collective-permute-start | bytes 196616 | tf_op jit(solution)/shard_map/ppermute | solution.py:321
  3.3 6.3 %collective-permute-start = (f32[16,1,1024]{2,1,0:T(1,128)S(1)}, f32[16,1,1024]{2,1,0:T(1,128)S(1)}, u32[]{:S(2)}, u32[]{:S(2)}) collective-permute-start(f32[16,1,1024]{2,1,0:T(1,128)S(1)} %get-tuple-element.12), channel_id=1, source_target_pairs={{0,1},{1,2},{2,3},{3,4},{4,5},{5,6},{6,7},{8,9},{9,10},{10,11},{11... | collective-permute-start | bytes 196616 | tf_op jit(solution)/shard_map/ppermute | solution.py:320
  8.3 1.3 %copy-start.1 = (f32[16,1,1024]{2,1,0:T(1,128)}, f32[16,1,1024]{2,1,0:T(1,128)S(1)}, u32[]{:S(2)}) copy-start(f32[16,1,1024]{2,1,0:T(1,128)S(1)} %collective-permute-done.1.high_ref) | copy-start | bytes 196612
  9.6 0.6 copy-start.2
  24.8 18.3 %all-to-all-start = ((f32[32,24,128]{2,1,0:T(8,128)}), f32[32,24,128]{2,1,0:T(8,128)S(1)}, u32[]{:S(2)}, u32[]{:S(2)}) async-start(f32[32,24,128]{2,1,0:T(8,128)} %bitcast.33), calls=%async_computation | async-start | bytes 786432 | tf_op jit(solution)/shard_map/all_to_all | solution.py:293

commit v5 on v4

v5 whole, which is shorter than its diff:
```python
import functools
import math

import jax
import jax.numpy as jnp
from jax import lax
from jax.experimental import pallas as pl
from jax.experimental.pallas import tpu as pltpu
from jax.sharding import PartitionSpec as P

LANES = 128
SUBLANES = 8
LEVELS_STEP = 4
OBS_STEP = 2048
KEYS = 256
PACK_ROWS = 3 * SUBLANES
VMEM_BYTES = 60 * 1024 * 1024
MIDDLE_VMEM_BYTES = 24 * 1024 * 1024
SMALL_VMEM_BYTES = 8 * 1024 * 1024


def pick(table, index):
    return jnp.take_along_axis(table, index, axis=1, mode="promise_in_bounds")


def diffusivity_of(land, weights):
    return land.astype(jnp.float32) * (0.24 * jax.nn.sigmoid(weights))


def laplacian_of(centre, above_row, below_row):
    cols = centre.shape[1]
    sub = lax.broadcasted_iota(jnp.int32, centre.shape, 0)
    above = jnp.where(sub == 0, above_row, pltpu.roll(centre, 1, 0))
    below = jnp.where(sub == SUBLANES - 1, below_row, pltpu.roll(centre, SUBLANES - 1, 0))
    return (
        above
        + below
        + pltpu.roll(centre, 1, 1)
        + pltpu.roll(centre, cols - 1, 1)
        - 4.0 * centre
    )


def sum_column(
    gain_ref, depth_ref, state_ref, weights_ref, land_ref, column_ref, held_ref, flow_ref, sems
):
    levels, rows, cols = state_ref.shape
    parts = sems.shape[0]
    per = levels // parts

    def copy(part):
        here = pl.ds(part * per, per)
        return pltpu.make_async_copy(state_ref.at[here], held_ref.at[here], sems.at[part])

    for part in range(parts):
        copy(part).start()
    for part in range(parts):
        copy(part).wait()
        for start in range(0, rows, SUBLANES):
            here = pl.ds(start, SUBLANES)
            column = flow = None
            for level in range(part * per, (part + 1) * per):
                weighted = depth_ref[level] * held_ref[level, here, :]
                moved = gain_ref[level] * weighted
                column = weighted if column is None else column + weighted
                flow = moved if flow is None else flow + moved
            if part > 0:
                column = column + column_ref[here, :]
                flow = flow + flow_ref[here, :]
            column_ref[here, :] = column
            flow_ref[here, :] = flow
    scale = 1.0 / math.sqrt(levels)
    blank = jnp.zeros((1, cols), jnp.float32)
    for start in range(0, rows, SUBLANES):
        here = pl.ds(start, SUBLANES)
        end = start + SUBLANES
        laplacian = laplacian_of(
            flow_ref[here, :],
            flow_ref[pl.ds(start - 1, 1), :] if start > 0 else blank,
            flow_ref[pl.ds(end, 1), :] if end < rows else blank,
        )
        diffusivity = diffusivity_of(land_ref[here, :], weights_ref[here, :])
        column_ref[here, :] = scale * (column_ref[here, :] + diffusivity * laplacian)


def has_neighbours(tile_count, tile_ref):
    tile = tile_ref[0]
    return jnp.where(tile > 0, 1.0, 0.0), jnp.where(tile < tile_count - 1, 1.0, 0.0)


def step_levels(
    tile_count, tile_ref, gain_ref, state_ref, low_ref, high_ref, weights_ref, land_ref, after_ref, stepped_ref,
    mark_ref, diffusivity_ref,
):
    del after_ref
    step = pl.program_id(0)
    levels, rows, cols = state_ref.shape
    has_low, has_high = has_neighbours(tile_count, tile_ref)

    @pl.when(step == 0)
    def _():
        diffusivity_ref[...] = diffusivity_of(land_ref[...], weights_ref[...])
        mark_ref[...] = jnp.zeros_like(mark_ref)

    for start in range(0, rows, SUBLANES):
        here = pl.ds(start, SUBLANES)
        end = start + SUBLANES
        for level in range(levels):
            centre = state_ref[level, here, :]
            laplacian = laplacian_of(
                centre,
                state_ref[level, pl.ds(start - 1, 1), :] if start > 0 else has_low * low_ref[level],
                state_ref[level, pl.ds(end, 1), :] if end < rows else has_high * high_ref[level],
            )
            factor = gain_ref[step * levels + level] * diffusivity_ref[here, :]
            stepped_ref[level, here, :] = centre + factor * laplacian


def sample_column(
    tile_count,
    tile_ref,
    gain_ref,
    depth_ref,
    column_ref,
    low_ref,
    high_ref,
    weights_ref,
    land_ref,
    row_ref,
    col_ref,
    quad_ref,
    frac_ref,
    value_ref,
    noise_ref,
    sampled_ref,
    even_ref,
    odd_ref,
):
    rows, cols = column_ref.shape
    levels = low_ref.shape[0]
    for tile in range(rows * cols // (SUBLANES * LANES)):
        at_row, at_col = divmod(tile * LANES, cols)
        to = (tile // 2) * PACK_ROWS + (1 + tile % 2) * SUBLANES
        sampled_ref[pl.ds(to, SUBLANES), :] = weights_ref[
            pl.ds(at_row * SUBLANES, SUBLANES), pl.ds(at_col, LANES)
        ]

    def edge(ref, row, factor):
        one = pl.ds(row, 1)
        flow = jnp.zeros((1, cols), jnp.float32)
        for level in range(levels):
            flow = flow + (gain_ref[level] * depth_ref[level]) * ref[level]
        diffusivity = diffusivity_of(land_ref[one, :], weights_ref[one, :])
        return (factor / math.sqrt(levels)) * diffusivity * flow

    has_low, has_high = has_neighbours(tile_count, tile_ref)
    low, high = edge(low_ref, 0, has_low), edge(high_ref, rows - 1, has_high)
    sub = lax.broadcasted_iota(jnp.int32, (SUBLANES, LANES), 0)

    def column_tile(start, first):
        tile = column_ref[pl.ds(start, SUBLANES), pl.ds(first, LANES)]
        lanes = slice(first, first + LANES)
        if start == 0:
            tile = tile + jnp.where(sub == 0, low[:, lanes], 0.0)
        if start + SUBLANES == rows:
            tile = tile + jnp.where(sub == SUBLANES - 1, high[:, lanes], 0.0)
        return tile

    lane = lax.broadcasted_iota(jnp.int32, (SUBLANES, LANES), 1)
    doubled = (2 * lane) % LANES
    first_half = lane < LANES // 2
    for block in range(cols // (2 * LANES)):
        evens, odds = [], []
        for start in range(0, rows, SUBLANES):
            left = column_tile(start, 2 * block * LANES)
            right = column_tile(start, (2 * block + 1) * LANES)
            evens.append(jnp.where(first_half, pick(left, doubled), pick(right, doubled)))
            odds.append(
                jnp.where(first_half, pick(left, doubled + 1), pick(right, doubled + 1))
            )
        part, key = divmod(block * LANES, KEYS)
        for ref, pieces in ((even_ref, evens), (odd_ref, odds)):
            table = jnp.concatenate(pieces, axis=0)
            coarse = table.astype(jnp.bfloat16)
            fine = (table - coarse.astype(jnp.float32)).astype(jnp.bfloat16)
            ref[pl.ds(2 * part * rows, rows), pl.ds(key, LANES)] = coarse
            ref[pl.ds((2 * part + 1) * rows, rows), pl.ds(key, LANES)] = fine

    count = OBS_STEP // LANES
    keys = lax.broadcasted_iota(jnp.int32, (KEYS, OBS_STEP), 0)
    grid_row = lax.broadcasted_iota(jnp.int32, (rows, OBS_STEP), 0)
    shard_rows = SUBLANES // 2

    def look_up(ref, at):
        chosen = jnp.where(keys == (at & (KEYS - 1)), 1.0, 0.0).astype(jnp.bfloat16)
        found = jnp.dot(ref[...], chosen, preferred_element_type=jnp.float32)
        result = found[:rows] + found[rows : 2 * rows]
        for part in range(1, cols // (2 * KEYS)):
            base = 2 * part * rows
            other = found[base : base + rows] + found[base + rows : base + 2 * rows]
            result = jnp.where(at // KEYS == part, other, result)
        return result

    def sample(i, carry):
        def line(ref):
            return jnp.concatenate(
                [ref[pl.ds(i * count + q, 1), :] for q in range(count)], axis=1
            )

        row, col, quad = line(row_ref), line(col_ref), line(quad_ref)
        place = pl.ds(pl.multiple_of(i * OBS_STEP, OBS_STEP), OBS_STEP)
        first = frac_ref[pl.ds(0, 1), place]
        second = frac_ref[pl.ds(1, 1), place]
        row_other = row + jnp.where((quad & 1) == 1, 1, -1)
        col_other = (col + jnp.where((quad >> 1) == 1, 1, -1)) & (cols - 1)
        is_even = (col & 1) == 0
        even_at = jnp.where(is_even, col, col_other) >> 1
        odd_at = jnp.where(is_even, col_other, col) >> 1
        even_by = jnp.where(is_even, 1.0 - second, second)
        odd_by = jnp.where(is_even, second, 1.0 - second)
        along = even_by * look_up(even_ref, even_at) + odd_by * look_up(odd_ref, odd_at)
        by_row = jnp.where(
            grid_row == row, 1.0 - first, jnp.where(grid_row == row_other, first, 0.0)
        )
        predicted = jnp.sum(by_row * along, axis=0, keepdims=True)
        residual = line(value_ref) + line(noise_ref) - predicted
        for q in range(count):
            shard, inner = divmod(q, shard_rows)
            to = (i * (count // shard_rows) + shard) * PACK_ROWS + inner
            lanes = slice(q * LANES, (q + 1) * LANES)
            sampled_ref[pl.ds(to, 1), :] = predicted[:, lanes]
            sampled_ref[pl.ds(to + shard_rows, 1), :] = residual[:, lanes]
        return carry

    lax.fori_loop(0, row_ref.shape[0] // count, sample, 0)


def forward(tile_count, tile, level_gain, depth, state, low, high, weights, land_mask, obs):
    levels, rows, cols = state.shape
    per = LEVELS_STEP
    packed = (obs[0].shape[0] // (SUBLANES // 2) * PACK_ROWS, LANES)
    smem = pl.BlockSpec(memory_space=pltpu.SMEM)
    vmem = pl.BlockSpec(memory_space=pltpu.VMEM)
    plane = pl.BlockSpec((rows, cols), lambda i: (0, 0))
    halo = pl.BlockSpec((per, 1, cols), lambda i: (i, 0, 0))
    field = pl.BlockSpec((per, rows, cols), lambda i: (i, 0, 0))
    column = pl.pallas_call(
        sum_column,
        in_specs=[smem, smem, pl.BlockSpec(memory_space=pl.ANY), vmem, vmem],
        out_specs=vmem,
        out_shape=jax.ShapeDtypeStruct((rows, cols), jnp.float32),
        scratch_shapes=[
            pltpu.VMEM(state.shape, jnp.float32),
            pltpu.VMEM((rows, cols), jnp.float32),
            pltpu.SemaphoreType.DMA((levels // per,)),
        ],
        compiler_params=pltpu.CompilerParams(vmem_limit_bytes=VMEM_BYTES),
        cost_estimate=pl.CostEstimate(
            flops=6 * state.size, bytes_accessed=4 * state.size, transcendentals=0
        ),
        name="sum_column",
    )(level_gain, depth, state, weights, land_mask)
    table = pltpu.VMEM((2 * rows * cols // (2 * KEYS), KEYS), jnp.bfloat16)
    sampled = pl.pallas_call(
        functools.partial(sample_column, tile_count),
        in_specs=[smem, smem, smem] + [vmem] * (5 + len(obs)),
        out_specs=vmem,
        out_shape=jax.ShapeDtypeStruct(packed, jnp.float32),
        scratch_shapes=[table, table],
        compiler_params=pltpu.CompilerParams(vmem_limit_bytes=MIDDLE_VMEM_BYTES),
        name="sample_column",
    )(tile, level_gain, depth, column, low, high, weights, land_mask, *obs)
    stepped, mark = pl.pallas_call(
        functools.partial(step_levels, tile_count),
        grid=(levels // per,),
        in_specs=[smem, smem, field, halo, halo, plane, plane, pl.BlockSpec(memory_space=pl.ANY)],
        out_specs=[field, pl.BlockSpec((SUBLANES, LANES), lambda i: (0, 0))],
        out_shape=[
            jax.ShapeDtypeStruct(state.shape, jnp.float32),
            jax.ShapeDtypeStruct((SUBLANES, LANES), jnp.float32),
        ],
        scratch_shapes=[pltpu.VMEM((rows, cols), jnp.float32)],
        compiler_params=pltpu.CompilerParams(vmem_limit_bytes=MIDDLE_VMEM_BYTES),
        cost_estimate=pl.CostEstimate(
            flops=10 * state.size, bytes_accessed=8 * state.size, transcendentals=0
        ),
        name="step_levels",
    )(tile, level_gain, state, low, high, weights, land_mask, sampled)
    return stepped, mark, sampled


def shard_products(index_ref, grouped_ref, error_ref, after_ref, misfit_ref, products_ref):
    del after_ref
    members = misfit_ref.shape[0]
    half_rows = SUBLANES // 2

    def lines(first):
        return jnp.concatenate(
            [grouped_ref[pl.ds(first + q, members, stride=PACK_ROWS), :] for q in range(half_rows)],
            axis=1,
        )

    grouped, misfit = lines(0), lines(half_rows)
    misfit_ref[...] = misfit
    error = jnp.concatenate(
        [error_ref[pl.ds(index_ref[0] * half_rows + q, 1), :] for q in range(half_rows)], axis=1
    )
    anomaly = grouped - jnp.sum(grouped, axis=0, keepdims=True) * (1.0 / members)
    weighted = anomaly / error
    blank = jnp.zeros((LANES - 2 * members, grouped.shape[1]), jnp.float32)
    products = lax.dot_general(
        weighted,
        jnp.concatenate([misfit, anomaly, blank], axis=0),
        (((1,), (1,)), ((), ())),
        precision=lax.Precision.HIGHEST,
        preferred_element_type=jnp.float32,
    )
    half = members // 2
    packed = jnp.concatenate(
        [products[:half, : 2 * members], products[half:, : 2 * members]], axis=1
    )
    for receiver in range(products_ref.shape[0] // half):
        products_ref[pl.ds(receiver * half, half), :] = packed


def total_of(ref, rows):
    total = ref[pl.ds(0, rows), :]
    for sender in range(1, ref.shape[0] // rows):
        total = total + ref[pl.ds(sender * rows, rows), :]
    return total


def sum_and_spread(rows, parts_ref, out_ref):
    total = total_of(parts_ref, rows)
    for receiver in range(out_ref.shape[0] // rows):
        out_ref[pl.ds(receiver * rows, rows), :] = total


def solve_and_combine(total_obs, parts_ref, grouped_ref, out_ref):
    piece = PACK_ROWS - SUBLANES
    members = out_ref.shape[0] // piece
    packed = total_of(parts_ref, members // 2)
    row = lax.broadcasted_iota(jnp.int32, (members, 2 * members), 0)
    lane = lax.broadcasted_iota(jnp.int32, (members, 2 * members), 1)
    system = jnp.concatenate([packed[:, : 2 * members], packed[:, 2 * members :]], axis=0)
    system = system / total_obs + jnp.where(row + members == lane, 1.0, 0.0)
    for k in range(members):
        at = slice(members + k, members + k + 1)
        pivot_row = system[k : k + 1, :] * (1.0 / system[k : k + 1, at])
        system = jnp.where(row == k, pivot_row, system - system[:, at] * pivot_row)
    coefficients = system[:, :members]
    combination = coefficients - jnp.sum(coefficients, axis=0, keepdims=True) * (1.0 / members)
    combination = combination + jnp.where(row == lane, 1.0, 0.0)[:, :members]
    weights = jnp.concatenate(
        [grouped_ref[pl.ds(SUBLANES + s, members, stride=PACK_ROWS), :] for s in range(piece)],
        axis=1,
    )
    combined = lax.dot_general(
        combination,
        weights,
        (((0,), (0,)), ((), ())),
        precision=lax.Precision.HIGHEST,
        preferred_element_type=jnp.float32,
    )
    for s in range(piece):
        out_ref[pl.ds(s, members, stride=piece), :] = combined[:, s * LANES : (s + 1) * LANES]


def local(kernel, name, out_shapes, *args):
    vmem = pl.BlockSpec(memory_space=pltpu.VMEM)
    smem = pl.BlockSpec(memory_space=pltpu.SMEM)
    return pl.pallas_call(
        kernel,
        in_specs=[smem if array.dtype == jnp.int32 else vmem for array in args],
        out_specs=[vmem] * len(out_shapes),
        out_shape=[jax.ShapeDtypeStruct(shape, jnp.float32) for shape in out_shapes],
        compiler_params=pltpu.CompilerParams(vmem_limit_bytes=SMALL_VMEM_BYTES),
        name=name,
    )(*args)


def swap(array, axes):
    count = lax.axis_size(axes)
    pieces = array.reshape(count, array.shape[0] // count, array.shape[1])
    moved = lax.all_to_all(pieces, axes, split_axis=0, concat_axis=0, tiled=True)
    return moved.reshape(array.shape)


def on_device(
    state,
    weights,
    land_mask,
    level_gain,
    depth,
    obs_row,
    obs_col,
    obs_quad,
    obs_frac,
    obs_value,
    obs_error,
    noise,
):
    axes = ("half", "member")
    members = lax.axis_size(axes)
    index = lax.axis_index(axes).astype(jnp.int32).reshape(1)
    tile_count = lax.axis_size("tile")
    obs_local = obs_row.shape[0]
    total_obs = obs_local * tile_count
    own = state[0]
    up = [(i, (i + 1) % tile_count) for i in range(tile_count)]
    down = [(target, source) for source, target in up]
    low = lax.ppermute(own[:, -1:], "tile", up)
    high = lax.ppermute(own[:, :1], "tile", down)
    tile = lax.axis_index("tile").astype(jnp.int32).reshape(1)
    grid = (obs_local // LANES, LANES)
    obs = (
        obs_row.reshape(grid),
        obs_col.reshape(grid),
        obs_quad.reshape(grid),
        obs_frac,
        obs_value.reshape(grid),
        noise.reshape(grid),
    )
    stepped, stepped_mark, sampled = forward(
        tile_count, tile, level_gain, depth, own, low, high, weights[0], land_mask, obs
    )
    grouped = swap(sampled, axes)
    packed_rows = members // 2
    misfit, products = local(
        shard_products,
        "shard_products",
        [(members, obs_local // members), (members * packed_rows, LANES)],
        index,
        grouped,
        obs_error.reshape(grid),
        stepped_mark,
    )
    (products,) = local(
        functools.partial(sum_and_spread, packed_rows),
        "sum_and_spread",
        [(tile_count * packed_rows, LANES)],
        swap(products, axes),
    )
    (combined,) = local(
        functools.partial(solve_and_combine, total_obs),
        "solve_and_combine",
        [(members * (PACK_ROWS - SUBLANES), LANES)],
        swap(products, "tile"),
        grouped,
    )
    tiles = swap(combined, axes)
    _, rows, cols = weights.shape
    new_weights = (
        tiles.reshape(rows // SUBLANES, cols // LANES, SUBLANES, LANES)
        .transpose(0, 2, 1, 3)
        .reshape(weights.shape)
    )
    return (stepped[None], new_weights, misfit)


def solution(mesh):
    in_specs = (
        P(("half", "member"), None, "tile", None),
        P(("half", "member"), "tile", None),
        P("tile", None),
        P(),
        P(),
        P("tile"),
        P("tile"),
        P("tile"),
        P(None, "tile"),
        P("tile"),
        P("tile"),
        P(("half", "member"), "tile"),
    )
    out_specs = (
        P(("half", "member"), None, "tile", None),
        P(("half", "member"), "tile", None),
        P(None, ("half", "member", "tile")),
    )
    return jax.shard_map(
        on_device, mesh=mesh, in_specs=in_specs, out_specs=out_specs, check_vma=False
    )
```

time: 91.1 us -> 84.2 us (0.924)
  waiting for transfers between devices: 10.8 us -> 2.79 us
  blocking collectives: 43.1 us -> 36.8 us
  Pallas kernels: 18.4 us -> 22.4 us
  local copies, waits for them, and re-layouts: 2.67 us -> 5.26 us
    all_to_all x1, waiting for transfers between devices: 9.53 us -> 2.79 us  [swap(): lax.all_to_all(pieces, axes, split_axis=0, concat_axis=0, tiled=True)]
    all_to_all x3, blocking collectives: 43.1 us -> 36.8 us  [swap(): lax.all_to_all(pieces, axes, split_axis=0, concat_axis=0, tiled=True)]
    ppermute x1, starting transfers between devices: 1.29 us -> 6.48 us  [on_device(): high = lax.ppermute(own[:, :1], 'tile', down)]
    ppermute x1, starting transfers between devices: 5 us -> 0.01 us  [on_device(): low = lax.ppermute(own[:, -1:], 'tile', up)]
    pallas_call x1 -> x3, Pallas kernels: 14.6 us -> 18.6 us  [the longest x1 9.77 us: forward(): pl.pallas_call(functools.partial(sample_column, tile_count), in_specs=[sm...]
    unnamed x7 -> x27, local copies, waits for them, and re-layouts: 1.34 us -> 3.89 us
    ppermute x1, waiting for transfers between devices: 1.29 us -> 0.01 us  [on_device(): low = lax.ppermute(own[:, -1:], 'tile', up)]
  transfers between devices with their start and end apart: 3 -> 3, of which waited for: 2 -> 1; matrix products, arithmetic and copies ran while one was open for 0% -> 0% of each run, Pallas kernels for 0% -> 11%
where the time goes in v5:
time: 84.2 us; the launch traced here: 83.8 us
  blocking collectives  36.8 us (44%)
  Pallas kernels  22.4 us (27%)
  starting transfers between devices  15.7 us (19%)
  local copies, waits for them, and re-layouts  5.26 us (6%)
  waiting for transfers between devices  2.79 us (3%)
  between operations  0.87 us (1%)
    all_to_all x3, blocking collectives, swap(): lax.all_to_all(pieces, axes, split_axis=0, concat_axis=0, tiled=True)  36.8 us
    pallas_call x1, Pallas kernels, forward(): pl.pallas_call(functools.partial(sample_column, tile_count), in_specs=[sm...  9.77 us
    all_to_all x1, starting transfers between devices, swap(): lax.all_to_all(pieces, axes, split_axis=0, concat_axis=0, tiled=True)  9.17 us
    ppermute x1, starting transfers between devices, on_device(): high = lax.ppermute(own[:, :1], 'tile', down)  6.48 us
    pallas_call x1, Pallas kernels, forward(): pl.pallas_call(functools.partial(step_levels, tile_count), grid=(levels /...  4.55 us
    pallas_call x1, Pallas kernels, forward(): pl.pallas_call(sum_column, in_specs=[smem, smem, pl.BlockSpec(memory_spac...  4.32 us
    unnamed x27, local copies, waits for them, and re-layouts  3.89 us
    pallas_call x3, Pallas kernels, local(): pl.pallas_call(kernel, in_specs=[smem if array.dtype == jnp.int32 else vm...  3.8 us
  transfers between devices with their start and end apart: 3, of which 1 were waited for; matrix products, arithmetic and copies ran while one was open for 0% of the time, Pallas kernels for 11%

profile of v5, /device:TPU:1, one launch (start us, length us, event | category | flops | bytes accessed | tf_op | source)
XLA Modules:
  0.0 83.8 jit_solution(15674487390492997835)
XLA Ops:
  0.6 0.0 copy-start.11
  0.6 0.0 copy-start.2
  0.7 0.0 copy-start.12
  0.7 0.0 copy-start.1
  0.7 0.0 copy-start.9
  0.7 0.0 copy-start.8
  0.7 0.0 copy-start.4
  0.7 0.0 copy-start.7
  0.7 0.0 copy-start.6
  0.7 0.0 copy-start.5
  0.7 1.4 %fusion = (f32[16,1,1024]{2,1,0:T(1,128)S(1)}, f32[16,1,1024]{2,1,0:T(1,128)S(1)}) fusion(f32[16,64,1024]{2,1,0:T(8,128)} %bitcast.23), kind=kLoop, calls=%fused_computation | loop fusion | bytes 262144 | tf_op jit(solution)/shard_map/slice | solution.py:413
  2.1 6.5 %collective-permute-start.1 = (f32[16,1,1024]{2,1,0:T(1,128)S(1)}, f32[16,1,1024]{2,1,0:T(1,128)S(1)}, u32[]{:S(2)}, u32[]{:S(2)}) collective-permute-start(f32[16,1,1024]{2,1,0:T(1,128)S(1)} %get-tuple-element.11), channel_id=1, source_target_pairs={{1,0},{2,1},{3,2},{4,3},{5,4},{6,5},{7,6},{0,7},{9,8},{10,9},{11,1... | collective-permute-start | bytes 196616 | tf_op jit(solution)/shard_map/ppermute | solution.py:413
  8.6 0.0 collective-permute-start
  8.6 0.0 copy-start.10
  8.6 4.3 %sum_column.1.column_ref = f32[64,1024]{1,0:T(8,128)} custom-call(f32[16]{0:T(128)} %gain_ref.5, f32[16]{0:T(128)} %depth_ref.3, f32[16,64,1024]{2,1,0:T(8,128)} %bitcast.24, f32[64,1024]{1,0:T(8,128)} %bitcast.28, s32[64,1024]{1,0:T(8,128)} %land_ref.5), custom_call_target="tpu_custom_call" | custom-call | flops 6291456 | bytes 4194304 | tf_op jit(solution)/shard_map/sum_column/pallas_call | solution.py:247
  12.9 0.0 collective-permute-done.1.high_ref
  12.9 0.0 collective-permute-done.low_ref
  12.9 0.0 copy-done.11
  13.0 0.0 copy-done.2
  13.0 0.0 copy-done.12
  13.0 0.0 copy-done.1
  13.0 0.0 copy-done.9
  13.0 0.0 copy-done.8
  13.0 0.0 copy-done.4
  13.0 0.0 copy-done.7
  13.0 0.0 copy-done.6
  13.0 0.0 copy-done.5
  13.0 0.0 copy-start.3
  13.1 0.9 %copy-done.3 = f32[64,1024]{1,0:T(8,128)S(1)} copy-done((f32[64,1024]{1,0:T(8,128)S(1)}, f32[64,1024]{1,0:T(8,128)}, u32[]{:S(2)}) %copy-start.3) | copy-done | bytes 262168
  14.0 9.8 %sample_column.1.after_ref = f32[768,128]{1,0:T(8,128)} custom-call(s32[1]{0:T(128)} %bitcast.tile_ref, f32[16]{0:T(128)S(1)} %copy-done.11, f32[16]{0:T(128)S(1)} %copy-done.12, f32[64,1024]{1,0:T(8,128)S(1)} %copy-done.3, f32[16,1,1024]{2,1,0:T(1,128)S(1)} %collective-permute-done.low_ref, f32[16,1,1024]{2,1,0:T(1,128)S(1)} %collective-permute-done.1.high_ref, ...), custom_call_target="tpu_custom_call" | custom-call | tf_op jit(solution)/shard_map/sample_column/pallas_call | solution.py:264
  23.8 9.2 %all-to-all-start = ((f32[32,24,128]{2,1,0:T(8,128)}), f32[32,24,128]{2,1,0:T(8,128)S(1)}, u32[]{:S(2)}, u32[]{:S(2)}) async-start(f32[32,24,128]{2,1,0:T(8,128)} %bitcast.10), calls=%async_computation | async-start | bytes 786432 | tf_op jit(solution)/shard_map/all_to_all | solution.py:385
  33.0 0.0 copy-start
  33.0 2.2 %copy-done = f32[1,16,64,1024]{3,2,1,0:T(8,128)S(1)} copy-done((f32[1,16,64,1024]{3,2,1,0:T(8,128)S(1)}, f32[1,16,64,1024]{3,2,1,0:T(8,128)}, u32[]{:S(2)}) %copy-start) | copy-done | bytes 4194328
  35.1 4.6 %step_levels.1 = (f32[16,64,1024]{2,1,0:T(8,128)}, f32[8,128]{1,0:T(8,128)S(1)}) custom-call(s32[1]{0:T(128)} %bitcast.tile_ref, f32[16]{0:T(128)S(1)} %copy-done.11, f32[16,64,1024]{2,1,0:T(8,128)S(1)} %bitcast.25, f32[16,1,1024]{2,1,0:T(1,128)S(1)} %collective-permute-done.low_ref, f32[16,1,1024]{2,1,0:T(1,128)S(1)} %collective-permute-done.1.high_ref, ...), custom_call_target="tpu_custom_call" | custom-call | flops 10485760 | bytes 8388608 | tf_op jit(solution)/shard_map/step_levels/pallas_call | solution.py:273
  39.7 2.8 %all-to-all-done = f32[32,24,128]{2,1,0:T(8,128)S(1)} async-done(((f32[32,24,128]{2,1,0:T(8,128)}), f32[32,24,128]{2,1,0:T(8,128)S(1)}, u32[]{:S(2)}, u32[]{:S(2)}) %all-to-all-start) | async-done | bytes 393248 | tf_op jit(solution)/shard_map/all_to_all | solution.py:385
  42.5 0.0 copy-done.10
  42.5 0.7 shard_products.1
  43.1 12.7 %all_to_all.20 = f32[32,16,128]{2,1,0:T(8,128)S(1)} all-to-all(f32[32,16,128]{2,1,0:T(8,128)S(1)} %bitcast.34), channel_id=1, replica_groups=mesh['half'=2,'member'=16,'tile'=8] {'half','member'}, dimensions={0} | all-to-all | bytes 524288 | tf_op jit(solution)/shard_map/all_to_all | solution.py:385
  55.9 10.3 %all_to_all.21 = f32[8,16,128]{2,1,0:T(8,128)S(1)} all-to-all(f32[8,16,128]{2,1,0:T(8,128)S(1)} %bitcast.33), channel_id=1, replica_groups=mesh['half'=2,'member'=16,'tile'=8] {'tile'}, dimensions={0} | all-to-all | bytes 131072 | tf_op jit(solution)/shard_map/all_to_all | solution.py:385
  66.1 3.1 %solve_and_combine.1 = f32[512,128]{1,0:T(8,128)S(1)} custom-call(f32[128,128]{1,0:T(8,128)S(1)} %bitcast.35, f32[768,128]{1,0:T(8,128)S(1)} %bitcast.27), custom_call_target="tpu_custom_call" | custom-call | tf_op jit(solution)/shard_map/solve_and_combine/pallas_call | solution.py:372
  69.2 13.8 %all_to_all.22 = f32[32,16,128]{2,1,0:T(8,128)S(1)} all-to-all(f32[32,16,128]{2,1,0:T(8,128)S(1)} %bitcast.32), channel_id=1, replica_groups=mesh['half'=2,'member'=16,'tile'=8] {'half','member'}, dimensions={0} | all-to-all | bytes 524288 | tf_op jit(solution)/shard_map/all_to_all | solution.py:385
  83.1 0.7 copy.16
  (1 shorter events, 0.0 us)
Async XLA Ops:
  0.6 12.3 %copy-start.11 = (f32[16]{0:T(128)S(1)}, f32[16]{0:T(128)}, u32[]{:S(2)}) copy-start(f32[16]{0:T(128)} %gain_ref.5) | copy-start | bytes 196
  0.6 12.3 %copy-start.2 = (s32[64,1024]{1,0:T(8,128)S(1)}, s32[64,1024]{1,0:T(8,128)}, u32[]{:S(2)}) copy-start(s32[64,1024]{1,0:T(8,128)} %land_ref.5) | copy-start | bytes 786436
  0.7 12.3 %copy-start.12 = (f32[16]{0:T(128)S(1)}, f32[16]{0:T(128)}, u32[]{:S(2)}) copy-start(f32[16]{0:T(128)} %depth_ref.3) | copy-start | bytes 196
  0.7 12.3 %copy-start.1 = (f32[1,64,1024]{2,1,0:T(8,128)S(1)}, f32[1,64,1024]{2,1,0:T(8,128)}, u32[]{:S(2)}) copy-start(f32[1,64,1024]{2,1,0:T(8,128)} %param.13) | copy-start | bytes 786436
  0.7 12.3 %copy-start.9 = (f32[1,16384]{1,0:T(1,128)S(1)}, f32[1,16384]{1,0:T(1,128)}, u32[]{:S(2)}) copy-start(f32[1,16384]{1,0:T(1,128)} %param.23) | copy-start | bytes 196612
  0.7 12.3 %copy-start.8 = (f32[16384]{0:T(1024)S(1)}, f32[16384]{0:T(1024)}, u32[]{:S(2)}) copy-start(f32[16384]{0:T(1024)} %param.21) | copy-start | bytes 196612
  0.7 12.3 %copy-start.4 = (f32[2,16384]{1,0:T(2,128)S(1)}, f32[2,16384]{1,0:T(2,128)}, u32[]{:S(2)}) copy-start(f32[2,16384]{1,0:T(2,128)} %frac_ref.1) | copy-start | bytes 393220
  0.7 12.3 %copy-start.7 = (s32[16384]{0:T(1024)S(1)}, s32[16384]{0:T(1024)}, u32[]{:S(2)}) copy-start(s32[16384]{0:T(1024)} %param.19) | copy-start | bytes 196612
  0.7 12.3 %copy-start.6 = (s32[16384]{0:T(1024)S(1)}, s32[16384]{0:T(1024)}, u32[]{:S(2)}) copy-start(s32[16384]{0:T(1024)} %param.18) | copy-start | bytes 196612
  0.7 12.3 %copy-start.5 = (s32[16384]{0:T(1024)S(1)}, s32[16384]{0:T(1024)}, u32[]{:S(2)}) copy-start(s32[16384]{0:T(1024)} %param.17) | copy-start | bytes 196612
  2.1 10.8 %collective-permute-start.1 = (f32[16,1,1024]{2,1,0:T(1,128)S(1)}, f32[16,1,1024]{2,1,0:T(1,128)S(1)}, u32[]{:S(2)}, u32[]{:S(2)}) collective-permute-start(f32[16,1,1024]{2,1,0:T(1,128)S(1)} %get-tuple-element.11), channel_id=1, source_target_pairs={{1,0},{2,1},{3,2},{4,3},{5,4},{6,5},{7,6},{0,7},{9,8},{10,9},{11,1... | collective-permute-start | bytes 196616 | tf_op jit(solution)/shard_map/ppermute | solution.py:413
  8.6 4.3 %collective-permute-start = (f32[16,1,1024]{2,1,0:T(1,128)S(1)}, f32[16,1,1024]{2,1,0:T(1,128)S(1)}, u32[]{:S(2)}, u32[]{:S(2)}) collective-permute-start(f32[16,1,1024]{2,1,0:T(1,128)S(1)} %get-tuple-element.12), channel_id=1, source_target_pairs={{0,1},{1,2},{2,3},{3,4},{4,5},{5,6},{6,7},{7,0},{8,9},{9,10},{10,1... | collective-permute-start | bytes 196616 | tf_op jit(solution)/shard_map/ppermute | solution.py:412
  8.6 33.9 %copy-start.10 = (f32[16384]{0:T(1024)S(1)}, f32[16384]{0:T(1024)}, u32[]{:S(2)}) copy-start(f32[16384]{0:T(1024)} %param.22) | copy-start | bytes 196612
  13.0 1.0 %copy-start.3 = (f32[64,1024]{1,0:T(8,128)S(1)}, f32[64,1024]{1,0:T(8,128)}, u32[]{:S(2)}) copy-start(f32[64,1024]{1,0:T(8,128)} %sum_column.1.column_ref) | copy-start | bytes 786436
  23.8 18.7 %all-to-all-start = ((f32[32,24,128]{2,1,0:T(8,128)}), f32[32,24,128]{2,1,0:T(8,128)S(1)}, u32[]{:S(2)}, u32[]{:S(2)}) async-start(f32[32,24,128]{2,1,0:T(8,128)} %bitcast.10), calls=%async_computation | async-start | bytes 786432 | tf_op jit(solution)/shard_map/all_to_all | solution.py:385
  33.0 2.2 %copy-start = (f32[1,16,64,1024]{3,2,1,0:T(8,128)S(1)}, f32[1,16,64,1024]{3,2,1,0:T(8,128)}, u32[]{:S(2)}) copy-start(f32[1,16,64,1024]{3,2,1,0:T(8,128)} %param.12) | copy-start | bytes 12582916

commit v6 on v5

--- a/solution.py
+++ b/solution.py
@@ -42,18 +42,34 @@
 
 
 def sum_column(
-    gain_ref, depth_ref, state_ref, weights_ref, land_ref, column_ref, held_ref, flow_ref, sems
+    gain_ref,
+    depth_ref,
+    state_ref,
+    weights_far_ref,
+    land_far_ref,
+    column_ref,
+    held_ref,
+    flow_ref,
+    weights_ref,
+    land_ref,
+    sems,
 ):
     levels, rows, cols = state_ref.shape
-    parts = sems.shape[0]
+    parts = sems.shape[0] - 2
     per = levels // parts
 
     def copy(part):
         here = pl.ds(part * per, per)
         return pltpu.make_async_copy(state_ref.at[here], held_ref.at[here], sems.at[part])
 
+    planes = [
+        pltpu.make_async_copy(weights_far_ref, weights_ref, sems.at[parts]),
+        pltpu.make_async_copy(land_far_ref, land_ref, sems.at[parts + 1]),
+    ]
     for part in range(parts):
         copy(part).start()
+    for plane in planes:
+        plane.start()
     for part in range(parts):
         copy(part).wait()
         for start in range(0, rows, SUBLANES):
@@ -69,6 +85,8 @@
                 flow = flow + flow_ref[here, :]
             column_ref[here, :] = column
             flow_ref[here, :] = flow
+    for plane in planes:
+        plane.wait()
     scale = 1.0 / math.sqrt(levels)
     blank = jnp.zeros((1, cols), jnp.float32)
     for start in range(0, rows, SUBLANES):
@@ -187,12 +205,13 @@
             ref[pl.ds((2 * part + 1) * rows, rows), pl.ds(key, LANES)] = fine
 
     count = OBS_STEP // LANES
-    keys = lax.broadcasted_iota(jnp.int32, (KEYS, OBS_STEP), 0)
+    keys = lax.broadcasted_iota(jnp.int16, (KEYS, OBS_STEP), 0)
+    one, zero = jnp.bfloat16(1.0), jnp.bfloat16(0.0)
     grid_row = lax.broadcasted_iota(jnp.int32, (rows, OBS_STEP), 0)
     shard_rows = SUBLANES // 2
 
     def look_up(ref, at):
-        chosen = jnp.where(keys == (at & (KEYS - 1)), 1.0, 0.0).astype(jnp.bfloat16)
+        chosen = jnp.where(keys == (at & (KEYS - 1)).astype(jnp.int16), one, zero)
         found = jnp.dot(ref[...], chosen, preferred_element_type=jnp.float32)
         result = found[:rows] + found[rows : 2 * rows]
         for part in range(1, cols // (2 * KEYS)):
@@ -246,13 +265,15 @@
     field = pl.BlockSpec((per, rows, cols), lambda i: (i, 0, 0))
     column = pl.pallas_call(
         sum_column,
-        in_specs=[smem, smem, pl.BlockSpec(memory_space=pl.ANY), vmem, vmem],
+        in_specs=[smem, smem] + [pl.BlockSpec(memory_space=pl.ANY)] * 3,
         out_specs=vmem,
         out_shape=jax.ShapeDtypeStruct((rows, cols), jnp.float32),
         scratch_shapes=[
             pltpu.VMEM(state.shape, jnp.float32),
             pltpu.VMEM((rows, cols), jnp.float32),
-            pltpu.SemaphoreType.DMA((levels // per,)),
+            pltpu.VMEM((rows, cols), jnp.float32),
+            pltpu.VMEM((rows, cols), jnp.int32),
+            pltpu.SemaphoreType.DMA((levels // per + 2,)),
         ],
         compiler_params=pltpu.CompilerParams(vmem_limit_bytes=VMEM_BYTES),
         cost_estimate=pl.CostEstimate(

time: 84.2 us -> 82.2 us (0.976)
  Pallas kernels: 22.4 us -> 20.5 us
    pallas_call x1, Pallas kernels: 9.77 us -> 8.08 us  [forward(): pl.pallas_call(functools.partial(sample_column, tile_count), in_specs=[sm...]
  transfers between devices with their start and end apart: 3 -> 3, of which waited for: 1 -> 2; matrix products, arithmetic and copies ran while one was open for 0% -> 0% of each run, Pallas kernels for 11% -> 11%
where the time goes in v6:
time: 82.2 us; the launch traced here: 81.8 us
  blocking collectives  36.6 us (45%)
  Pallas kernels  20.5 us (25%)
  starting transfers between devices  15.7 us (19%)
  local copies, waits for them, and re-layouts  5.26 us (6%)
  waiting for transfers between devices  3 us (4%)
  between operations  0.84 us (1%)
    all_to_all x3, blocking collectives, swap(): lax.all_to_all(pieces, axes, split_axis=0, concat_axis=0, tiled=True)  36.6 us
    all_to_all x1, starting transfers between devices, swap(): lax.all_to_all(pieces, axes, split_axis=0, concat_axis=0, tiled=True)  9.18 us
    pallas_call x1, Pallas kernels, forward(): pl.pallas_call(functools.partial(sample_column, tile_count), in_specs=[sm...  8.08 us
    ppermute x1, starting transfers between devices, on_device(): high = lax.ppermute(own[:, :1], 'tile', down)  6.48 us
    pallas_call x1, Pallas kernels, forward(): pl.pallas_call(functools.partial(step_levels, tile_count), grid=(levels /...  4.55 us
    pallas_call x1, Pallas kernels, forward(): pl.pallas_call(sum_column, in_specs=[smem, smem] + [pl.BlockSpec(memory_s...  4.09 us
    unnamed x27, local copies, waits for them, and re-layouts  3.89 us
    pallas_call x3, Pallas kernels, local(): pl.pallas_call(kernel, in_specs=[smem if array.dtype == jnp.int32 else vm...  3.79 us
  transfers between devices with their start and end apart: 3, of which 2 were waited for; matrix products, arithmetic and copies ran while one was open for 0% of the time, Pallas kernels for 11%

profile of v6, /device:TPU:1, one launch (start us, length us, event | category | flops | bytes accessed | tf_op | source)
XLA Modules:
  0.0 81.8 jit_solution(16401070383292171141)
XLA Ops:
  0.6 0.0 copy-start.11
  0.6 0.0 copy-start.2
  0.7 0.0 copy-start.12
  0.7 0.0 copy-start.1
  0.7 0.0 copy-start.9
  0.7 0.0 copy-start.8
  0.7 0.0 copy-start.4
  0.7 0.0 copy-start.7
  0.7 0.0 copy-start.6
  0.7 0.0 copy-start.5
  0.7 1.4 %fusion = (f32[16,1,1024]{2,1,0:T(1,128)S(1)}, f32[16,1,1024]{2,1,0:T(1,128)S(1)}) fusion(f32[16,64,1024]{2,1,0:T(8,128)} %bitcast.23), kind=kLoop, calls=%fused_computation | loop fusion | bytes 262144 | tf_op jit(solution)/shard_map/slice | solution.py:434
  2.1 6.5 %collective-permute-start.1 = (f32[16,1,1024]{2,1,0:T(1,128)S(1)}, f32[16,1,1024]{2,1,0:T(1,128)S(1)}, u32[]{:S(2)}, u32[]{:S(2)}) collective-permute-start(f32[16,1,1024]{2,1,0:T(1,128)S(1)} %get-tuple-element.11), channel_id=1, source_target_pairs={{1,0},{2,1},{3,2},{4,3},{5,4},{6,5},{7,6},{0,7},{9,8},{10,9},{11,1... | collective-permute-start | bytes 196616 | tf_op jit(solution)/shard_map/ppermute | solution.py:434
  8.6 0.0 collective-permute-start
  8.6 0.0 copy-start.10
  8.6 4.1 %sum_column.1.column_ref = f32[64,1024]{1,0:T(8,128)} custom-call(f32[16]{0:T(128)} %gain_ref.5, f32[16]{0:T(128)} %depth_ref.3, f32[16,64,1024]{2,1,0:T(8,128)} %bitcast.24, f32[64,1024]{1,0:T(8,128)} %bitcast.28, s32[64,1024]{1,0:T(8,128)} %land_ref.3), custom_call_target="tpu_custom_call" | custom-call | flops 6291456 | bytes 4194304 | tf_op jit(solution)/shard_map/sum_column/pallas_call | solution.py:266
  12.7 0.0 collective-permute-done.1.high_ref
  12.7 0.2 collective-permute-done.low_ref
  12.9 0.0 copy-done.11
  12.9 0.0 copy-done.2
  12.9 0.0 copy-done.12
  12.9 0.0 copy-done.1
  12.9 0.0 copy-done.9
  13.0 0.0 copy-done.8
  13.0 0.0 copy-done.4
  13.0 0.0 copy-done.7
  13.0 0.0 copy-done.6
  13.0 0.0 copy-done.5
  13.0 0.0 copy-start.3
  13.0 0.9 %copy-done.3 = f32[64,1024]{1,0:T(8,128)S(1)} copy-done((f32[64,1024]{1,0:T(8,128)S(1)}, f32[64,1024]{1,0:T(8,128)}, u32[]{:S(2)}) %copy-start.3) | copy-done | bytes 262168
  14.0 8.1 %sample_column.1.after_ref = f32[768,128]{1,0:T(8,128)} custom-call(s32[1]{0:T(128)} %bitcast.tile_ref, f32[16]{0:T(128)S(1)} %copy-done.11, f32[16]{0:T(128)S(1)} %copy-done.12, f32[64,1024]{1,0:T(8,128)S(1)} %copy-done.3, f32[16,1,1024]{2,1,0:T(1,128)S(1)} %collective-permute-done.low_ref, f32[16,1,1024]{2,1,0:T(1,128)S(1)} %collective-permute-done.1.high_ref, ...), custom_call_target="tpu_custom_call" | custom-call | tf_op jit(solution)/shard_map/sample_column/pallas_call | solution.py:285
  22.0 9.2 %all-to-all-start = ((f32[32,24,128]{2,1,0:T(8,128)}), f32[32,24,128]{2,1,0:T(8,128)S(1)}, u32[]{:S(2)}, u32[]{:S(2)}) async-start(f32[32,24,128]{2,1,0:T(8,128)} %bitcast.10), calls=%async_computation | async-start | bytes 786432 | tf_op jit(solution)/shard_map/all_to_all | solution.py:406
  31.2 0.0 copy-start
  31.2 2.2 %copy-done = f32[1,16,64,1024]{3,2,1,0:T(8,128)S(1)} copy-done((f32[1,16,64,1024]{3,2,1,0:T(8,128)S(1)}, f32[1,16,64,1024]{3,2,1,0:T(8,128)}, u32[]{:S(2)}) %copy-start) | copy-done | bytes 4194328
  33.4 4.6 %step_levels.1 = (f32[16,64,1024]{2,1,0:T(8,128)}, f32[8,128]{1,0:T(8,128)S(1)}) custom-call(s32[1]{0:T(128)} %bitcast.tile_ref, f32[16]{0:T(128)S(1)} %copy-done.11, f32[16,64,1024]{2,1,0:T(8,128)S(1)} %bitcast.25, f32[16,1,1024]{2,1,0:T(1,128)S(1)} %collective-permute-done.low_ref, f32[16,1,1024]{2,1,0:T(1,128)S(1)} %collective-permute-done.1.high_ref, ...), custom_call_target="tpu_custom_call" | custom-call | flops 10485760 | bytes 8388608 | tf_op jit(solution)/shard_map/step_levels/pallas_call | solution.py:294
  38.0 2.8 %all-to-all-done = f32[32,24,128]{2,1,0:T(8,128)S(1)} async-done(((f32[32,24,128]{2,1,0:T(8,128)}), f32[32,24,128]{2,1,0:T(8,128)S(1)}, u32[]{:S(2)}, u32[]{:S(2)}) %all-to-all-start) | async-done | bytes 393248 | tf_op jit(solution)/shard_map/all_to_all | solution.py:406
  40.8 0.0 copy-done.10
  40.8 0.7 shard_products.1
  41.4 12.7 %all_to_all.20 = f32[32,16,128]{2,1,0:T(8,128)S(1)} all-to-all(f32[32,16,128]{2,1,0:T(8,128)S(1)} %bitcast.34), channel_id=1, replica_groups=mesh['half'=2,'member'=16,'tile'=8] {'half','member'}, dimensions={0} | all-to-all | bytes 524288 | tf_op jit(solution)/shard_map/all_to_all | solution.py:406
  54.1 10.1 %all_to_all.21 = f32[8,16,128]{2,1,0:T(8,128)S(1)} all-to-all(f32[8,16,128]{2,1,0:T(8,128)S(1)} %bitcast.33), channel_id=1, replica_groups=mesh['half'=2,'member'=16,'tile'=8] {'tile'}, dimensions={0} | all-to-all | bytes 131072 | tf_op jit(solution)/shard_map/all_to_all | solution.py:406
  64.2 3.1 %solve_and_combine.1 = f32[512,128]{1,0:T(8,128)S(1)} custom-call(f32[128,128]{1,0:T(8,128)S(1)} %bitcast.35, f32[768,128]{1,0:T(8,128)S(1)} %bitcast.27), custom_call_target="tpu_custom_call" | custom-call | tf_op jit(solution)/shard_map/solve_and_combine/pallas_call | solution.py:393
  67.3 13.8 %all_to_all.22 = f32[32,16,128]{2,1,0:T(8,128)S(1)} all-to-all(f32[32,16,128]{2,1,0:T(8,128)S(1)} %bitcast.32), channel_id=1, replica_groups=mesh['half'=2,'member'=16,'tile'=8] {'half','member'}, dimensions={0} | all-to-all | bytes 524288 | tf_op jit(solution)/shard_map/all_to_all | solution.py:406
  81.1 0.7 copy.16
  (1 shorter events, 0.0 us)
Async XLA Ops:
  0.6 12.3 %copy-start.11 = (f32[16]{0:T(128)S(1)}, f32[16]{0:T(128)}, u32[]{:S(2)}) copy-start(f32[16]{0:T(128)} %gain_ref.5) | copy-start | bytes 196
  0.6 12.3 %copy-start.2 = (s32[64,1024]{1,0:T(8,128)S(1)}, s32[64,1024]{1,0:T(8,128)}, u32[]{:S(2)}) copy-start(s32[64,1024]{1,0:T(8,128)} %land_ref.3) | copy-start | bytes 786436
  0.7 12.3 %copy-start.12 = (f32[16]{0:T(128)S(1)}, f32[16]{0:T(128)}, u32[]{:S(2)}) copy-start(f32[16]{0:T(128)} %depth_ref.3) | copy-start | bytes 196
  0.7 12.3 %copy-start.1 = (f32[1,64,1024]{2,1,0:T(8,128)S(1)}, f32[1,64,1024]{2,1,0:T(8,128)}, u32[]{:S(2)}) copy-start(f32[1,64,1024]{2,1,0:T(8,128)} %param.13) | copy-start | bytes 786436
  0.7 12.3 %copy-start.9 = (f32[1,16384]{1,0:T(1,128)S(1)}, f32[1,16384]{1,0:T(1,128)}, u32[]{:S(2)}) copy-start(f32[1,16384]{1,0:T(1,128)} %param.23) | copy-start | bytes 196612
  0.7 12.3 %copy-start.8 = (f32[16384]{0:T(1024)S(1)}, f32[16384]{0:T(1024)}, u32[]{:S(2)}) copy-start(f32[16384]{0:T(1024)} %param.21) | copy-start | bytes 196612
  0.7 12.3 %copy-start.4 = (f32[2,16384]{1,0:T(2,128)S(1)}, f32[2,16384]{1,0:T(2,128)}, u32[]{:S(2)}) copy-start(f32[2,16384]{1,0:T(2,128)} %frac_ref.1) | copy-start | bytes 393220
  0.7 12.3 %copy-start.7 = (s32[16384]{0:T(1024)S(1)}, s32[16384]{0:T(1024)}, u32[]{:S(2)}) copy-start(s32[16384]{0:T(1024)} %param.19) | copy-start | bytes 196612
  0.7 12.3 %copy-start.6 = (s32[16384]{0:T(1024)S(1)}, s32[16384]{0:T(1024)}, u32[]{:S(2)}) copy-start(s32[16384]{0:T(1024)} %param.18) | copy-start | bytes 196612
  0.7 12.3 %copy-start.5 = (s32[16384]{0:T(1024)S(1)}, s32[16384]{0:T(1024)}, u32[]{:S(2)}) copy-start(s32[16384]{0:T(1024)} %param.17) | copy-start | bytes 196612
  2.1 10.6 %collective-permute-start.1 = (f32[16,1,1024]{2,1,0:T(1,128)S(1)}, f32[16,1,1024]{2,1,0:T(1,128)S(1)}, u32[]{:S(2)}, u32[]{:S(2)}) collective-permute-start(f32[16,1,1024]{2,1,0:T(1,128)S(1)} %get-tuple-element.11), channel_id=1, source_target_pairs={{1,0},{2,1},{3,2},{4,3},{5,4},{6,5},{7,6},{0,7},{9,8},{10,9},{11,1... | collective-permute-start | bytes 196616 | tf_op jit(solution)/shard_map/ppermute | solution.py:434
  8.6 4.3 %collective-permute-start = (f32[16,1,1024]{2,1,0:T(1,128)S(1)}, f32[16,1,1024]{2,1,0:T(1,128)S(1)}, u32[]{:S(2)}, u32[]{:S(2)}) collective-permute-start(f32[16,1,1024]{2,1,0:T(1,128)S(1)} %get-tuple-element.12), channel_id=1, source_target_pairs={{0,1},{1,2},{2,3},{3,4},{4,5},{5,6},{6,7},{7,0},{8,9},{9,10},{10,1... | collective-permute-start | bytes 196616 | tf_op jit(solution)/shard_map/ppermute | solution.py:433
  8.6 32.2 %copy-start.10 = (f32[16384]{0:T(1024)S(1)}, f32[16384]{0:T(1024)}, u32[]{:S(2)}) copy-start(f32[16384]{0:T(1024)} %param.22) | copy-start | bytes 196612
  13.0 1.0 %copy-start.3 = (f32[64,1024]{1,0:T(8,128)S(1)}, f32[64,1024]{1,0:T(8,128)}, u32[]{:S(2)}) copy-start(f32[64,1024]{1,0:T(8,128)} %sum_column.1.column_ref) | copy-start | bytes 786436
  22.0 18.7 %all-to-all-start = ((f32[32,24,128]{2,1,0:T(8,128)}), f32[32,24,128]{2,1,0:T(8,128)S(1)}, u32[]{:S(2)}, u32[]{:S(2)}) async-start(f32[32,24,128]{2,1,0:T(8,128)} %bitcast.10), calls=%async_computation | async-start | bytes 786432 | tf_op jit(solution)/shard_map/all_to_all | solution.py:406
  31.2 2.2 %copy-start = (f32[1,16,64,1024]{3,2,1,0:T(8,128)S(1)}, f32[1,16,64,1024]{3,2,1,0:T(8,128)}, u32[]{:S(2)}) copy-start(f32[1,16,64,1024]{3,2,1,0:T(8,128)} %param.12) | copy-start | bytes 12582916

commit v7 on v6

--- a/solution.py
+++ b/solution.py
@@ -11,7 +11,8 @@
 LANES = 128
 SUBLANES = 8
 LEVELS_STEP = 4
-OBS_STEP = 2048
+OBS_STEP = 4096
+GATHERED_LINES = 10
 KEYS = 256
 PACK_ROWS = 3 * SUBLANES
 VMEM_BYTES = 60 * 1024 * 1024
@@ -153,6 +154,8 @@
     sampled_ref,
     even_ref,
     odd_ref,
+    even_whole_ref,
+    odd_whole_ref,
 ):
     rows, cols = column_ref.shape
     levels = low_ref.shape[0]
@@ -197,17 +200,22 @@
                 jnp.where(first_half, pick(left, doubled + 1), pick(right, doubled + 1))
             )
         part, key = divmod(block * LANES, KEYS)
-        for ref, pieces in ((even_ref, evens), (odd_ref, odds)):
+        for ref, whole_ref, pieces in (
+            (even_ref, even_whole_ref, evens),
+            (odd_ref, odd_whole_ref, odds),
+        ):
             table = jnp.concatenate(pieces, axis=0)
+            whole_ref[:, pl.ds(block * LANES, LANES)] = table
             coarse = table.astype(jnp.bfloat16)
             fine = (table - coarse.astype(jnp.float32)).astype(jnp.bfloat16)
             ref[pl.ds(2 * part * rows, rows), pl.ds(key, LANES)] = coarse
             ref[pl.ds((2 * part + 1) * rows, rows), pl.ds(key, LANES)] = fine
 
     count = OBS_STEP // LANES
-    keys = lax.broadcasted_iota(jnp.int16, (KEYS, OBS_STEP), 0)
+    width = OBS_STEP - GATHERED_LINES * LANES
+    keys = lax.broadcasted_iota(jnp.int16, (KEYS, width), 0)
     one, zero = jnp.bfloat16(1.0), jnp.bfloat16(0.0)
-    grid_row = lax.broadcasted_iota(jnp.int32, (rows, OBS_STEP), 0)
+    grid_row = lax.broadcasted_iota(jnp.int32, (rows, width), 0)
     shard_rows = SUBLANES // 2
 
     def look_up(ref, at):
@@ -220,16 +228,19 @@
             result = jnp.where(at // KEYS == part, other, result)
         return result
 
-    def sample(i, carry):
-        def line(ref):
-            return jnp.concatenate(
-                [ref[pl.ds(i * count + q, 1), :] for q in range(count)], axis=1
-            )
-
-        row, col, quad = line(row_ref), line(col_ref), line(quad_ref)
-        place = pl.ds(pl.multiple_of(i * OBS_STEP, OBS_STEP), OBS_STEP)
-        first = frac_ref[pl.ds(0, 1), place]
-        second = frac_ref[pl.ds(1, 1), place]
+    def gather(ref, at):
+        at_lane, at_block = at & (LANES - 1), at // LANES
+        groups = []
+        for start in range(0, rows, SUBLANES):
+            here = pl.ds(start, SUBLANES)
+            group = pick(ref[here, pl.ds(0, LANES)], at_lane)
+            for block in range(1, cols // (2 * LANES)):
+                found = pick(ref[here, pl.ds(block * LANES, LANES)], at_lane)
+                group = jnp.where(at_block == block, found, group)
+            groups.append(group)
+        return groups
+
+    def places(row, col, quad, second):
         row_other = row + jnp.where((quad & 1) == 1, 1, -1)
         col_other = (col + jnp.where((quad >> 1) == 1, 1, -1)) & (cols - 1)
         is_even = (col & 1) == 0
@@ -237,18 +248,60 @@
         odd_at = jnp.where(is_even, col_other, col) >> 1
         even_by = jnp.where(is_even, 1.0 - second, second)
         odd_by = jnp.where(is_even, second, 1.0 - second)
+        return row_other, even_at, odd_at, even_by, odd_by
+
+    def sample(i, carry):
+        def put(q, predicted, perturbed):
+            shard, inner = divmod(q, shard_rows)
+            to = (i * (count // shard_rows) + shard) * PACK_ROWS + inner
+            sampled_ref[pl.ds(to, 1), :] = predicted
+            sampled_ref[pl.ds(to + shard_rows, 1), :] = perturbed - predicted
+
+        def line(ref):
+            return jnp.concatenate(
+                [ref[pl.ds(i * count + q, 1), :] for q in range(GATHERED_LINES, count)], axis=1
+            )
+
+        row = line(row_ref)
+        begin = i * OBS_STEP + GATHERED_LINES * LANES
+        place = pl.ds(pl.multiple_of(begin, LANES), width)
+        first = frac_ref[pl.ds(0, 1), place]
+        second = frac_ref[pl.ds(1, 1), place]
+        row_other, even_at, odd_at, even_by, odd_by = places(
+            row, line(col_ref), line(quad_ref), second
+        )
         along = even_by * look_up(even_ref, even_at) + odd_by * look_up(odd_ref, odd_at)
         by_row = jnp.where(
             grid_row == row, 1.0 - first, jnp.where(grid_row == row_other, first, 0.0)
         )
         predicted = jnp.sum(by_row * along, axis=0, keepdims=True)
-        residual = line(value_ref) + line(noise_ref) - predicted
-        for q in range(count):
-            shard, inner = divmod(q, shard_rows)
-            to = (i * (count // shard_rows) + shard) * PACK_ROWS + inner
-            lanes = slice(q * LANES, (q + 1) * LANES)
-            sampled_ref[pl.ds(to, 1), :] = predicted[:, lanes]
-            sampled_ref[pl.ds(to + shard_rows, 1), :] = residual[:, lanes]
+        perturbed = line(value_ref) + line(noise_ref)
+        for q in range(GATHERED_LINES, count):
+            lanes = slice((q - GATHERED_LINES) * LANES, (q - GATHERED_LINES + 1) * LANES)
+            put(q, predicted[:, lanes], perturbed[:, lanes])
+
+        for q in range(GATHERED_LINES):
+            here = pl.ds(i * count + q, 1)
+            place = pl.ds(pl.multiple_of((i * count + q) * LANES, LANES), LANES)
+
+            def spread(value):
+                return jnp.broadcast_to(value, (SUBLANES, LANES))
+
+            row = spread(row_ref[here, :])
+            first = spread(frac_ref[pl.ds(0, 1), place])
+            second = spread(frac_ref[pl.ds(1, 1), place])
+            row_other, even_at, odd_at, even_by, odd_by = places(
+                row, spread(col_ref[here, :]), spread(quad_ref[here, :]), second
+            )
+            evens, odds = gather(even_whole_ref, even_at), gather(odd_whole_ref, odd_at)
+            total = jnp.zeros((SUBLANES, LANES), jnp.float32)
+            for start, even, odd in zip(range(0, rows, SUBLANES), evens, odds):
+                by_row = jnp.where(
+                    sub == row - start, 1.0 - first, jnp.where(sub == row_other - start, first, 0.0)
+                )
+                total = total + by_row * (even_by * even + odd_by * odd)
+            predicted = jnp.sum(total, axis=0, keepdims=True)
+            put(q, predicted, value_ref[here, :] + noise_ref[here, :])
         return carry
 
     lax.fori_loop(0, row_ref.shape[0] // count, sample, 0)
@@ -287,7 +340,7 @@
         in_specs=[smem, smem, smem] + [vmem] * (5 + len(obs)),
         out_specs=vmem,
         out_shape=jax.ShapeDtypeStruct(packed, jnp.float32),
-        scratch_shapes=[table, table],
+        scratch_shapes=[table, table] + [pltpu.VMEM((rows, cols // 2), jnp.float32)] * 2,
         compiler_params=pltpu.CompilerParams(vmem_limit_bytes=MIDDLE_VMEM_BYTES),
         name="sample_column",
     )(tile, level_gain, depth, column, low, high, weights, land_mask, *obs)

time: 82.2 us -> 80.7 us (0.982)
  Pallas kernels: 20.5 us -> 19 us
    pallas_call x1, Pallas kernels: 8.08 us -> 6.58 us  [forward(): pl.pallas_call(functools.partial(sample_column, tile_count), in_specs=[sm...]
where the time goes in v7:
time: 80.7 us; the launch traced here: 80.3 us
  blocking collectives  36.5 us (45%)
  Pallas kernels  19 us (24%)
  starting transfers between devices  15.7 us (19%)
  local copies, waits for them, and re-layouts  5.26 us (7%)
  waiting for transfers between devices  3 us (4%)
  between operations  0.84 us (1%)
    all_to_all x3, blocking collectives, swap(): lax.all_to_all(pieces, axes, split_axis=0, concat_axis=0, tiled=True)  36.5 us
    all_to_all x1, starting transfers between devices, swap(): lax.all_to_all(pieces, axes, split_axis=0, concat_axis=0, tiled=True)  9.2 us
    pallas_call x1, Pallas kernels, forward(): pl.pallas_call(functools.partial(sample_column, tile_count), in_specs=[sm...  6.58 us
    ppermute x1, starting transfers between devices, on_device(): high = lax.ppermute(own[:, :1], 'tile', down)  6.48 us
    pallas_call x1, Pallas kernels, forward(): pl.pallas_call(functools.partial(step_levels, tile_count), grid=(levels /...  4.55 us
    pallas_call x1, Pallas kernels, forward(): pl.pallas_call(sum_column, in_specs=[smem, smem] + [pl.BlockSpec(memory_s...  4.09 us
    unnamed x27, local copies, waits for them, and re-layouts  3.89 us
    pallas_call x3, Pallas kernels, local(): pl.pallas_call(kernel, in_specs=[smem if array.dtype == jnp.int32 else vm...  3.79 us
  transfers between devices with their start and end apart: 3, of which 2 were waited for; matrix products, arithmetic and copies ran while one was open for 0% of the time, Pallas kernels for 11%

profile of v7, /device:TPU:1, one launch (start us, length us, event | category | flops | bytes accessed | tf_op | source)
XLA Modules:
  0.0 80.3 jit_solution(14727941520197338839)
XLA Ops:
  0.6 0.0 copy-start.11
  0.6 0.0 copy-start.2
  0.7 0.0 copy-start.12
  0.7 0.0 copy-start.1
  0.7 0.0 copy-start.9
  0.7 0.0 copy-start.8
  0.7 0.0 copy-start.4
  0.7 0.0 copy-start.7
  0.7 0.0 copy-start.6
  0.7 0.0 copy-start.5
  0.7 1.4 %fusion = (f32[16,1,1024]{2,1,0:T(1,128)S(1)}, f32[16,1,1024]{2,1,0:T(1,128)S(1)}) fusion(f32[16,64,1024]{2,1,0:T(8,128)} %bitcast.23), kind=kLoop, calls=%fused_computation | loop fusion | bytes 262144 | tf_op jit(solution)/shard_map/slice | solution.py:487
  2.1 6.5 %collective-permute-start.1 = (f32[16,1,1024]{2,1,0:T(1,128)S(1)}, f32[16,1,1024]{2,1,0:T(1,128)S(1)}, u32[]{:S(2)}, u32[]{:S(2)}) collective-permute-start(f32[16,1,1024]{2,1,0:T(1,128)S(1)} %get-tuple-element.11), channel_id=1, source_target_pairs={{1,0},{2,1},{3,2},{4,3},{5,4},{6,5},{7,6},{0,7},{9,8},{10,9},{11,1... | collective-permute-start | bytes 196616 | tf_op jit(solution)/shard_map/ppermute | solution.py:487
  8.6 0.0 collective-permute-start
  8.6 0.0 copy-start.10
  8.6 4.1 %sum_column.1.column_ref = f32[64,1024]{1,0:T(8,128)} custom-call(f32[16]{0:T(128)} %gain_ref.5, f32[16]{0:T(128)} %depth_ref.3, f32[16,64,1024]{2,1,0:T(8,128)} %bitcast.24, f32[64,1024]{1,0:T(8,128)} %bitcast.28, s32[64,1024]{1,0:T(8,128)} %land_ref.3), custom_call_target="tpu_custom_call" | custom-call | flops 6291456 | bytes 4194304 | tf_op jit(solution)/shard_map/sum_column/pallas_call | solution.py:319
  12.7 0.0 collective-permute-done.1.high_ref
  12.7 0.2 collective-permute-done.low_ref
  12.9 0.0 copy-done.11
  12.9 0.0 copy-done.2
  12.9 0.0 copy-done.12
  12.9 0.0 copy-done.1
  12.9 0.0 copy-done.9
  13.0 0.0 copy-done.8
  13.0 0.0 copy-done.4
  13.0 0.0 copy-done.7
  13.0 0.0 copy-done.6
  13.0 0.0 copy-done.5
  13.0 0.0 copy-start.3
  13.0 0.9 %copy-done.3 = f32[64,1024]{1,0:T(8,128)S(1)} copy-done((f32[64,1024]{1,0:T(8,128)S(1)}, f32[64,1024]{1,0:T(8,128)}, u32[]{:S(2)}) %copy-start.3) | copy-done | bytes 262168
  14.0 6.6 %sample_column.1.after_ref = f32[768,128]{1,0:T(8,128)} custom-call(s32[1]{0:T(128)} %bitcast.tile_ref, f32[16]{0:T(128)S(1)} %copy-done.11, f32[16]{0:T(128)S(1)} %copy-done.12, f32[64,1024]{1,0:T(8,128)S(1)} %copy-done.3, f32[16,1,1024]{2,1,0:T(1,128)S(1)} %collective-permute-done.low_ref, f32[16,1,1024]{2,1,0:T(1,128)S(1)} %collective-permute-done.1.high_ref, ...), custom_call_target="tpu_custom_call" | custom-call | tf_op jit(solution)/shard_map/sample_column/pallas_call | solution.py:338
  20.5 9.2 %all-to-all-start = ((f32[32,24,128]{2,1,0:T(8,128)}), f32[32,24,128]{2,1,0:T(8,128)S(1)}, u32[]{:S(2)}, u32[]{:S(2)}) async-start(f32[32,24,128]{2,1,0:T(8,128)} %bitcast.10), calls=%async_computation | async-start | bytes 786432 | tf_op jit(solution)/shard_map/all_to_all | solution.py:459
  29.7 0.0 copy-start
  29.8 2.2 %copy-done = f32[1,16,64,1024]{3,2,1,0:T(8,128)S(1)} copy-done((f32[1,16,64,1024]{3,2,1,0:T(8,128)S(1)}, f32[1,16,64,1024]{3,2,1,0:T(8,128)}, u32[]{:S(2)}) %copy-start) | copy-done | bytes 4194328
  31.9 4.6 %step_levels.1 = (f32[16,64,1024]{2,1,0:T(8,128)}, f32[8,128]{1,0:T(8,128)S(1)}) custom-call(s32[1]{0:T(128)} %bitcast.tile_ref, f32[16]{0:T(128)S(1)} %copy-done.11, f32[16,64,1024]{2,1,0:T(8,128)S(1)} %bitcast.25, f32[16,1,1024]{2,1,0:T(1,128)S(1)} %collective-permute-done.low_ref, f32[16,1,1024]{2,1,0:T(1,128)S(1)} %collective-permute-done.1.high_ref, ...), custom_call_target="tpu_custom_call" | custom-call | flops 10485760 | bytes 8388608 | tf_op jit(solution)/shard_map/step_levels/pallas_call | solution.py:347
  36.5 2.8 %all-to-all-done = f32[32,24,128]{2,1,0:T(8,128)S(1)} async-done(((f32[32,24,128]{2,1,0:T(8,128)}), f32[32,24,128]{2,1,0:T(8,128)S(1)}, u32[]{:S(2)}, u32[]{:S(2)}) %all-to-all-start) | async-done | bytes 393248 | tf_op jit(solution)/shard_map/all_to_all | solution.py:459
  39.3 0.0 copy-done.10
  39.3 0.7 shard_products.1
  39.9 12.7 %all_to_all.20 = f32[32,16,128]{2,1,0:T(8,128)S(1)} all-to-all(f32[32,16,128]{2,1,0:T(8,128)S(1)} %bitcast.34), channel_id=1, replica_groups=mesh['half'=2,'member'=16,'tile'=8] {'half','member'}, dimensions={0} | all-to-all | bytes 524288 | tf_op jit(solution)/shard_map/all_to_all | solution.py:459
  52.6 10.0 %all_to_all.21 = f32[8,16,128]{2,1,0:T(8,128)S(1)} all-to-all(f32[8,16,128]{2,1,0:T(8,128)S(1)} %bitcast.33), channel_id=1, replica_groups=mesh['half'=2,'member'=16,'tile'=8] {'tile'}, dimensions={0} | all-to-all | bytes 131072 | tf_op jit(solution)/shard_map/all_to_all | solution.py:459
  62.7 3.1 %solve_and_combine.1 = f32[512,128]{1,0:T(8,128)S(1)} custom-call(f32[128,128]{1,0:T(8,128)S(1)} %bitcast.35, f32[768,128]{1,0:T(8,128)S(1)} %bitcast.27), custom_call_target="tpu_custom_call" | custom-call | tf_op jit(solution)/shard_map/solve_and_combine/pallas_call | solution.py:446
  65.8 13.8 %all_to_all.22 = f32[32,16,128]{2,1,0:T(8,128)S(1)} all-to-all(f32[32,16,128]{2,1,0:T(8,128)S(1)} %bitcast.32), channel_id=1, replica_groups=mesh['half'=2,'member'=16,'tile'=8] {'half','member'}, dimensions={0} | all-to-all | bytes 524288 | tf_op jit(solution)/shard_map/all_to_all | solution.py:459
  79.6 0.7 copy.16
  (1 shorter events, 0.0 us)
Async XLA Ops:
  0.6 12.3 %copy-start.11 = (f32[16]{0:T(128)S(1)}, f32[16]{0:T(128)}, u32[]{:S(2)}) copy-start(f32[16]{0:T(128)} %gain_ref.5) | copy-start | bytes 196
  0.6 12.3 %copy-start.2 = (s32[64,1024]{1,0:T(8,128)S(1)}, s32[64,1024]{1,0:T(8,128)}, u32[]{:S(2)}) copy-start(s32[64,1024]{1,0:T(8,128)} %land_ref.3) | copy-start | bytes 786436
  0.7 12.3 %copy-start.12 = (f32[16]{0:T(128)S(1)}, f32[16]{0:T(128)}, u32[]{:S(2)}) copy-start(f32[16]{0:T(128)} %depth_ref.3) | copy-start | bytes 196
  0.7 12.3 %copy-start.1 = (f32[1,64,1024]{2,1,0:T(8,128)S(1)}, f32[1,64,1024]{2,1,0:T(8,128)}, u32[]{:S(2)}) copy-start(f32[1,64,1024]{2,1,0:T(8,128)} %param.13) | copy-start | bytes 786436
  0.7 12.3 %copy-start.9 = (f32[1,16384]{1,0:T(1,128)S(1)}, f32[1,16384]{1,0:T(1,128)}, u32[]{:S(2)}) copy-start(f32[1,16384]{1,0:T(1,128)} %param.23) | copy-start | bytes 196612
  0.7 12.3 %copy-start.8 = (f32[16384]{0:T(1024)S(1)}, f32[16384]{0:T(1024)}, u32[]{:S(2)}) copy-start(f32[16384]{0:T(1024)} %param.21) | copy-start | bytes 196612
  0.7 12.3 %copy-start.4 = (f32[2,16384]{1,0:T(2,128)S(1)}, f32[2,16384]{1,0:T(2,128)}, u32[]{:S(2)}) copy-start(f32[2,16384]{1,0:T(2,128)} %frac_ref.1) | copy-start | bytes 393220
  0.7 12.3 %copy-start.7 = (s32[16384]{0:T(1024)S(1)}, s32[16384]{0:T(1024)}, u32[]{:S(2)}) copy-start(s32[16384]{0:T(1024)} %param.19) | copy-start | bytes 196612
  0.7 12.3 %copy-start.6 = (s32[16384]{0:T(1024)S(1)}, s32[16384]{0:T(1024)}, u32[]{:S(2)}) copy-start(s32[16384]{0:T(1024)} %param.18) | copy-start | bytes 196612
  0.7 12.3 %copy-start.5 = (s32[16384]{0:T(1024)S(1)}, s32[16384]{0:T(1024)}, u32[]{:S(2)}) copy-start(s32[16384]{0:T(1024)} %param.17) | copy-start | bytes 196612
  2.1 10.6 %collective-permute-start.1 = (f32[16,1,1024]{2,1,0:T(1,128)S(1)}, f32[16,1,1024]{2,1,0:T(1,128)S(1)}, u32[]{:S(2)}, u32[]{:S(2)}) collective-permute-start(f32[16,1,1024]{2,1,0:T(1,128)S(1)} %get-tuple-element.11), channel_id=1, source_target_pairs={{1,0},{2,1},{3,2},{4,3},{5,4},{6,5},{7,6},{0,7},{9,8},{10,9},{11,1... | collective-permute-start | bytes 196616 | tf_op jit(solution)/shard_map/ppermute | solution.py:487
  8.6 4.3 %collective-permute-start = (f32[16,1,1024]{2,1,0:T(1,128)S(1)}, f32[16,1,1024]{2,1,0:T(1,128)S(1)}, u32[]{:S(2)}, u32[]{:S(2)}) collective-permute-start(f32[16,1,1024]{2,1,0:T(1,128)S(1)} %get-tuple-element.12), channel_id=1, source_target_pairs={{0,1},{1,2},{2,3},{3,4},{4,5},{5,6},{6,7},{7,0},{8,9},{9,10},{10,1... | collective-permute-start | bytes 196616 | tf_op jit(solution)/shard_map/ppermute | solution.py:486
  8.6 30.7 %copy-start.10 = (f32[16384]{0:T(1024)S(1)}, f32[16384]{0:T(1024)}, u32[]{:S(2)}) copy-start(f32[16384]{0:T(1024)} %param.22) | copy-start | bytes 196612
  13.0 1.0 %copy-start.3 = (f32[64,1024]{1,0:T(8,128)S(1)}, f32[64,1024]{1,0:T(8,128)}, u32[]{:S(2)}) copy-start(f32[64,1024]{1,0:T(8,128)} %sum_column.1.column_ref) | copy-start | bytes 786436
  20.5 18.7 %all-to-all-start = ((f32[32,24,128]{2,1,0:T(8,128)}), f32[32,24,128]{2,1,0:T(8,128)S(1)}, u32[]{:S(2)}, u32[]{:S(2)}) async-start(f32[32,24,128]{2,1,0:T(8,128)} %bitcast.10), calls=%async_computation | async-start | bytes 786432 | tf_op jit(solution)/shard_map/all_to_all | solution.py:459
  29.7 2.2 %copy-start = (f32[1,16,64,1024]{3,2,1,0:T(8,128)S(1)}, f32[1,16,64,1024]{3,2,1,0:T(8,128)}, u32[]{:S(2)}) copy-start(f32[1,16,64,1024]{3,2,1,0:T(8,128)} %param.12) | copy-start | bytes 12582916

commit v8 on v7

--- a/solution.py
+++ b/solution.py
@@ -42,13 +42,23 @@
     )
 
 
+def factor_place(side, levels, level):
+    row, block = level % SUBLANES, side * (levels // SUBLANES) + level // SUBLANES
+    return row, pl.ds(block * LANES, LANES)
+
+
 def sum_column(
-    gain_ref,
-    depth_ref,
+    tile_count,
+    gain_far_ref,
+    depth_far_ref,
     state_ref,
     weights_far_ref,
     land_far_ref,
+    tile_far_ref,
     column_ref,
+    gain_ref,
+    depth_ref,
+    tile_ref,
     held_ref,
     flow_ref,
     weights_ref,
@@ -56,7 +66,7 @@
     sems,
 ):
     levels, rows, cols = state_ref.shape
-    parts = sems.shape[0] - 2
+    parts = sems.shape[0] - 5
     per = levels // parts
 
     def copy(part):
@@ -67,10 +77,17 @@
         pltpu.make_async_copy(weights_far_ref, weights_ref, sems.at[parts]),
         pltpu.make_async_copy(land_far_ref, land_ref, sems.at[parts + 1]),
     ]
+    factors = [
+        pltpu.make_async_copy(gain_far_ref, gain_ref, sems.at[parts + 2]),
+        pltpu.make_async_copy(depth_far_ref, depth_ref, sems.at[parts + 3]),
+        pltpu.make_async_copy(tile_far_ref, tile_ref, sems.at[parts + 4]),
+    ]
     for part in range(parts):
         copy(part).start()
-    for plane in planes:
-        plane.start()
+    for small in factors + planes:
+        small.start()
+    for factor in factors:
+        factor.wait()
     for part in range(parts):
         copy(part).wait()
         for start in range(0, rows, SUBLANES):
@@ -89,6 +106,11 @@
     for plane in planes:
         plane.wait()
     scale = 1.0 / math.sqrt(levels)
+    for side, has in enumerate(has_neighbours(tile_count, tile_ref)):
+        for level in range(levels):
+            row, lanes = factor_place(side, levels, level)
+            factor = (has * scale) * (gain_ref[level] * depth_ref[level])
+            column_ref[pl.ds(rows + row, 1), lanes] = jnp.full((1, LANES), factor)
     blank = jnp.zeros((1, cols), jnp.float32)
     for start in range(0, rows, SUBLANES):
         here = pl.ds(start, SUBLANES)
@@ -136,10 +158,6 @@
 
 
 def sample_column(
-    tile_count,
-    tile_ref,
-    gain_ref,
-    depth_ref,
     column_ref,
     low_ref,
     high_ref,
@@ -157,7 +175,7 @@
     even_whole_ref,
     odd_whole_ref,
 ):
-    rows, cols = column_ref.shape
+    rows, cols = weights_ref.shape
     levels = low_ref.shape[0]
     for tile in range(rows * cols // (SUBLANES * LANES)):
         at_row, at_col = divmod(tile * LANES, cols)
@@ -166,16 +184,16 @@
             pl.ds(at_row * SUBLANES, SUBLANES), pl.ds(at_col, LANES)
         ]
 
-    def edge(ref, row, factor):
+    def edge(side, ref, row):
         one = pl.ds(row, 1)
         flow = jnp.zeros((1, cols), jnp.float32)
         for level in range(levels):
-            flow = flow + (gain_ref[level] * depth_ref[level]) * ref[level]
-        diffusivity = diffusivity_of(land_ref[one, :], weights_ref[one, :])
-        return (factor / math.sqrt(levels)) * diffusivity * flow
-
-    has_low, has_high = has_neighbours(tile_count, tile_ref)
-    low, high = edge(low_ref, 0, has_low), edge(high_ref, rows - 1, has_high)
+            factor_row, lanes = factor_place(side, levels, level)
+            factor = column_ref[pl.ds(rows + factor_row, 1), lanes]
+            flow = flow + jnp.concatenate([factor] * (cols // LANES), axis=1) * ref[level]
+        return diffusivity_of(land_ref[one, :], weights_ref[one, :]) * flow
+
+    low, high = edge(0, low_ref, 0), edge(1, high_ref, rows - 1)
     sub = lax.broadcasted_iota(jnp.int32, (SUBLANES, LANES), 0)
 
     def column_tile(start, first):
@@ -317,33 +335,36 @@
     halo = pl.BlockSpec((per, 1, cols), lambda i: (i, 0, 0))
     field = pl.BlockSpec((per, rows, cols), lambda i: (i, 0, 0))
     column = pl.pallas_call(
-        sum_column,
-        in_specs=[smem, smem] + [pl.BlockSpec(memory_space=pl.ANY)] * 3,
+        functools.partial(sum_column, tile_count),
+        in_specs=[pl.BlockSpec(memory_space=pl.ANY)] * 6,
         out_specs=vmem,
-        out_shape=jax.ShapeDtypeStruct((rows, cols), jnp.float32),
+        out_shape=jax.ShapeDtypeStruct((rows + SUBLANES, cols), jnp.float32),
         scratch_shapes=[
+            pltpu.SMEM((levels,), jnp.float32),
+            pltpu.SMEM((levels,), jnp.float32),
+            pltpu.SMEM((1,), jnp.int32),
             pltpu.VMEM(state.shape, jnp.float32),
             pltpu.VMEM((rows, cols), jnp.float32),
             pltpu.VMEM((rows, cols), jnp.float32),
             pltpu.VMEM((rows, cols), jnp.int32),
-            pltpu.SemaphoreType.DMA((levels // per + 2,)),
+            pltpu.SemaphoreType.DMA((levels // per + 5,)),
         ],
         compiler_params=pltpu.CompilerParams(vmem_limit_bytes=VMEM_BYTES),
         cost_estimate=pl.CostEstimate(
             flops=6 * state.size, bytes_accessed=4 * state.size, transcendentals=0
         ),
         name="sum_column",
-    )(level_gain, depth, state, weights, land_mask)
+    )(level_gain, depth, state, weights, land_mask, tile)
     table = pltpu.VMEM((2 * rows * cols // (2 * KEYS), KEYS), jnp.bfloat16)
     sampled = pl.pallas_call(
-        functools.partial(sample_column, tile_count),
-        in_specs=[smem, smem, smem] + [vmem] * (5 + len(obs)),
+        sample_column,
+        in_specs=[vmem] * (5 + len(obs)),
         out_specs=vmem,
         out_shape=jax.ShapeDtypeStruct(packed, jnp.float32),
         scratch_shapes=[table, table] + [pltpu.VMEM((rows, cols // 2), jnp.float32)] * 2,
         compiler_params=pltpu.CompilerParams(vmem_limit_bytes=MIDDLE_VMEM_BYTES),
         name="sample_column",
-    )(tile, level_gain, depth, column, low, high, weights, land_mask, *obs)
+    )(column, low, high, weights, land_mask, *obs)
     stepped, mark = pl.pallas_call(
         functools.partial(step_levels, tile_count),
         grid=(levels // per,),
@@ -503,7 +524,7 @@
     misfit, products = local(
         shard_products,
         "shard_products",
-        [(members, obs_local // members), (members * packed_rows, LANES)],
+        [(members, obs_local // members), (tile_count * packed_rows, LANES)],
         index,
         grouped,
         obs_error.reshape(grid),
@@ -512,14 +533,14 @@
     (products,) = local(
         functools.partial(sum_and_spread, packed_rows),
         "sum_and_spread",
-        [(tile_count * packed_rows, LANES)],
-        swap(products, axes),
+        [(members * packed_rows, LANES)],
+        swap(products, "tile"),
     )
     (combined,) = local(
         functools.partial(solve_and_combine, total_obs),
         "solve_and_combine",
         [(members * (PACK_ROWS - SUBLANES), LANES)],
-        swap(products, "tile"),
+        swap(products, axes),
         grouped,
     )
     tiles = swap(combined, axes)

time: 80.7 us -> 79.6 us (0.986)
  Pallas kernels: 19 us -> 17.8 us
    pallas_call x2, Pallas kernels: 10.7 us -> 9.42 us  [the longest x1 6.06 us: forward(): pl.pallas_call(sample_column, in_specs=[vmem] * (5 + len(obs)), out_specs...]
    unnamed x27 -> x25, local copies, waits for them, and re-layouts: 3.89 us -> 3.89 us
  transfers between devices with their start and end apart: 3 -> 3, of which waited for: 2 -> 2; matrix products, arithmetic and copies ran while one was open for 0% -> 0% of each run, Pallas kernels for 11% -> 10%
where the time goes in v8:
time: 79.6 us; the launch traced here: 79.2 us
  blocking collectives  36 us (45%)
  Pallas kernels  17.8 us (22%)
  starting transfers between devices  15.7 us (20%)
  local copies, waits for them, and re-layouts  5.26 us (7%)
  waiting for transfers between devices  3.72 us (5%)
  between operations  0.82 us (1%)
    all_to_all x3, blocking collectives, swap(): lax.all_to_all(pieces, axes, split_axis=0, concat_axis=0, tiled=True)  36 us
    all_to_all x1, starting transfers between devices, swap(): lax.all_to_all(pieces, axes, split_axis=0, concat_axis=0, tiled=True)  9.19 us
    ppermute x1, starting transfers between devices, on_device(): high = lax.ppermute(own[:, :1], 'tile', down)  6.48 us
    pallas_call x1, Pallas kernels, forward(): pl.pallas_call(sample_column, in_specs=[vmem] * (5 + len(obs)), out_specs...  6.06 us
    pallas_call x1, Pallas kernels, forward(): pl.pallas_call(functools.partial(step_levels, tile_count), grid=(levels /...  4.55 us
    unnamed x25, local copies, waits for them, and re-layouts  3.89 us
    pallas_call x3, Pallas kernels, local(): pl.pallas_call(kernel, in_specs=[smem if array.dtype == jnp.int32 else vm...  3.81 us
    pallas_call x1, Pallas kernels, forward(): pl.pallas_call(functools.partial(sum_column, tile_count), in_specs=[pl.Bl...  3.36 us
  transfers between devices with their start and end apart: 3, of which 2 were waited for; matrix products, arithmetic and copies ran while one was open for 0% of the time, Pallas kernels for 10%

profile of v8, /device:TPU:1, one launch (start us, length us, event | category | flops | bytes accessed | tf_op | source)
XLA Modules:
  0.0 79.2 jit_solution(3847630759665665598)
XLA Ops:
  0.6 0.0 copy-start.2
  0.6 0.0 copy-start.11
  0.7 0.0 copy-start.1
  0.7 0.0 copy-start.9
  0.7 0.0 copy-start.8
  0.7 0.0 copy-start.4
  0.7 0.0 copy-start.7
  0.7 0.0 copy-start.6
  0.7 0.0 copy-start.5
  0.7 1.4 %fusion = (f32[16,1,1024]{2,1,0:T(1,128)S(1)}, f32[16,1,1024]{2,1,0:T(1,128)S(1)}) fusion(f32[16,64,1024]{2,1,0:T(8,128)} %bitcast.23), kind=kLoop, calls=%fused_computation | loop fusion | bytes 262144 | tf_op jit(solution)/shard_map/slice | solution.py:508
  2.1 6.5 %collective-permute-start.1 = (f32[16,1,1024]{2,1,0:T(1,128)S(1)}, f32[16,1,1024]{2,1,0:T(1,128)S(1)}, u32[]{:S(2)}, u32[]{:S(2)}) collective-permute-start(f32[16,1,1024]{2,1,0:T(1,128)S(1)} %get-tuple-element.11), channel_id=1, source_target_pairs={{1,0},{2,1},{3,2},{4,3},{5,4},{6,5},{7,6},{0,7},{9,8},{10,9},{11,1... | collective-permute-start | bytes 196616 | tf_op jit(solution)/shard_map/ppermute | solution.py:508
  8.6 0.0 collective-permute-start
  8.6 0.0 copy-start.10
  8.6 3.4 %sum_column.1.column_ref = f32[72,1024]{1,0:T(8,128)} custom-call(f32[16]{0:T(128)} %gain_ref.1, f32[16]{0:T(128)} %depth_far_ref.1, f32[16,64,1024]{2,1,0:T(8,128)} %bitcast.24, f32[64,1024]{1,0:T(8,128)} %bitcast.28, s32[64,1024]{1,0:T(8,128)} %land_ref.3, s32[1]{0:T(128)} %bitcast.tile_far_ref.tile_ref), custom_call_target="tpu_custom_call" | custom-call | flops 6291456 | bytes 4194304 | tf_op jit(solution)/shard_map/sum_column/pallas_call | solution.py:337
  12.0 0.0 collective-permute-done.1.high_ref
  12.0 0.9 %collective-permute-done.low_ref = f32[16,1,1024]{2,1,0:T(1,128)S(1)} collective-permute-done((f32[16,1,1024]{2,1,0:T(1,128)S(1)}, f32[16,1,1024]{2,1,0:T(1,128)S(1)}, u32[]{:S(2)}, u32[]{:S(2)}) %collective-permute-start) | collective-permute-done | bytes 65568 | tf_op jit(solution)/shard_map/ppermute | solution.py:507
  12.9 0.0 copy-done.2
  12.9 0.0 copy-done.1
  12.9 0.0 copy-done.9
  12.9 0.0 copy-done.8
  12.9 0.0 copy-done.4
  12.9 0.0 copy-done.7
  12.9 0.0 copy-done.6
  13.0 0.0 copy-done.5
  13.0 0.0 copy-start.3
  13.0 1.0 %copy-done.3 = f32[72,1024]{1,0:T(8,128)S(1)} copy-done((f32[72,1024]{1,0:T(8,128)S(1)}, f32[72,1024]{1,0:T(8,128)}, u32[]{:S(2)}) %copy-start.3) | copy-done | bytes 294936
  13.9 6.1 %sample_column.1.after_ref = f32[768,128]{1,0:T(8,128)} custom-call(f32[72,1024]{1,0:T(8,128)S(1)} %copy-done.3, f32[16,1,1024]{2,1,0:T(1,128)S(1)} %collective-permute-done.low_ref, f32[16,1,1024]{2,1,0:T(1,128)S(1)} %collective-permute-done.1.high_ref, f32[64,1024]{1,0:T(8,128)S(1)} %bitcast.29, s32[64,1024]{1,0:T(8,128)S(1)} %copy-done.2, ...), custom_call_target="tpu_custom_call" | custom-call | tf_op jit(solution)/shard_map/sample_column/pallas_call | solution.py:359
  20.0 9.2 %all-to-all-start = ((f32[32,24,128]{2,1,0:T(8,128)}), f32[32,24,128]{2,1,0:T(8,128)S(1)}, u32[]{:S(2)}, u32[]{:S(2)}) async-start(f32[32,24,128]{2,1,0:T(8,128)} %bitcast.10), calls=%async_computation | async-start | bytes 786432 | tf_op jit(solution)/shard_map/all_to_all | solution.py:480
  29.2 0.0 copy-done.11
  29.2 0.0 copy-start
  29.2 2.2 %copy-done = f32[1,16,64,1024]{3,2,1,0:T(8,128)S(1)} copy-done((f32[1,16,64,1024]{3,2,1,0:T(8,128)S(1)}, f32[1,16,64,1024]{3,2,1,0:T(8,128)}, u32[]{:S(2)}) %copy-start) | copy-done | bytes 4194328
  31.4 4.6 %step_levels.1 = (f32[16,64,1024]{2,1,0:T(8,128)}, f32[8,128]{1,0:T(8,128)S(1)}) custom-call(s32[1]{0:T(128)} %bitcast.tile_far_ref.tile_ref, f32[16]{0:T(128)S(1)} %copy-done.11, f32[16,64,1024]{2,1,0:T(8,128)S(1)} %bitcast.25, f32[16,1,1024]{2,1,0:T(1,128)S(1)} %collective-permute-done.low_ref, f32[16,1,1024]{2,1,0:T(1,128)S(1)} %collective-permute-done.1.high_ref, ...), custom_call_target="tpu_custom_call" | custom-call | flops 10485760 | bytes 8388608 | tf_op jit(solution)/shard_map/step_levels/pallas_call | solution.py:368
  36.0 2.8 %all-to-all-done = f32[32,24,128]{2,1,0:T(8,128)S(1)} async-done(((f32[32,24,128]{2,1,0:T(8,128)}), f32[32,24,128]{2,1,0:T(8,128)S(1)}, u32[]{:S(2)}, u32[]{:S(2)}) %all-to-all-start) | async-done | bytes 393248 | tf_op jit(solution)/shard_map/all_to_all | solution.py:480
  38.7 0.0 copy-done.10
  38.7 0.7 shard_products.1
  39.4 9.6 %all_to_all.20 = f32[8,16,128]{2,1,0:T(8,128)S(1)} all-to-all(f32[8,16,128]{2,1,0:T(8,128)S(1)} %bitcast.40), channel_id=1, replica_groups=mesh['half'=2,'member'=16,'tile'=8] {'tile'}, dimensions={0} | all-to-all | bytes 131072 | tf_op jit(solution)/shard_map/all_to_all | solution.py:480
  49.0 14.0 %all_to_all.21 = f32[32,16,128]{2,1,0:T(8,128)S(1)} all-to-all(f32[32,16,128]{2,1,0:T(8,128)S(1)} %bitcast.33), channel_id=1, replica_groups=mesh['half'=2,'member'=16,'tile'=8] {'half','member'}, dimensions={0} | all-to-all | bytes 524288 | tf_op jit(solution)/shard_map/all_to_all | solution.py:480
  63.0 3.1 %solve_and_combine.1 = f32[512,128]{1,0:T(8,128)S(1)} custom-call(f32[512,128]{1,0:T(8,128)S(1)} %bitcast.31, f32[768,128]{1,0:T(8,128)S(1)} %bitcast.27), custom_call_target="tpu_custom_call" | custom-call | tf_op jit(solution)/shard_map/solve_and_combine/pallas_call | solution.py:467
  66.1 12.4 %all_to_all.22 = f32[32,16,128]{2,1,0:T(8,128)S(1)} all-to-all(f32[32,16,128]{2,1,0:T(8,128)S(1)} %bitcast.32), channel_id=1, replica_groups=mesh['half'=2,'member'=16,'tile'=8] {'half','member'}, dimensions={0} | all-to-all | bytes 524288 | tf_op jit(solution)/shard_map/all_to_all | solution.py:480
  78.5 0.7 copy.16
  (1 shorter events, 0.0 us)
Async XLA Ops:
  0.6 12.3 %copy-start.2 = (s32[64,1024]{1,0:T(8,128)S(1)}, s32[64,1024]{1,0:T(8,128)}, u32[]{:S(2)}) copy-start(s32[64,1024]{1,0:T(8,128)} %land_ref.3) | copy-start | bytes 786436
  0.6 28.6 %copy-start.11 = (f32[16]{0:T(128)S(1)}, f32[16]{0:T(128)}, u32[]{:S(2)}) copy-start(f32[16]{0:T(128)} %gain_ref.1) | copy-start | bytes 196
  0.7 12.3 %copy-start.1 = (f32[1,64,1024]{2,1,0:T(8,128)S(1)}, f32[1,64,1024]{2,1,0:T(8,128)}, u32[]{:S(2)}) copy-start(f32[1,64,1024]{2,1,0:T(8,128)} %param.13) | copy-start | bytes 786436
  0.7 12.2 %copy-start.9 = (f32[1,16384]{1,0:T(1,128)S(1)}, f32[1,16384]{1,0:T(1,128)}, u32[]{:S(2)}) copy-start(f32[1,16384]{1,0:T(1,128)} %param.23) | copy-start | bytes 196612
  0.7 12.2 %copy-start.8 = (f32[16384]{0:T(1024)S(1)}, f32[16384]{0:T(1024)}, u32[]{:S(2)}) copy-start(f32[16384]{0:T(1024)} %param.21) | copy-start | bytes 196612
  0.7 12.2 %copy-start.4 = (f32[2,16384]{1,0:T(2,128)S(1)}, f32[2,16384]{1,0:T(2,128)}, u32[]{:S(2)}) copy-start(f32[2,16384]{1,0:T(2,128)} %frac_ref.1) | copy-start | bytes 393220
  0.7 12.2 %copy-start.7 = (s32[16384]{0:T(1024)S(1)}, s32[16384]{0:T(1024)}, u32[]{:S(2)}) copy-start(s32[16384]{0:T(1024)} %param.19) | copy-start | bytes 196612
  0.7 12.2 %copy-start.6 = (s32[16384]{0:T(1024)S(1)}, s32[16384]{0:T(1024)}, u32[]{:S(2)}) copy-start(s32[16384]{0:T(1024)} %param.18) | copy-start | bytes 196612
  0.7 12.2 %copy-start.5 = (s32[16384]{0:T(1024)S(1)}, s32[16384]{0:T(1024)}, u32[]{:S(2)}) copy-start(s32[16384]{0:T(1024)} %param.17) | copy-start | bytes 196612
  2.1 9.9 %collective-permute-start.1 = (f32[16,1,1024]{2,1,0:T(1,128)S(1)}, f32[16,1,1024]{2,1,0:T(1,128)S(1)}, u32[]{:S(2)}, u32[]{:S(2)}) collective-permute-start(f32[16,1,1024]{2,1,0:T(1,128)S(1)} %get-tuple-element.11), channel_id=1, source_target_pairs={{1,0},{2,1},{3,2},{4,3},{5,4},{6,5},{7,6},{0,7},{9,8},{10,9},{11,1... | collective-permute-start | bytes 196616 | tf_op jit(solution)/shard_map/ppermute | solution.py:508
  8.6 4.3 %collective-permute-start = (f32[16,1,1024]{2,1,0:T(1,128)S(1)}, f32[16,1,1024]{2,1,0:T(1,128)S(1)}, u32[]{:S(2)}, u32[]{:S(2)}) collective-permute-start(f32[16,1,1024]{2,1,0:T(1,128)S(1)} %get-tuple-element.12), channel_id=1, source_target_pairs={{0,1},{1,2},{2,3},{3,4},{4,5},{5,6},{6,7},{7,0},{8,9},{9,10},{10,1... | collective-permute-start | bytes 196616 | tf_op jit(solution)/shard_map/ppermute | solution.py:507
  8.6 30.2 %copy-start.10 = (f32[16384]{0:T(1024)S(1)}, f32[16384]{0:T(1024)}, u32[]{:S(2)}) copy-start(f32[16384]{0:T(1024)} %param.22) | copy-start | bytes 196612
  13.0 1.0 %copy-start.3 = (f32[72,1024]{1,0:T(8,128)S(1)}, f32[72,1024]{1,0:T(8,128)}, u32[]{:S(2)}) copy-start(f32[72,1024]{1,0:T(8,128)} %sum_column.1.column_ref) | copy-start | bytes 884740
  20.0 18.7 %all-to-all-start = ((f32[32,24,128]{2,1,0:T(8,128)}), f32[32,24,128]{2,1,0:T(8,128)S(1)}, u32[]{:S(2)}, u32[]{:S(2)}) async-start(f32[32,24,128]{2,1,0:T(8,128)} %bitcast.10), calls=%async_computation | async-start | bytes 786432 | tf_op jit(solution)/shard_map/all_to_all | solution.py:480
  29.2 2.2 %copy-start = (f32[1,16,64,1024]{3,2,1,0:T(8,128)S(1)}, f32[1,16,64,1024]{3,2,1,0:T(8,128)}, u32[]{:S(2)}) copy-start(f32[1,16,64,1024]{3,2,1,0:T(8,128)} %param.12) | copy-start | bytes 12582916

commit v9 on v8

--- a/solution.py
+++ b/solution.py
@@ -439,10 +439,18 @@
     lane = lax.broadcasted_iota(jnp.int32, (members, 2 * members), 1)
     system = jnp.concatenate([packed[:, : 2 * members], packed[:, 2 * members :]], axis=0)
     system = system / total_obs + jnp.where(row + members == lane, 1.0, 0.0)
-    for k in range(members):
-        at = slice(members + k, members + k + 1)
-        pivot_row = system[k : k + 1, :] * (1.0 / system[k : k + 1, at])
-        system = jnp.where(row == k, pivot_row, system - system[:, at] * pivot_row)
+    for k in range(0, members, 2):
+        at, at_next = (slice(members + i, members + i + 1) for i in (k, k + 1))
+        left = jnp.broadcast_to(system[:, at], system.shape)
+        right = jnp.broadcast_to(system[:, at_next], system.shape)
+        first, second = system[k : k + 1, :], system[k + 1 : k + 2, :]
+        a, b = left[k : k + 1, :], right[k : k + 1, :]
+        c, d = left[k + 1 : k + 2, :], right[k + 1 : k + 2, :]
+        scale = 1.0 / (a * d - b * c)
+        pivot = (d * first - b * second) * scale
+        pivot_next = (a * second - c * first) * scale
+        others = system - left * pivot - right * pivot_next
+        system = jnp.where(row == k, pivot, jnp.where(row == k + 1, pivot_next, others))
     coefficients = system[:, :members]
     combination = coefficients - jnp.sum(coefficients, axis=0, keepdims=True) * (1.0 / members)
     combination = combination + jnp.where(row == lane, 1.0, 0.0)[:, :members]

time: 79.6 us -> 78.5 us (0.986)
  Pallas kernels: 17.8 us -> 16.6 us
    pallas_call x3, Pallas kernels: 3.81 us -> 2.66 us  [local(): pl.pallas_call(kernel, in_specs=[smem if array.dtype == jnp.int32 else vm...]
where the time goes in v9:
time: 78.5 us; the launch traced here: 78.1 us
  blocking collectives  36 us (46%)
  Pallas kernels  16.6 us (21%)
  starting transfers between devices  15.7 us (20%)
  local copies, waits for them, and re-layouts  5.26 us (7%)
  waiting for transfers between devices  3.72 us (5%)
  between operations  0.82 us (1%)
    all_to_all x3, blocking collectives, swap(): lax.all_to_all(pieces, axes, split_axis=0, concat_axis=0, tiled=True)  36 us
    all_to_all x1, starting transfers between devices, swap(): lax.all_to_all(pieces, axes, split_axis=0, concat_axis=0, tiled=True)  9.19 us
    ppermute x1, starting transfers between devices, on_device(): high = lax.ppermute(own[:, :1], 'tile', down)  6.48 us
    pallas_call x1, Pallas kernels, forward(): pl.pallas_call(sample_column, in_specs=[vmem] * (5 + len(obs)), out_specs...  6.06 us
    pallas_call x1, Pallas kernels, forward(): pl.pallas_call(functools.partial(step_levels, tile_count), grid=(levels /...  4.55 us
    unnamed x25, local copies, waits for them, and re-layouts  3.89 us
    pallas_call x1, Pallas kernels, forward(): pl.pallas_call(functools.partial(sum_column, tile_count), in_specs=[pl.Bl...  3.36 us
    all_to_all x1, waiting for transfers between devices, swap(): lax.all_to_all(pieces, axes, split_axis=0, concat_axis=0, tiled=True)  2.78 us
  transfers between devices with their start and end apart: 3, of which 2 were waited for; matrix products, arithmetic and copies ran while one was open for 0% of the time, Pallas kernels for 10%

profile of v9, /device:TPU:1, one launch (start us, length us, event | category | flops | bytes accessed | tf_op | source)
XLA Modules:
  0.0 78.1 jit_solution(2109715356886170500)
XLA Ops:
  0.6 0.0 copy-start.2
  0.6 0.0 copy-start.11
  0.7 0.0 copy-start.1
  0.7 0.0 copy-start.9
  0.7 0.0 copy-start.8
  0.7 0.0 copy-start.4
  0.7 0.0 copy-start.7
  0.7 0.0 copy-start.6
  0.7 0.0 copy-start.5
  0.7 1.4 %fusion = (f32[16,1,1024]{2,1,0:T(1,128)S(1)}, f32[16,1,1024]{2,1,0:T(1,128)S(1)}) fusion(f32[16,64,1024]{2,1,0:T(8,128)} %bitcast.23), kind=kLoop, calls=%fused_computation | loop fusion | bytes 262144 | tf_op jit(solution)/shard_map/slice | solution.py:516
  2.1 6.5 %collective-permute-start.1 = (f32[16,1,1024]{2,1,0:T(1,128)S(1)}, f32[16,1,1024]{2,1,0:T(1,128)S(1)}, u32[]{:S(2)}, u32[]{:S(2)}) collective-permute-start(f32[16,1,1024]{2,1,0:T(1,128)S(1)} %get-tuple-element.11), channel_id=1, source_target_pairs={{1,0},{2,1},{3,2},{4,3},{5,4},{6,5},{7,6},{0,7},{9,8},{10,9},{11,1... | collective-permute-start | bytes 196616 | tf_op jit(solution)/shard_map/ppermute | solution.py:516
  8.6 0.0 collective-permute-start
  8.6 0.0 copy-start.10
  8.6 3.4 %sum_column.1.column_ref = f32[72,1024]{1,0:T(8,128)} custom-call(f32[16]{0:T(128)} %gain_ref.1, f32[16]{0:T(128)} %depth_far_ref.1, f32[16,64,1024]{2,1,0:T(8,128)} %bitcast.24, f32[64,1024]{1,0:T(8,128)} %bitcast.28, s32[64,1024]{1,0:T(8,128)} %land_ref.3, s32[1]{0:T(128)} %bitcast.tile_far_ref.tile_ref), custom_call_target="tpu_custom_call" | custom-call | flops 6291456 | bytes 4194304 | tf_op jit(solution)/shard_map/sum_column/pallas_call | solution.py:337
  12.0 0.0 collective-permute-done.1.high_ref
  12.0 0.9 %collective-permute-done.low_ref = f32[16,1,1024]{2,1,0:T(1,128)S(1)} collective-permute-done((f32[16,1,1024]{2,1,0:T(1,128)S(1)}, f32[16,1,1024]{2,1,0:T(1,128)S(1)}, u32[]{:S(2)}, u32[]{:S(2)}) %collective-permute-start) | collective-permute-done | bytes 65568 | tf_op jit(solution)/shard_map/ppermute | solution.py:515
  12.9 0.0 copy-done.2
  12.9 0.0 copy-done.1
  12.9 0.0 copy-done.9
  12.9 0.0 copy-done.8
  12.9 0.0 copy-done.4
  12.9 0.0 copy-done.7
  12.9 0.0 copy-done.6
  13.0 0.0 copy-done.5
  13.0 0.0 copy-start.3
  13.0 1.0 %copy-done.3 = f32[72,1024]{1,0:T(8,128)S(1)} copy-done((f32[72,1024]{1,0:T(8,128)S(1)}, f32[72,1024]{1,0:T(8,128)}, u32[]{:S(2)}) %copy-start.3) | copy-done | bytes 294936
  13.9 6.1 %sample_column.1.after_ref = f32[768,128]{1,0:T(8,128)} custom-call(f32[72,1024]{1,0:T(8,128)S(1)} %copy-done.3, f32[16,1,1024]{2,1,0:T(1,128)S(1)} %collective-permute-done.low_ref, f32[16,1,1024]{2,1,0:T(1,128)S(1)} %collective-permute-done.1.high_ref, f32[64,1024]{1,0:T(8,128)S(1)} %bitcast.29, s32[64,1024]{1,0:T(8,128)S(1)} %copy-done.2, ...), custom_call_target="tpu_custom_call" | custom-call | tf_op jit(solution)/shard_map/sample_column/pallas_call | solution.py:359
  20.0 9.2 %all-to-all-start = ((f32[32,24,128]{2,1,0:T(8,128)}), f32[32,24,128]{2,1,0:T(8,128)S(1)}, u32[]{:S(2)}, u32[]{:S(2)}) async-start(f32[32,24,128]{2,1,0:T(8,128)} %bitcast.10), calls=%async_computation | async-start | bytes 786432 | tf_op jit(solution)/shard_map/all_to_all | solution.py:488
  29.2 0.0 copy-done.11
  29.2 0.0 copy-start
  29.2 2.2 %copy-done = f32[1,16,64,1024]{3,2,1,0:T(8,128)S(1)} copy-done((f32[1,16,64,1024]{3,2,1,0:T(8,128)S(1)}, f32[1,16,64,1024]{3,2,1,0:T(8,128)}, u32[]{:S(2)}) %copy-start) | copy-done | bytes 4194328
  31.4 4.6 %step_levels.1 = (f32[16,64,1024]{2,1,0:T(8,128)}, f32[8,128]{1,0:T(8,128)S(1)}) custom-call(s32[1]{0:T(128)} %bitcast.tile_far_ref.tile_ref, f32[16]{0:T(128)S(1)} %copy-done.11, f32[16,64,1024]{2,1,0:T(8,128)S(1)} %bitcast.25, f32[16,1,1024]{2,1,0:T(1,128)S(1)} %collective-permute-done.low_ref, f32[16,1,1024]{2,1,0:T(1,128)S(1)} %collective-permute-done.1.high_ref, ...), custom_call_target="tpu_custom_call" | custom-call | flops 10485760 | bytes 8388608 | tf_op jit(solution)/shard_map/step_levels/pallas_call | solution.py:368
  36.0 2.8 %all-to-all-done = f32[32,24,128]{2,1,0:T(8,128)S(1)} async-done(((f32[32,24,128]{2,1,0:T(8,128)}), f32[32,24,128]{2,1,0:T(8,128)S(1)}, u32[]{:S(2)}, u32[]{:S(2)}) %all-to-all-start) | async-done | bytes 393248 | tf_op jit(solution)/shard_map/all_to_all | solution.py:488
  38.7 0.0 copy-done.10
  38.7 0.7 shard_products.1
  39.4 9.6 %all_to_all.20 = f32[8,16,128]{2,1,0:T(8,128)S(1)} all-to-all(f32[8,16,128]{2,1,0:T(8,128)S(1)} %bitcast.40), channel_id=1, replica_groups=mesh['half'=2,'member'=16,'tile'=8] {'tile'}, dimensions={0} | all-to-all | bytes 131072 | tf_op jit(solution)/shard_map/all_to_all | solution.py:488
  49.0 14.0 %all_to_all.21 = f32[32,16,128]{2,1,0:T(8,128)S(1)} all-to-all(f32[32,16,128]{2,1,0:T(8,128)S(1)} %bitcast.33), channel_id=1, replica_groups=mesh['half'=2,'member'=16,'tile'=8] {'half','member'}, dimensions={0} | all-to-all | bytes 524288 | tf_op jit(solution)/shard_map/all_to_all | solution.py:488
  63.0 2.0 %solve_and_combine.1 = f32[512,128]{1,0:T(8,128)S(1)} custom-call(f32[512,128]{1,0:T(8,128)S(1)} %bitcast.31, f32[768,128]{1,0:T(8,128)S(1)} %bitcast.27), custom_call_target="tpu_custom_call" | custom-call | tf_op jit(solution)/shard_map/solve_and_combine/pallas_call | solution.py:475
  65.0 12.4 %all_to_all.22 = f32[32,16,128]{2,1,0:T(8,128)S(1)} all-to-all(f32[32,16,128]{2,1,0:T(8,128)S(1)} %bitcast.32), channel_id=1, replica_groups=mesh['half'=2,'member'=16,'tile'=8] {'half','member'}, dimensions={0} | all-to-all | bytes 524288 | tf_op jit(solution)/shard_map/all_to_all | solution.py:488
  77.4 0.7 copy.16
  (1 shorter events, 0.0 us)
Async XLA Ops:
  0.6 12.3 %copy-start.2 = (s32[64,1024]{1,0:T(8,128)S(1)}, s32[64,1024]{1,0:T(8,128)}, u32[]{:S(2)}) copy-start(s32[64,1024]{1,0:T(8,128)} %land_ref.3) | copy-start | bytes 786436
  0.6 28.6 %copy-start.11 = (f32[16]{0:T(128)S(1)}, f32[16]{0:T(128)}, u32[]{:S(2)}) copy-start(f32[16]{0:T(128)} %gain_ref.1) | copy-start | bytes 196
  0.7 12.3 %copy-start.1 = (f32[1,64,1024]{2,1,0:T(8,128)S(1)}, f32[1,64,1024]{2,1,0:T(8,128)}, u32[]{:S(2)}) copy-start(f32[1,64,1024]{2,1,0:T(8,128)} %param.13) | copy-start | bytes 786436
  0.7 12.2 %copy-start.9 = (f32[1,16384]{1,0:T(1,128)S(1)}, f32[1,16384]{1,0:T(1,128)}, u32[]{:S(2)}) copy-start(f32[1,16384]{1,0:T(1,128)} %param.23) | copy-start | bytes 196612
  0.7 12.2 %copy-start.8 = (f32[16384]{0:T(1024)S(1)}, f32[16384]{0:T(1024)}, u32[]{:S(2)}) copy-start(f32[16384]{0:T(1024)} %param.21) | copy-start | bytes 196612
  0.7 12.2 %copy-start.4 = (f32[2,16384]{1,0:T(2,128)S(1)}, f32[2,16384]{1,0:T(2,128)}, u32[]{:S(2)}) copy-start(f32[2,16384]{1,0:T(2,128)} %frac_ref.1) | copy-start | bytes 393220
  0.7 12.2 %copy-start.7 = (s32[16384]{0:T(1024)S(1)}, s32[16384]{0:T(1024)}, u32[]{:S(2)}) copy-start(s32[16384]{0:T(1024)} %param.19) | copy-start | bytes 196612
  0.7 12.2 %copy-start.6 = (s32[16384]{0:T(1024)S(1)}, s32[16384]{0:T(1024)}, u32[]{:S(2)}) copy-start(s32[16384]{0:T(1024)} %param.18) | copy-start | bytes 196612
  0.7 12.2 %copy-start.5 = (s32[16384]{0:T(1024)S(1)}, s32[16384]{0:T(1024)}, u32[]{:S(2)}) copy-start(s32[16384]{0:T(1024)} %param.17) | copy-start | bytes 196612
  2.1 9.9 %collective-permute-start.1 = (f32[16,1,1024]{2,1,0:T(1,128)S(1)}, f32[16,1,1024]{2,1,0:T(1,128)S(1)}, u32[]{:S(2)}, u32[]{:S(2)}) collective-permute-start(f32[16,1,1024]{2,1,0:T(1,128)S(1)} %get-tuple-element.11), channel_id=1, source_target_pairs={{1,0},{2,1},{3,2},{4,3},{5,4},{6,5},{7,6},{0,7},{9,8},{10,9},{11,1... | collective-permute-start | bytes 196616 | tf_op jit(solution)/shard_map/ppermute | solution.py:516
  8.6 4.3 %collective-permute-start = (f32[16,1,1024]{2,1,0:T(1,128)S(1)}, f32[16,1,1024]{2,1,0:T(1,128)S(1)}, u32[]{:S(2)}, u32[]{:S(2)}) collective-permute-start(f32[16,1,1024]{2,1,0:T(1,128)S(1)} %get-tuple-element.12), channel_id=1, source_target_pairs={{0,1},{1,2},{2,3},{3,4},{4,5},{5,6},{6,7},{7,0},{8,9},{9,10},{10,1... | collective-permute-start | bytes 196616 | tf_op jit(solution)/shard_map/ppermute | solution.py:515
  8.6 30.2 %copy-start.10 = (f32[16384]{0:T(1024)S(1)}, f32[16384]{0:T(1024)}, u32[]{:S(2)}) copy-start(f32[16384]{0:T(1024)} %param.22) | copy-start | bytes 196612
  13.0 1.0 %copy-start.3 = (f32[72,1024]{1,0:T(8,128)S(1)}, f32[72,1024]{1,0:T(8,128)}, u32[]{:S(2)}) copy-start(f32[72,1024]{1,0:T(8,128)} %sum_column.1.column_ref) | copy-start | bytes 884740
  20.0 18.7 %all-to-all-start = ((f32[32,24,128]{2,1,0:T(8,128)}), f32[32,24,128]{2,1,0:T(8,128)S(1)}, u32[]{:S(2)}, u32[]{:S(2)}) async-start(f32[32,24,128]{2,1,0:T(8,128)} %bitcast.10), calls=%async_computation | async-start | bytes 786432 | tf_op jit(solution)/shard_map/all_to_all | solution.py:488
  29.2 2.2 %copy-start = (f32[1,16,64,1024]{3,2,1,0:T(8,128)S(1)}, f32[1,16,64,1024]{3,2,1,0:T(8,128)}, u32[]{:S(2)}) copy-start(f32[1,16,64,1024]{3,2,1,0:T(8,128)} %param.12) | copy-start | bytes 12582916

commit v10 on v8

--- a/solution.py
+++ b/solution.py
@@ -439,10 +439,31 @@
     lane = lax.broadcasted_iota(jnp.int32, (members, 2 * members), 1)
     system = jnp.concatenate([packed[:, : 2 * members], packed[:, 2 * members :]], axis=0)
     system = system / total_obs + jnp.where(row + members == lane, 1.0, 0.0)
-    for k in range(members):
-        at = slice(members + k, members + k + 1)
-        pivot_row = system[k : k + 1, :] * (1.0 / system[k : k + 1, at])
-        system = jnp.where(row == k, pivot_row, system - system[:, at] * pivot_row)
+    def pair(a, b, c, d):
+        scale = 1.0 / (a * d - b * c)
+        return lambda u, v: ((d * u - b * v) * scale, (a * v - c * u) * scale)
+
+    for k in range(0, members, 4):
+        spread = [
+            jnp.broadcast_to(system[:, at : at + 1], system.shape)
+            for at in range(members + k, members + k + 4)
+        ]
+        m = [[column[k + i : k + i + 1, :] for column in spread] for i in range(4)]
+        r = [system[k + i : k + i + 1, :] for i in range(4)]
+        solved = pair(m[0][0], m[0][1], m[1][0], m[1][1])
+        p0, p1 = solved(r[0], r[1])
+        (x0, x1), (y0, y1) = solved(m[0][2], m[1][2]), solved(m[0][3], m[1][3])
+        r2, r3 = (r[i] - m[i][0] * p0 - m[i][1] * p1 for i in (2, 3))
+        a, c = (m[i][2] - m[i][0] * x0 - m[i][1] * x1 for i in (2, 3))
+        b, d = (m[i][3] - m[i][0] * y0 - m[i][1] * y1 for i in (2, 3))
+        p2, p3 = pair(a, b, c, d)(r2, r3)
+        pivots = [p0 - x0 * p2 - y0 * p3, p1 - x1 * p2 - y1 * p3, p2, p3]
+        others = system
+        for column, pivot in zip(spread, pivots):
+            others = others - column * pivot
+        for i, pivot in enumerate(pivots):
+            others = jnp.where(row == k + i, pivot, others)
+        system = others
     coefficients = system[:, :members]
     combination = coefficients - jnp.sum(coefficients, axis=0, keepdims=True) * (1.0 / members)
     combination = combination + jnp.where(row == lane, 1.0, 0.0)[:, :members]

time: 79.6 us -> 78 us (0.980)
  Pallas kernels: 17.8 us -> 16.1 us
    pallas_call x3, Pallas kernels: 3.81 us -> 2.16 us  [local(): pl.pallas_call(kernel, in_specs=[smem if array.dtype == jnp.int32 else vm...]
where the time goes in v10:
time: 78 us; the launch traced here: 77.6 us
  blocking collectives  36 us (46%)
  Pallas kernels  16.1 us (21%)
  starting transfers between devices  15.7 us (20%)
  local copies, waits for them, and re-layouts  5.26 us (7%)
  waiting for transfers between devices  3.72 us (5%)
  between operations  0.82 us (1%)
    all_to_all x3, blocking collectives, swap(): lax.all_to_all(pieces, axes, split_axis=0, concat_axis=0, tiled=True)  36 us
    all_to_all x1, starting transfers between devices, swap(): lax.all_to_all(pieces, axes, split_axis=0, concat_axis=0, tiled=True)  9.19 us
    ppermute x1, starting transfers between devices, on_device(): high = lax.ppermute(own[:, :1], 'tile', down)  6.48 us
    pallas_call x1, Pallas kernels, forward(): pl.pallas_call(sample_column, in_specs=[vmem] * (5 + len(obs)), out_specs...  6.06 us
    pallas_call x1, Pallas kernels, forward(): pl.pallas_call(functools.partial(step_levels, tile_count), grid=(levels /...  4.55 us
    unnamed x25, local copies, waits for them, and re-layouts  3.89 us
    pallas_call x1, Pallas kernels, forward(): pl.pallas_call(functools.partial(sum_column, tile_count), in_specs=[pl.Bl...  3.36 us
    all_to_all x1, waiting for transfers between devices, swap(): lax.all_to_all(pieces, axes, split_axis=0, concat_axis=0, tiled=True)  2.78 us
  transfers between devices with their start and end apart: 3, of which 2 were waited for; matrix products, arithmetic and copies ran while one was open for 0% of the time, Pallas kernels for 10%

profile of v10, /device:TPU:1, one launch (start us, length us, event | category | flops | bytes accessed | tf_op | source)
XLA Modules:
  0.0 77.6 jit_solution(1203963367022166203)
XLA Ops:
  0.6 0.0 copy-start.2
  0.6 0.0 copy-start.11
  0.7 0.0 copy-start.1
  0.7 0.0 copy-start.9
  0.7 0.0 copy-start.8
  0.7 0.0 copy-start.4
  0.7 0.0 copy-start.7
  0.7 0.0 copy-start.6
  0.7 0.0 copy-start.5
  0.7 1.4 %fusion = (f32[16,1,1024]{2,1,0:T(1,128)S(1)}, f32[16,1,1024]{2,1,0:T(1,128)S(1)}) fusion(f32[16,64,1024]{2,1,0:T(8,128)} %bitcast.23), kind=kLoop, calls=%fused_computation | loop fusion | bytes 262144 | tf_op jit(solution)/shard_map/slice | solution.py:529
  2.1 6.5 %collective-permute-start.1 = (f32[16,1,1024]{2,1,0:T(1,128)S(1)}, f32[16,1,1024]{2,1,0:T(1,128)S(1)}, u32[]{:S(2)}, u32[]{:S(2)}) collective-permute-start(f32[16,1,1024]{2,1,0:T(1,128)S(1)} %get-tuple-element.11), channel_id=1, source_target_pairs={{1,0},{2,1},{3,2},{4,3},{5,4},{6,5},{7,6},{0,7},{9,8},{10,9},{11,1... | collective-permute-start | bytes 196616 | tf_op jit(solution)/shard_map/ppermute | solution.py:529
  8.6 0.0 collective-permute-start
  8.6 0.0 copy-start.10
  8.6 3.4 %sum_column.1.column_ref = f32[72,1024]{1,0:T(8,128)} custom-call(f32[16]{0:T(128)} %gain_ref.1, f32[16]{0:T(128)} %depth_far_ref.1, f32[16,64,1024]{2,1,0:T(8,128)} %bitcast.24, f32[64,1024]{1,0:T(8,128)} %bitcast.28, s32[64,1024]{1,0:T(8,128)} %land_ref.3, s32[1]{0:T(128)} %bitcast.tile_far_ref.tile_ref), custom_call_target="tpu_custom_call" | custom-call | flops 6291456 | bytes 4194304 | tf_op jit(solution)/shard_map/sum_column/pallas_call | solution.py:337
  12.0 0.0 collective-permute-done.1.high_ref
  12.0 0.9 %collective-permute-done.low_ref = f32[16,1,1024]{2,1,0:T(1,128)S(1)} collective-permute-done((f32[16,1,1024]{2,1,0:T(1,128)S(1)}, f32[16,1,1024]{2,1,0:T(1,128)S(1)}, u32[]{:S(2)}, u32[]{:S(2)}) %collective-permute-start) | collective-permute-done | bytes 65568 | tf_op jit(solution)/shard_map/ppermute | solution.py:528
  12.9 0.0 copy-done.2
  12.9 0.0 copy-done.1
  12.9 0.0 copy-done.9
  12.9 0.0 copy-done.8
  12.9 0.0 copy-done.4
  12.9 0.0 copy-done.7
  12.9 0.0 copy-done.6
  13.0 0.0 copy-done.5
  13.0 0.0 copy-start.3
  13.0 1.0 %copy-done.3 = f32[72,1024]{1,0:T(8,128)S(1)} copy-done((f32[72,1024]{1,0:T(8,128)S(1)}, f32[72,1024]{1,0:T(8,128)}, u32[]{:S(2)}) %copy-start.3) | copy-done | bytes 294936
  13.9 6.1 %sample_column.1.after_ref = f32[768,128]{1,0:T(8,128)} custom-call(f32[72,1024]{1,0:T(8,128)S(1)} %copy-done.3, f32[16,1,1024]{2,1,0:T(1,128)S(1)} %collective-permute-done.low_ref, f32[16,1,1024]{2,1,0:T(1,128)S(1)} %collective-permute-done.1.high_ref, f32[64,1024]{1,0:T(8,128)S(1)} %bitcast.29, s32[64,1024]{1,0:T(8,128)S(1)} %copy-done.2, ...), custom_call_target="tpu_custom_call" | custom-call | tf_op jit(solution)/shard_map/sample_column/pallas_call | solution.py:359
  20.0 9.2 %all-to-all-start = ((f32[32,24,128]{2,1,0:T(8,128)}), f32[32,24,128]{2,1,0:T(8,128)S(1)}, u32[]{:S(2)}, u32[]{:S(2)}) async-start(f32[32,24,128]{2,1,0:T(8,128)} %bitcast.10), calls=%async_computation | async-start | bytes 786432 | tf_op jit(solution)/shard_map/all_to_all | solution.py:501
  29.2 0.0 copy-done.11
  29.2 0.0 copy-start
  29.2 2.2 %copy-done = f32[1,16,64,1024]{3,2,1,0:T(8,128)S(1)} copy-done((f32[1,16,64,1024]{3,2,1,0:T(8,128)S(1)}, f32[1,16,64,1024]{3,2,1,0:T(8,128)}, u32[]{:S(2)}) %copy-start) | copy-done | bytes 4194328
  31.4 4.6 %step_levels.1 = (f32[16,64,1024]{2,1,0:T(8,128)}, f32[8,128]{1,0:T(8,128)S(1)}) custom-call(s32[1]{0:T(128)} %bitcast.tile_far_ref.tile_ref, f32[16]{0:T(128)S(1)} %copy-done.11, f32[16,64,1024]{2,1,0:T(8,128)S(1)} %bitcast.25, f32[16,1,1024]{2,1,0:T(1,128)S(1)} %collective-permute-done.low_ref, f32[16,1,1024]{2,1,0:T(1,128)S(1)} %collective-permute-done.1.high_ref, ...), custom_call_target="tpu_custom_call" | custom-call | flops 10485760 | bytes 8388608 | tf_op jit(solution)/shard_map/step_levels/pallas_call | solution.py:368
  36.0 2.8 %all-to-all-done = f32[32,24,128]{2,1,0:T(8,128)S(1)} async-done(((f32[32,24,128]{2,1,0:T(8,128)}), f32[32,24,128]{2,1,0:T(8,128)S(1)}, u32[]{:S(2)}, u32[]{:S(2)}) %all-to-all-start) | async-done | bytes 393248 | tf_op jit(solution)/shard_map/all_to_all | solution.py:501
  38.7 0.0 copy-done.10
  38.7 0.7 shard_products.1
  39.4 9.6 %all_to_all.20 = f32[8,16,128]{2,1,0:T(8,128)S(1)} all-to-all(f32[8,16,128]{2,1,0:T(8,128)S(1)} %bitcast.40), channel_id=1, replica_groups=mesh['half'=2,'member'=16,'tile'=8] {'tile'}, dimensions={0} | all-to-all | bytes 131072 | tf_op jit(solution)/shard_map/all_to_all | solution.py:501
  49.0 14.0 %all_to_all.21 = f32[32,16,128]{2,1,0:T(8,128)S(1)} all-to-all(f32[32,16,128]{2,1,0:T(8,128)S(1)} %bitcast.33), channel_id=1, replica_groups=mesh['half'=2,'member'=16,'tile'=8] {'half','member'}, dimensions={0} | all-to-all | bytes 524288 | tf_op jit(solution)/shard_map/all_to_all | solution.py:501
  63.0 1.5 %solve_and_combine.1 = f32[512,128]{1,0:T(8,128)S(1)} custom-call(f32[512,128]{1,0:T(8,128)S(1)} %bitcast.31, f32[768,128]{1,0:T(8,128)S(1)} %bitcast.27), custom_call_target="tpu_custom_call" | custom-call | tf_op jit(solution)/shard_map/solve_and_combine/pallas_call | solution.py:488
  64.5 12.4 %all_to_all.22 = f32[32,16,128]{2,1,0:T(8,128)S(1)} all-to-all(f32[32,16,128]{2,1,0:T(8,128)S(1)} %bitcast.32), channel_id=1, replica_groups=mesh['half'=2,'member'=16,'tile'=8] {'half','member'}, dimensions={0} | all-to-all | bytes 524288 | tf_op jit(solution)/shard_map/all_to_all | solution.py:501
  76.9 0.7 copy.16
  (1 shorter events, 0.0 us)
Async XLA Ops:
  0.6 12.3 %copy-start.2 = (s32[64,1024]{1,0:T(8,128)S(1)}, s32[64,1024]{1,0:T(8,128)}, u32[]{:S(2)}) copy-start(s32[64,1024]{1,0:T(8,128)} %land_ref.3) | copy-start | bytes 786436
  0.6 28.6 %copy-start.11 = (f32[16]{0:T(128)S(1)}, f32[16]{0:T(128)}, u32[]{:S(2)}) copy-start(f32[16]{0:T(128)} %gain_ref.1) | copy-start | bytes 196
  0.7 12.3 %copy-start.1 = (f32[1,64,1024]{2,1,0:T(8,128)S(1)}, f32[1,64,1024]{2,1,0:T(8,128)}, u32[]{:S(2)}) copy-start(f32[1,64,1024]{2,1,0:T(8,128)} %param.13) | copy-start | bytes 786436
  0.7 12.2 %copy-start.9 = (f32[1,16384]{1,0:T(1,128)S(1)}, f32[1,16384]{1,0:T(1,128)}, u32[]{:S(2)}) copy-start(f32[1,16384]{1,0:T(1,128)} %param.23) | copy-start | bytes 196612
  0.7 12.2 %copy-start.8 = (f32[16384]{0:T(1024)S(1)}, f32[16384]{0:T(1024)}, u32[]{:S(2)}) copy-start(f32[16384]{0:T(1024)} %param.21) | copy-start | bytes 196612
  0.7 12.2 %copy-start.4 = (f32[2,16384]{1,0:T(2,128)S(1)}, f32[2,16384]{1,0:T(2,128)}, u32[]{:S(2)}) copy-start(f32[2,16384]{1,0:T(2,128)} %frac_ref.1) | copy-start | bytes 393220
  0.7 12.2 %copy-start.7 = (s32[16384]{0:T(1024)S(1)}, s32[16384]{0:T(1024)}, u32[]{:S(2)}) copy-start(s32[16384]{0:T(1024)} %param.19) | copy-start | bytes 196612
  0.7 12.2 %copy-start.6 = (s32[16384]{0:T(1024)S(1)}, s32[16384]{0:T(1024)}, u32[]{:S(2)}) copy-start(s32[16384]{0:T(1024)} %param.18) | copy-start | bytes 196612
  0.7 12.2 %copy-start.5 = (s32[16384]{0:T(1024)S(1)}, s32[16384]{0:T(1024)}, u32[]{:S(2)}) copy-start(s32[16384]{0:T(1024)} %param.17) | copy-start | bytes 196612
  2.1 9.9 %collective-permute-start.1 = (f32[16,1,1024]{2,1,0:T(1,128)S(1)}, f32[16,1,1024]{2,1,0:T(1,128)S(1)}, u32[]{:S(2)}, u32[]{:S(2)}) collective-permute-start(f32[16,1,1024]{2,1,0:T(1,128)S(1)} %get-tuple-element.11), channel_id=1, source_target_pairs={{1,0},{2,1},{3,2},{4,3},{5,4},{6,5},{7,6},{0,7},{9,8},{10,9},{11,1... | collective-permute-start | bytes 196616 | tf_op jit(solution)/shard_map/ppermute | solution.py:529
  8.6 4.3 %collective-permute-start = (f32[16,1,1024]{2,1,0:T(1,128)S(1)}, f32[16,1,1024]{2,1,0:T(1,128)S(1)}, u32[]{:S(2)}, u32[]{:S(2)}) collective-permute-start(f32[16,1,1024]{2,1,0:T(1,128)S(1)} %get-tuple-element.12), channel_id=1, source_target_pairs={{0,1},{1,2},{2,3},{3,4},{4,5},{5,6},{6,7},{7,0},{8,9},{9,10},{10,1... | collective-permute-start | bytes 196616 | tf_op jit(solution)/shard_map/ppermute | solution.py:528
  8.6 30.2 %copy-start.10 = (f32[16384]{0:T(1024)S(1)}, f32[16384]{0:T(1024)}, u32[]{:S(2)}) copy-start(f32[16384]{0:T(1024)} %param.22) | copy-start | bytes 196612
  13.0 1.0 %copy-start.3 = (f32[72,1024]{1,0:T(8,128)S(1)}, f32[72,1024]{1,0:T(8,128)}, u32[]{:S(2)}) copy-start(f32[72,1024]{1,0:T(8,128)} %sum_column.1.column_ref) | copy-start | bytes 884740
  20.0 18.7 %all-to-all-start = ((f32[32,24,128]{2,1,0:T(8,128)}), f32[32,24,128]{2,1,0:T(8,128)S(1)}, u32[]{:S(2)}, u32[]{:S(2)}) async-start(f32[32,24,128]{2,1,0:T(8,128)} %bitcast.10), calls=%async_computation | async-start | bytes 786432 | tf_op jit(solution)/shard_map/all_to_all | solution.py:501
  29.2 2.2 %copy-start = (f32[1,16,64,1024]{3,2,1,0:T(8,128)S(1)}, f32[1,16,64,1024]{3,2,1,0:T(8,128)}, u32[]{:S(2)}) copy-start(f32[1,16,64,1024]{3,2,1,0:T(8,128)} %param.12) | copy-start | bytes 12582916
